TPU v7x, 512 devices: a whole 4x8x8 slice. The times are simulated.
512 devices in a mesh: gx: 64 (over y_hi, z, core), gy: 8 (over x, y_lo).
Axes of the slice: x: 4, y: 8 (y_hi: 4, y_lo: 2; y = y_hi * 2 + y_lo), z: 8, core: 2. Of those that a mesh axis runs over, the one named last changes fastest.
Arguments:
- gas_state: float32 [5, 512, 64, 256], P(None, 'gx', 'gy'), may hold values from -3 to 3
- pressure_guess: float32 [512, 64, 256], P('gx', 'gy'), may hold values from -6 to 6
- drop_motion: float32 [4, 64, 32768], P(None, 'gx', 'gy'), may hold values from -6 to 6
- drop_size: float32 [64, 32768], P('gx', 'gy'), may hold values from 0.5 to 2
- drop_cell: int32 [64, 32768], P('gx', 'gy'), may hold values from 0 to 16383
- drop_target: int32 [64, 32768], P('gx', 'gy'), may hold values from -1 to 4, as said below
- spray_on: int32 [64, 64], P('gx', 'gy'), may hold values 0 or 1
- spray_time: int32 [64, 64], P('gx', 'gy'), may hold values from 0 to 100
- spray_cell: int32 [64, 64], P('gx', 'gy'), may hold values from 0 to 16383
Outputs:
- gas_next: float32 [5, 512, 64, 256], P(None, 'gx', 'gy')
- pressure: float32 [512, 64, 256], P('gx', 'gy')
- drop_kept: float32 [5, 64, 32768], P(None, 'gx', 'gy')
- drop_arrived: float32 [4, 5, 64, 4096], P(None, None, 'gx', 'gy')
Inputs may be any that keep to these rules, and one draw needn't show every extreme that they name: `drop_target`: in each device's 4096 slots at most 512 droplets have any one of the targets 0, 1, 2, 3, and on every device one of these targets has exactly 512.
All inputs are finite; a program needn't handle non-finite values. No bound on the sum of `spray_on` on one device may be relied on, other than what follows from the above.
Results may differ from a plain program's by a relative error of at most 0.00002.
Values sent between devices are 32-bit elements; how exact they have to be, the bound alone decides.
No kernel may reach another device: no remote copies, remote signals or barrier semaphores. Data moves between devices by JAX's collectives and lax.ppermute only.
A program may use at most 128 MiB of HBM per device.

v0:
```python
import jax
import jax.numpy as jnp
from jax import lax
from jax.sharding import PartitionSpec as P

ITERS = 8
CAP = 512


TIME_STEP = 0.2
DIFFUSION = 0.1
DRAG_TIME = 0.5
HEAT_TIME = 1.0
GRAVITY = 1.0
VAPOUR_RATE = 0.5
DRAG_COUPLING = 0.5
LATENT = 2.0
VAPOUR_YIELD = 1.0
SPRAY_RATE = 3.0
CLOCK = 100.0
SPRAY_RAMP = 50.0


def padded_2(shard, sides, width):
    for axis, dim in sides:
        peers, length = (lax.axis_size(axis), shard.shape[dim])
        up = [(i, (i + 1) % peers) for i in range(peers - 1)]
        down = [(j, i) for i, j in up]
        last = lax.slice_in_dim(shard, length - width, length, axis=dim)
        leading = lax.slice_in_dim(shard, 0, width, axis=dim)
        before = lax.ppermute(last, axis, up)
        after = lax.ppermute(leading, axis, down)
        shard = jnp.concatenate([before, shard, after], axis=dim)
    return shard


def shifted(shard, axis, by):
    peers = lax.axis_size(axis)
    pairs = [(i, i + by) for i in range(peers) if 0 <= i + by < peers]
    return lax.ppermute(shard, axis, pairs)


def window(padded, along_x, along_y, along_z):
    a = padded.shape[-3] - 4
    b = padded.shape[-2] - 4
    c = padded.shape[-1] - 4
    return padded[
        ...,
        2 + along_x : 2 + along_x + a,
        2 + along_y : 2 + along_y + b,
        2 + along_z : 2 + along_z + c,
    ]


def gradient(padded, along_x, along_y, along_z):
    near = window(padded, along_x, along_y, along_z) - window(padded, -along_x, -along_y, -along_z)
    far = window(padded, 2 * along_x, 2 * along_y, 2 * along_z) - window(
        padded, -2 * along_x, -2 * along_y, -2 * along_z
    )
    return (8.0 * near - far) / 12.0


def predict(padded):
    speed_x = window(padded[0], 0, 0, 0)
    speed_y = window(padded[1], 0, 0, 0)
    speed_z = window(padded[2], 0, 0, 0)
    results = []
    for field in range(padded.shape[0]):
        single = padded[field]
        centre = window(single, 0, 0, 0)
        laplace = window(single, 1, 0, 0) + window(single, -1, 0, 0) + window(single, 0, 1, 0)
        laplace = (
            laplace
            + window(single, 0, -1, 0)
            + window(single, 0, 0, 1)
            + window(single, 0, 0, -1)
            - 6.0 * centre
        )
        transport = (
            speed_x * gradient(single, 1, 0, 0)
            + speed_y * gradient(single, 0, 1, 0)
            + speed_z * gradient(single, 0, 0, 1)
        )
        results.append(centre + TIME_STEP * (DIFFUSION * laplace - transport))
    return jnp.stack(results)


def divergence(flow_x, flow_y, vertical):
    lifted = jnp.pad(vertical, ((0, 0), (0, 0), (1, 1)))
    spread = 0.5 * (flow_x[2:, 1:-1] - flow_x[:-2, 1:-1]) + 0.5 * (
        flow_y[1:-1, 2:] - flow_y[1:-1, :-2]
    )
    spread = spread + 0.5 * (lifted[:, :, 2:] - lifted[:, :, :-2])
    return spread / TIME_STEP


def sweep(bordered, source):
    inner = bordered[1:-1, 1:-1]
    lifted = jnp.pad(inner, ((0, 0), (0, 0), (1, 1)))
    beside_all = bordered[2:, 1:-1] + bordered[:-2, 1:-1] + bordered[1:-1, 2:] + bordered[1:-1, :-2]
    beside_all = beside_all + lifted[:, :, 2:] + lifted[:, :, :-2]
    return (beside_all - source) / 6.0


def correct(star, bordered):
    inner = bordered[1:-1, 1:-1]
    lifted = jnp.pad(inner, ((0, 0), (0, 0), (1, 1)))
    flow_x = star[0] - TIME_STEP * 0.5 * (bordered[2:, 1:-1] - bordered[:-2, 1:-1])
    flow_y = star[1] - TIME_STEP * 0.5 * (bordered[1:-1, 2:] - bordered[1:-1, :-2])
    vertical = star[2] - TIME_STEP * 0.5 * (lifted[:, :, 2:] - lifted[:, :, :-2])
    return jnp.concatenate([jnp.stack([flow_x, flow_y, vertical]), star[3:]], axis=0)


def droplets(motion, diameter, local):
    excess = local[3] - motion[3]
    vapour = VAPOUR_RATE * diameter * jax.nn.sigmoid(excess)
    renewed = jnp.stack(
        [
            motion[0] + TIME_STEP * (local[0] - motion[0]) / DRAG_TIME,
            motion[1] + TIME_STEP * (local[1] - motion[1]) / DRAG_TIME,
            motion[2] + TIME_STEP * ((local[2] - motion[2]) / DRAG_TIME - GRAVITY),
            motion[3] + TIME_STEP * excess / HEAT_TIME,
            diameter - TIME_STEP * vapour,
        ]
    )
    sources = jnp.stack(
        [
            DRAG_COUPLING * diameter * diameter * (motion[2] - local[2]),
            -LATENT * vapour,
            VAPOUR_YIELD * vapour,
        ]
    )
    return (renewed, sources)


def spray(flags, times):
    ramp = jnp.clip((CLOCK - times.astype(jnp.float32)) / SPRAY_RAMP, 0.0, 1.0)
    strength = SPRAY_RATE * ramp * flags.astype(jnp.float32)
    return jnp.stack([-strength, -strength, jnp.zeros_like(strength)])


def add_sources(star, sources):
    return jnp.concatenate([star[:2], star[2:] + TIME_STEP * sources], axis=0)


def body(
    gas_state,
    pressure_guess,
    drop_motion,
    drop_size,
    drop_cell,
    drop_target,
    spray_on,
    spray_time,
    spray_cell,
):
    fields, wide_x, wide_y, depth = gas_state.shape
    volume = wide_x * wide_y * depth
    flat = gas_state.reshape(fields, volume)
    cells = drop_cell[0]
    target = drop_target[0]
    local = flat[:, cells]
    renewed, drop_sources = droplets(drop_motion[:, 0], drop_size[0], local)
    drop_sources = jnp.where((target >= 0)[None], drop_sources, 0.0)
    sources = jnp.zeros((3, volume), jnp.float32).at[:, cells].add(drop_sources)
    sources = sources.at[:, spray_cell[0]].add(spray(spray_on[0], spray_time[0]))
    sources = sources.reshape(3, wide_x, wide_y, depth)
    padded = padded_2(gas_state, (("gx", 1), ("gy", 2)), 2)
    padded = jnp.pad(padded, ((0, 0), (0, 0), (0, 0), (2, 2)))
    star = add_sources(predict(padded), sources)
    flows = padded_2(star[:2], (("gx", 1), ("gy", 2)), 1)
    source = divergence(flows[0], flows[1], star[2])
    field = pressure_guess
    for turn in range(ITERS):
        bordered = padded_2(field, (("gx", 0), ("gy", 1)), 1)
        field = sweep(bordered, source)
    final_rim = padded_2(field, (("gx", 0), ("gy", 1)), 1)
    gas_next = correct(star, final_rim)
    parcels = []
    for heading in range(4):
        chosen = target == heading
        order = jnp.cumsum(chosen.astype(jnp.int32)) - 1
        place = jnp.where(chosen, order, CAP)
        parcel = jnp.zeros((5, CAP + 1), jnp.float32).at[:, place].set(renewed)
        parcels.append(parcel[:, None, :CAP])
    arrived = jnp.stack(
        [
            shifted(parcels[0], "gx", 1),
            shifted(parcels[1], "gx", -1),
            shifted(parcels[2], "gy", 1),
            shifted(parcels[3], "gy", -1),
        ]
    )
    drop_kept = jnp.where((target == 4)[None], renewed, 0.0)[:, None, :]
    return (gas_next, field, drop_kept, arrived)


def solution(mesh):
    in_specs = (
        P(None, "gx", "gy", None),
        P("gx", "gy", None),
        P(None, "gx", "gy"),
        P("gx", "gy"),
        P("gx", "gy"),
        P("gx", "gy"),
        P("gx", "gy"),
        P("gx", "gy"),
        P("gx", "gy"),
    )
    out_specs = (
        P(None, "gx", "gy", None),
        P("gx", "gy", None),
        P(None, "gx", "gy"),
        P(None, None, "gx", "gy"),
    )
    return jax.shard_map(body, mesh=mesh, in_specs=in_specs, out_specs=out_specs, check_vma=False)
```

profile of v0, /device:TPU:40, one launch (start us, length us, event | category | flops | bytes accessed | tf_op | source)
XLA Modules:
  0.0 341.3 jit_solution(15655475633029428582)
XLA Ops:
  3.5 11.1 %collective-permute-start.1 = (f32[5,2,8,256]{3,2,1,0:T(8,128)S(1)}, f32[5,2,8,256]{3,2,1,0:T(8,128)S(1)}, u32[]{:S(2)}, u32[]{:S(2)}) collective-permute-start(f32[5,2,8,256]{3,2,1,0:T(8,128)S(1)} %get-tuple-element.44), channel_id=1, source_target_pairs={{8,0},{16,8},{24,16},{32,24},{40,32},{48,40},{56,48},{64,56},{72,6... | collective-permute-start | bytes 245768 | tf_op jit(solution)/shard_map/ppermute | solution.py:32
  17.2 7.9 %collective-permute-start.4 = (f32[1,8,256]{2,1,0:T(8,128)S(1)}, f32[1,8,256]{2,1,0:T(8,128)S(1)}, u32[]{:S(2)}, u32[]{:S(2)}) collective-permute-start(f32[1,8,256]{2,1,0:T(8,128)S(1)} %get-tuple-element.87), channel_id=1, source_target_pairs={{8,0},{16,8},{24,16},{32,24},{40,32},{48,40},{56,48},{64,56},{72,6... | collective-permute-start | bytes 24584 | tf_op jit(solution)/shard_map/ppermute | solution.py:32
  25.1 5.9 %copy.86 = f32[5,8,8,256]{0,3,2,1:T(8,128)} copy(f32[5,8,8,256]{3,2,1,0:T(8,128)} %param.9) | data formatting | bytes 655360 | tf_op args[0]
  31.1 14.1 %gather_fusion = f32[4096,5]{1,0:T(8,128)S(1)} fusion(f32[5,16384]{0,1:T(8,128)} %bitcast.126, s32[4096]{0:T(1024)S(1)} %broadcast_clamp_fusion), kind=kCustom, calls=%fused_computation | custom fusion | bytes 180224 | tf_op jit(solution)/shard_map/gather | solution.py:162
  47.2 26.1 %scatter_custom_fusion = f32[3,16384]{0,1:T(8,128)} fusion(s32[4096]{0:T(1024)S(1)} %bitcast.147, f32[4096,3]{1,0:T(8,128)S(1)} %copy.88, f32[]{:T(128)} %constant.73.clone.1), kind=kCustom, calls=%fused_computation.8 | custom fusion | flops 12288 | bytes 196612 | tf_op jit(solution)/shard_map/scatter-add | solution.py:165
  73.4 7.2 %scatter_fusion = f32[3,16384]{0,1:T(8,128)} fusion(f32[3,16384]{0,1:T(8,128)} %scatter_custom_fusion, s32[8]{0:T(128)S(1)} %fusion.164, f32[8,3]{1,0:T(8,128)S(1)} %copy.89), kind=kCustom, calls=%fused_computation.2 | custom fusion | flops 24 | bytes 320 | tf_op jit(solution)/shard_map/scatter-add | solution.py:166
  80.6 5.8 %broadcast_multiply_fusion = f32[3,16384]{0,1:T(8,128)} fusion(f32[3,16384]{0,1:T(8,128)} %scatter_fusion), kind=kLoop, calls=%fused_computation.7 | loop fusion | flops 49152 | bytes 393216 | tf_op jit(solution)/shard_map/mul | solution.py:143
  86.5 5.3 %copy.90 = f32[3,8,8,256]{3,2,1,0:T(8,128)S(1)} copy(f32[3,8,8,256]{0,3,2,1:T(8,128)} %bitcast.125) | data formatting | bytes 393216 | tf_op jit(solution)/shard_map/mul | solution.py:143
  94.3 4.4 %collective-permute-start.2 = (f32[5,12,2,256]{3,2,1,0:T(2,128)S(1)}, f32[5,12,2,256]{3,2,1,0:T(2,128)S(1)}, u32[]{:S(2)}, u32[]{:S(2)}) collective-permute-start(f32[5,12,2,256]{3,2,1,0:T(2,128)S(1)} %get-tuple-element.40), channel_id=1, source_target_pairs={{0,1},{1,2},{2,3},{3,4},{4,5},{5,6},{6,7},{8,9},{9,10},{10,11},{11... | collective-permute-start | bytes 368648 | tf_op jit(solution)/shard_map/ppermute | solution.py:31
  111.7 6.8 %collective-permute-done.8 = f32[2,1,8,256]{3,2,1,0:T(8,128)S(1)} collective-permute-done((f32[2,1,8,256]{3,2,1,0:T(8,128)S(1)}, f32[2,1,8,256]{3,2,1,0:T(8,128)S(1)}, u32[]{:S(2)}, u32[]{:S(2)}) %collective-permute-start.8) | collective-permute-done | bytes 16416 | tf_op jit(solution)/shard_map/ppermute | solution.py:31
  120.5 4.8 %collective-permute-start.10 = (f32[2,10,1,256]{3,2,1,0:T(1,128)S(1)}, f32[2,10,1,256]{3,2,1,0:T(1,128)S(1)}, u32[]{:S(2)}, u32[]{:S(2)}) collective-permute-start(f32[2,10,1,256]{3,2,1,0:T(1,128)S(1)} %get-tuple-element.46), channel_id=1, source_target_pairs={{0,1},{1,2},{2,3},{3,4},{4,5},{5,6},{6,7},{8,9},{9,10},{10,11},{11... | collective-permute-start | bytes 61448 | tf_op jit(solution)/shard_map/ppermute | solution.py:31
  131.8 6.4 %collective-permute-done.13 = f32[1,8,256]{2,1,0:T(8,128)S(1)} collective-permute-done((f32[1,8,256]{2,1,0:T(8,128)S(1)}, f32[1,8,256]{2,1,0:T(8,128)S(1)}, u32[]{:S(2)}, u32[]{:S(2)}) %collective-permute-start.13) | collective-permute-done | bytes 8224 | tf_op jit(solution)/shard_map/ppermute | solution.py:31
  138.2 5.2 %collective-permute-start.15 = (f32[10,1,256]{2,1,0:T(1,128)S(1)}, f32[10,1,256]{2,1,0:T(1,128)S(1)}, u32[]{:S(2)}, u32[]{:S(2)}) collective-permute-start(f32[10,1,256]{2,1,0:T(1,128)S(1)} %get-tuple-element.67), channel_id=1, source_target_pairs={{0,1},{1,2},{2,3},{3,4},{4,5},{5,6},{6,7},{8,9},{9,10},{10,11},{11... | collective-permute-start | bytes 30728 | tf_op jit(solution)/shard_map/ppermute | solution.py:31
  145.4 4.4 %collective-permute-done.14 = f32[10,1,256]{2,1,0:T(1,128)S(1)} collective-permute-done((f32[10,1,256]{2,1,0:T(1,128)S(1)}, f32[10,1,256]{2,1,0:T(1,128)S(1)}, u32[]{:S(2)}, u32[]{:S(2)}) %collective-permute-start.14) | collective-permute-done | bytes 10272 | tf_op jit(solution)/shard_map/ppermute | solution.py:32
  154.8 6.3 %collective-permute-done.17 = f32[1,8,256]{2,1,0:T(8,128)S(1)} collective-permute-done((f32[1,8,256]{2,1,0:T(8,128)S(1)}, f32[1,8,256]{2,1,0:T(8,128)S(1)}, u32[]{:S(2)}, u32[]{:S(2)}) %collective-permute-start.17) | collective-permute-done | bytes 8224 | tf_op jit(solution)/shard_map/ppermute | solution.py:31
  163.1 3.9 %collective-permute-start.18 = (f32[10,1,256]{2,1,0:T(1,128)S(1)}, f32[10,1,256]{2,1,0:T(1,128)S(1)}, u32[]{:S(2)}, u32[]{:S(2)}) collective-permute-start(f32[10,1,256]{2,1,0:T(1,128)S(1)} %get-tuple-element.64), channel_id=1, source_target_pairs={{1,0},{2,1},{3,2},{4,3},{5,4},{6,5},{7,6},{9,8},{10,9},{11,10},{12... | collective-permute-start | bytes 30728 | tf_op jit(solution)/shard_map/ppermute | solution.py:32
  174.5 6.3 %collective-permute-done.21 = f32[1,8,256]{2,1,0:T(8,128)S(1)} collective-permute-done((f32[1,8,256]{2,1,0:T(8,128)S(1)}, f32[1,8,256]{2,1,0:T(8,128)S(1)}, u32[]{:S(2)}, u32[]{:S(2)}) %collective-permute-start.21) | collective-permute-done | bytes 8224 | tf_op jit(solution)/shard_map/ppermute | solution.py:31
  180.8 3.9 %collective-permute-start.23 = (f32[10,1,256]{2,1,0:T(1,128)S(1)}, f32[10,1,256]{2,1,0:T(1,128)S(1)}, u32[]{:S(2)}, u32[]{:S(2)}) collective-permute-start(f32[10,1,256]{2,1,0:T(1,128)S(1)} %get-tuple-element.63), channel_id=1, source_target_pairs={{0,1},{1,2},{2,3},{3,4},{4,5},{5,6},{6,7},{8,9},{9,10},{10,11},{11... | collective-permute-start | bytes 30728 | tf_op jit(solution)/shard_map/ppermute | solution.py:31
  186.8 4.4 %collective-permute-done.22 = f32[10,1,256]{2,1,0:T(1,128)S(1)} collective-permute-done((f32[10,1,256]{2,1,0:T(1,128)S(1)}, f32[10,1,256]{2,1,0:T(1,128)S(1)}, u32[]{:S(2)}, u32[]{:S(2)}) %collective-permute-start.22) | collective-permute-done | bytes 10272 | tf_op jit(solution)/shard_map/ppermute | solution.py:32
  196.1 6.3 %collective-permute-done.25 = f32[1,8,256]{2,1,0:T(8,128)S(1)} collective-permute-done((f32[1,8,256]{2,1,0:T(8,128)S(1)}, f32[1,8,256]{2,1,0:T(8,128)S(1)}, u32[]{:S(2)}, u32[]{:S(2)}) %collective-permute-start.25) | collective-permute-done | bytes 8224 | tf_op jit(solution)/shard_map/ppermute | solution.py:31
  204.4 3.9 %collective-permute-start.26 = (f32[10,1,256]{2,1,0:T(1,128)S(1)}, f32[10,1,256]{2,1,0:T(1,128)S(1)}, u32[]{:S(2)}, u32[]{:S(2)}) collective-permute-start(f32[10,1,256]{2,1,0:T(1,128)S(1)} %get-tuple-element.60), channel_id=1, source_target_pairs={{1,0},{2,1},{3,2},{4,3},{5,4},{6,5},{7,6},{9,8},{10,9},{11,10},{12... | collective-permute-start | bytes 30728 | tf_op jit(solution)/shard_map/ppermute | solution.py:32
  215.4 6.7 %collective-permute-done.29 = f32[1,8,256]{2,1,0:T(8,128)S(1)} collective-permute-done((f32[1,8,256]{2,1,0:T(8,128)S(1)}, f32[1,8,256]{2,1,0:T(8,128)S(1)}, u32[]{:S(2)}, u32[]{:S(2)}) %collective-permute-start.29) | collective-permute-done | bytes 8224 | tf_op jit(solution)/shard_map/ppermute | solution.py:31
  222.1 3.9 %collective-permute-start.31 = (f32[10,1,256]{2,1,0:T(1,128)S(1)}, f32[10,1,256]{2,1,0:T(1,128)S(1)}, u32[]{:S(2)}, u32[]{:S(2)}) collective-permute-start(f32[10,1,256]{2,1,0:T(1,128)S(1)} %get-tuple-element.59), channel_id=1, source_target_pairs={{0,1},{1,2},{2,3},{3,4},{4,5},{5,6},{6,7},{8,9},{9,10},{10,11},{11... | collective-permute-start | bytes 30728 | tf_op jit(solution)/shard_map/ppermute | solution.py:31
  228.8 10.7 %scatter_custom_fusion.5 = f32[5,513]{0,1:T(8,128)S(1)} fusion(s32[4096]{0:T(1024)S(1)} %bitcast.155, f32[4096,5]{1,0:T(8,128)S(1)} %copy.91, f32[]{:T(128)} %constant.73.clone.1), kind=kCustom, calls=%fused_computation.30 | custom fusion | bytes 10264 | tf_op jit(solution)/shard_map/scatter | solution.py:184
  246.0 10.7 %scatter_custom_fusion.4 = f32[5,513]{0,1:T(8,128)S(1)} fusion(s32[4096]{0:T(1024)S(1)} %bitcast.154, f32[4096,5]{1,0:T(8,128)S(1)} %copy.91, f32[]{:T(128)} %constant.73.clone.1), kind=kCustom, calls=%fused_computation.32 | custom fusion | bytes 10264 | tf_op jit(solution)/shard_map/scatter | solution.py:184
  257.3 4.8 %collective-permute-start.35 = (f32[10,1,256]{2,1,0:T(1,128)}, f32[10,1,256]{2,1,0:T(1,128)S(1)}, u32[]{:S(2)}, u32[]{:S(2)}) collective-permute-start(f32[10,1,256]{2,1,0:T(1,128)} %get-tuple-element.57), channel_id=1, source_target_pairs={{0,1},{1,2},{2,3},{3,4},{4,5},{5,6},{6,7},{8,9},{9,10},{10,11},{11... | collective-permute-start | bytes 30728 | tf_op jit(solution)/shard_map/ppermute | solution.py:31
  264.7 4.8 %collective-permute-start.46 = (f32[5,1,512]{0,2,1:T(8,128)}, f32[5,1,512]{0,2,1:T(8,128)}, u32[]{:S(2)}, u32[]{:S(2)}) collective-permute-start(f32[5,1,512]{0,2,1:T(8,128)} %slice_bitcast_fusion.6), channel_id=1, source_target_pairs={{0,1},{1,2},{2,3},{3,4},{4,5},{5,6},{6,7},{8,9},{9,10},{10,11},{11... | collective-permute-start | bytes 30728 | tf_op jit(solution)/shard_map/ppermute | solution.py:40
  269.6 10.7 %scatter_custom_fusion.3 = f32[5,513]{0,1:T(8,128)S(1)} fusion(s32[4096]{0:T(1024)S(1)} %bitcast.153, f32[4096,5]{1,0:T(8,128)S(1)} %copy.91, f32[]{:T(128)} %constant.73.clone.1), kind=kCustom, calls=%fused_computation.34 | custom fusion | bytes 10264 | tf_op jit(solution)/shard_map/scatter | solution.py:184
  281.1 6.5 %collective-permute-start.36 = (f32[1,8,256]{2,1,0:T(8,128)S(1)}, f32[1,8,256]{2,1,0:T(8,128)S(1)}, u32[]{:S(2)}, u32[]{:S(2)}) collective-permute-start(f32[1,8,256]{2,1,0:T(8,128)S(1)} %get-tuple-element.74), channel_id=1, source_target_pairs={{8,0},{16,8},{24,16},{32,24},{40,32},{48,40},{56,48},{64,56},{72,6... | collective-permute-start | bytes 24584 | tf_op jit(solution)/shard_map/ppermute | solution.py:32
  290.3 7.8 %collective-permute-start.45 = (f32[5,1,512]{0,2,1:T(8,128)}, f32[5,1,512]{0,2,1:T(8,128)}, u32[]{:S(2)}, u32[]{:S(2)}) collective-permute-start(f32[5,1,512]{0,2,1:T(8,128)} %slice_bitcast_fusion.7), channel_id=1, source_target_pairs={{8,0},{16,8},{24,16},{32,24},{40,32},{48,40},{56,48},{64,56},{72,6... | collective-permute-start | bytes 30728 | tf_op jit(solution)/shard_map/ppermute | solution.py:40
  298.1 10.7 %scatter_custom_fusion.2 = f32[5,513]{0,1:T(8,128)S(1)} fusion(s32[4096]{0:T(1024)S(1)} %bitcast.152, f32[4096,5]{1,0:T(8,128)S(1)} %copy.91, f32[]{:T(128)} %constant.73.clone.1), kind=kCustom, calls=%fused_computation.36 | custom fusion | bytes 10264 | tf_op jit(solution)/shard_map/scatter | solution.py:184
  320.1 7.9 %collective-permute-start.40 = (f32[1,8,256]{2,1,0:T(8,128)S(1)}, f32[1,8,256]{2,1,0:T(8,128)S(1)}, u32[]{:S(2)}, u32[]{:S(2)}) collective-permute-start(f32[1,8,256]{2,1,0:T(8,128)S(1)} %get-tuple-element.72), channel_id=1, source_target_pairs={{8,0},{16,8},{24,16},{32,24},{40,32},{48,40},{56,48},{64,56},{72,6... | collective-permute-start | bytes 24584 | tf_op jit(solution)/shard_map/ppermute | solution.py:32
  (195 shorter events, 104.0 us)
Async XLA Ops:
  1.6 90.2 %collective-permute-start = (f32[5,2,8,256]{3,2,1,0:T(8,128)S(1)}, f32[5,2,8,256]{3,2,1,0:T(8,128)S(1)}, u32[]{:S(2)}, u32[]{:S(2)}) collective-permute-start(f32[5,2,8,256]{3,2,1,0:T(8,128)S(1)} %get-tuple-element.45), channel_id=1, source_target_pairs={{0,8},{8,16},{16,24},{24,32},{32,40},{40,48},{48,56},{56,64},{64,7... | collective-permute-start | bytes 245768 | tf_op jit(solution)/shard_map/ppermute | solution.py:31
  3.5 88.4 %collective-permute-start.1 = (f32[5,2,8,256]{3,2,1,0:T(8,128)S(1)}, f32[5,2,8,256]{3,2,1,0:T(8,128)S(1)}, u32[]{:S(2)}, u32[]{:S(2)}) collective-permute-start(f32[5,2,8,256]{3,2,1,0:T(8,128)S(1)} %get-tuple-element.44), channel_id=1, source_target_pairs={{8,0},{16,8},{24,16},{32,24},{40,32},{48,40},{56,48},{64,56},{72,6... | collective-permute-start | bytes 245768 | tf_op jit(solution)/shard_map/ppermute | solution.py:32
  15.3 76.4 %collective-permute-start.5 = (f32[1,8,256]{2,1,0:T(8,128)S(1)}, f32[1,8,256]{2,1,0:T(8,128)S(1)}, u32[]{:S(2)}, u32[]{:S(2)}) collective-permute-start(f32[1,8,256]{2,1,0:T(8,128)S(1)} %get-tuple-element.88), channel_id=1, source_target_pairs={{0,8},{8,16},{16,24},{24,32},{32,40},{40,48},{48,56},{56,64},{64,7... | collective-permute-start | bytes 24584 | tf_op jit(solution)/shard_map/ppermute | solution.py:31
  17.2 74.6 %collective-permute-start.4 = (f32[1,8,256]{2,1,0:T(8,128)S(1)}, f32[1,8,256]{2,1,0:T(8,128)S(1)}, u32[]{:S(2)}, u32[]{:S(2)}) collective-permute-start(f32[1,8,256]{2,1,0:T(8,128)S(1)} %get-tuple-element.87), channel_id=1, source_target_pairs={{8,0},{16,8},{24,16},{32,24},{40,32},{48,40},{56,48},{64,56},{72,6... | collective-permute-start | bytes 24584 | tf_op jit(solution)/shard_map/ppermute | solution.py:32
  92.0 12.6 %collective-permute-start.3 = (f32[5,12,2,256]{3,2,1,0:T(2,128)S(1)}, f32[5,12,2,256]{3,2,1,0:T(2,128)S(1)}, u32[]{:S(2)}, u32[]{:S(2)}) collective-permute-start(f32[5,12,2,256]{3,2,1,0:T(2,128)S(1)} %get-tuple-element.41), channel_id=1, source_target_pairs={{1,0},{2,1},{3,2},{4,3},{5,4},{6,5},{7,6},{9,8},{10,9},{11,10},{12... | collective-permute-start | bytes 368648 | tf_op jit(solution)/shard_map/ppermute | solution.py:32
  94.3 10.3 %collective-permute-start.2 = (f32[5,12,2,256]{3,2,1,0:T(2,128)S(1)}, f32[5,12,2,256]{3,2,1,0:T(2,128)S(1)}, u32[]{:S(2)}, u32[]{:S(2)}) collective-permute-start(f32[5,12,2,256]{3,2,1,0:T(2,128)S(1)} %get-tuple-element.40), channel_id=1, source_target_pairs={{0,1},{1,2},{2,3},{3,4},{4,5},{5,6},{6,7},{8,9},{9,10},{10,11},{11... | collective-permute-start | bytes 368648 | tf_op jit(solution)/shard_map/ppermute | solution.py:31
  98.8 28.1 %collective-permute-start.7 = (f32[10,1,256]{2,1,0:T(1,128)S(1)}, f32[10,1,256]{2,1,0:T(1,128)S(1)}, u32[]{:S(2)}, u32[]{:S(2)}) collective-permute-start(f32[10,1,256]{2,1,0:T(1,128)S(1)} %get-tuple-element.69), channel_id=1, source_target_pairs={{0,1},{1,2},{2,3},{3,4},{4,5},{5,6},{6,7},{8,9},{9,10},{10,11},{11... | collective-permute-start | bytes 30728 | tf_op jit(solution)/shard_map/ppermute | solution.py:31
  101.2 25.7 %collective-permute-start.6 = (f32[10,1,256]{2,1,0:T(1,128)S(1)}, f32[10,1,256]{2,1,0:T(1,128)S(1)}, u32[]{:S(2)}, u32[]{:S(2)}) collective-permute-start(f32[10,1,256]{2,1,0:T(1,128)S(1)} %get-tuple-element.68), channel_id=1, source_target_pairs={{1,0},{2,1},{3,2},{4,3},{5,4},{6,5},{7,6},{9,8},{10,9},{11,10},{12... | collective-permute-start | bytes 30728 | tf_op jit(solution)/shard_map/ppermute | solution.py:32
  109.3 9.3 %collective-permute-start.8 = (f32[2,1,8,256]{3,2,1,0:T(8,128)S(1)}, f32[2,1,8,256]{3,2,1,0:T(8,128)S(1)}, u32[]{:S(2)}, u32[]{:S(2)}) collective-permute-start(f32[2,1,8,256]{3,2,1,0:T(8,128)S(1)} %get-tuple-element.48), channel_id=1, source_target_pairs={{0,8},{8,16},{16,24},{24,32},{32,40},{40,48},{48,56},{56,64},{64,7... | collective-permute-start | bytes 49160 | tf_op jit(solution)/shard_map/ppermute | solution.py:31
  118.6 6.8 %collective-permute-start.11 = (f32[2,10,1,256]{3,2,1,0:T(1,128)S(1)}, f32[2,10,1,256]{3,2,1,0:T(1,128)S(1)}, u32[]{:S(2)}, u32[]{:S(2)}) collective-permute-start(f32[2,10,1,256]{3,2,1,0:T(1,128)S(1)} %get-tuple-element.47), channel_id=1, source_target_pairs={{1,0},{2,1},{3,2},{4,3},{5,4},{6,5},{7,6},{9,8},{10,9},{11,10},{12... | collective-permute-start | bytes 61448 | tf_op jit(solution)/shard_map/ppermute | solution.py:32
  129.0 9.2 %collective-permute-start.13 = (f32[1,8,256]{2,1,0:T(8,128)S(1)}, f32[1,8,256]{2,1,0:T(8,128)S(1)}, u32[]{:S(2)}, u32[]{:S(2)}) collective-permute-start(f32[1,8,256]{2,1,0:T(8,128)S(1)} %get-tuple-element.85), channel_id=1, source_target_pairs={{0,8},{8,16},{16,24},{24,32},{32,40},{40,48},{48,56},{56,64},{64,7... | collective-permute-start | bytes 24584 | tf_op jit(solution)/shard_map/ppermute | solution.py:31
  138.2 7.2 %collective-permute-start.15 = (f32[10,1,256]{2,1,0:T(1,128)S(1)}, f32[10,1,256]{2,1,0:T(1,128)S(1)}, u32[]{:S(2)}, u32[]{:S(2)}) collective-permute-start(f32[10,1,256]{2,1,0:T(1,128)S(1)} %get-tuple-element.67), channel_id=1, source_target_pairs={{0,1},{1,2},{2,3},{3,4},{4,5},{5,6},{6,7},{8,9},{9,10},{10,11},{11... | collective-permute-start | bytes 30728 | tf_op jit(solution)/shard_map/ppermute | solution.py:31
  151.9 9.2 %collective-permute-start.17 = (f32[1,8,256]{2,1,0:T(8,128)S(1)}, f32[1,8,256]{2,1,0:T(8,128)S(1)}, u32[]{:S(2)}, u32[]{:S(2)}) collective-permute-start(f32[1,8,256]{2,1,0:T(8,128)S(1)} %get-tuple-element.83), channel_id=1, source_target_pairs={{0,8},{8,16},{16,24},{24,32},{32,40},{40,48},{48,56},{56,64},{64,7... | collective-permute-start | bytes 24584 | tf_op jit(solution)/shard_map/ppermute | solution.py:31
  171.6 9.2 %collective-permute-start.21 = (f32[1,8,256]{2,1,0:T(8,128)S(1)}, f32[1,8,256]{2,1,0:T(8,128)S(1)}, u32[]{:S(2)}, u32[]{:S(2)}) collective-permute-start(f32[1,8,256]{2,1,0:T(8,128)S(1)} %get-tuple-element.81), channel_id=1, source_target_pairs={{0,8},{8,16},{16,24},{24,32},{32,40},{40,48},{48,56},{56,64},{64,7... | collective-permute-start | bytes 24584 | tf_op jit(solution)/shard_map/ppermute | solution.py:31
  193.2 9.2 %collective-permute-start.25 = (f32[1,8,256]{2,1,0:T(8,128)S(1)}, f32[1,8,256]{2,1,0:T(8,128)S(1)}, u32[]{:S(2)}, u32[]{:S(2)}) collective-permute-start(f32[1,8,256]{2,1,0:T(8,128)S(1)} %get-tuple-element.79), channel_id=1, source_target_pairs={{0,8},{8,16},{16,24},{24,32},{32,40},{40,48},{48,56},{56,64},{64,7... | collective-permute-start | bytes 24584 | tf_op jit(solution)/shard_map/ppermute | solution.py:31
  212.9 9.2 %collective-permute-start.29 = (f32[1,8,256]{2,1,0:T(8,128)S(1)}, f32[1,8,256]{2,1,0:T(8,128)S(1)}, u32[]{:S(2)}, u32[]{:S(2)}) collective-permute-start(f32[1,8,256]{2,1,0:T(8,128)S(1)} %get-tuple-element.77), channel_id=1, source_target_pairs={{0,8},{8,16},{16,24},{24,32},{32,40},{40,48},{48,56},{56,64},{64,7... | collective-permute-start | bytes 24584 | tf_op jit(solution)/shard_map/ppermute | solution.py:31
  222.1 17.4 %collective-permute-start.31 = (f32[10,1,256]{2,1,0:T(1,128)S(1)}, f32[10,1,256]{2,1,0:T(1,128)S(1)}, u32[]{:S(2)}, u32[]{:S(2)}) collective-permute-start(f32[10,1,256]{2,1,0:T(1,128)S(1)} %get-tuple-element.59), channel_id=1, source_target_pairs={{0,1},{1,2},{2,3},{3,4},{4,5},{5,6},{6,7},{8,9},{9,10},{10,11},{11... | collective-permute-start | bytes 30728 | tf_op jit(solution)/shard_map/ppermute | solution.py:31
  226.0 13.5 %collective-permute-start.30 = (f32[10,1,256]{2,1,0:T(1,128)S(1)}, f32[10,1,256]{2,1,0:T(1,128)S(1)}, u32[]{:S(2)}, u32[]{:S(2)}) collective-permute-start(f32[10,1,256]{2,1,0:T(1,128)S(1)} %get-tuple-element.58), channel_id=1, source_target_pairs={{1,0},{2,1},{3,2},{4,3},{5,4},{6,5},{7,6},{9,8},{10,9},{11,10},{12... | collective-permute-start | bytes 30728 | tf_op jit(solution)/shard_map/ppermute | solution.py:32
  239.7 17.0 %collective-permute-start.32 = (f32[1,8,256]{2,1,0:T(8,128)S(1)}, f32[1,8,256]{2,1,0:T(8,128)S(1)}, u32[]{:S(2)}, u32[]{:S(2)}) collective-permute-start(f32[1,8,256]{2,1,0:T(8,128)S(1)} %get-tuple-element.76), channel_id=1, source_target_pairs={{8,0},{16,8},{24,16},{32,24},{40,32},{48,40},{56,48},{64,56},{72,6... | collective-permute-start | bytes 24584 | tf_op jit(solution)/shard_map/ppermute | solution.py:32
  241.6 15.1 %collective-permute-start.33 = (f32[1,8,256]{2,1,0:T(8,128)S(1)}, f32[1,8,256]{2,1,0:T(8,128)S(1)}, u32[]{:S(2)}, u32[]{:S(2)}) collective-permute-start(f32[1,8,256]{2,1,0:T(8,128)S(1)} %get-tuple-element.75), channel_id=1, source_target_pairs={{0,8},{8,16},{16,24},{24,32},{32,40},{40,48},{48,56},{56,64},{64,7... | collective-permute-start | bytes 24584 | tf_op jit(solution)/shard_map/ppermute | solution.py:31
  244.0 76.1 %collective-permute-start.47 = (f32[5,1,512]{0,2,1:T(8,128)S(1)}, f32[5,1,512]{0,2,1:T(8,128)S(1)}, u32[]{:S(2)}, u32[]{:S(2)}) collective-permute-start(f32[5,1,512]{0,2,1:T(8,128)S(1)} %slice_bitcast_fusion.5), channel_id=1, source_target_pairs={{1,0},{2,1},{3,2},{4,3},{5,4},{6,5},{7,6},{9,8},{10,9},{11,10},{12... | collective-permute-start | bytes 30728 | tf_op jit(solution)/shard_map/ppermute | solution.py:40
  257.3 23.0 %collective-permute-start.35 = (f32[10,1,256]{2,1,0:T(1,128)}, f32[10,1,256]{2,1,0:T(1,128)S(1)}, u32[]{:S(2)}, u32[]{:S(2)}) collective-permute-start(f32[10,1,256]{2,1,0:T(1,128)} %get-tuple-element.57), channel_id=1, source_target_pairs={{0,1},{1,2},{2,3},{3,4},{4,5},{5,6},{6,7},{8,9},{9,10},{10,11},{11... | collective-permute-start | bytes 30728 | tf_op jit(solution)/shard_map/ppermute | solution.py:31
  262.1 18.2 %collective-permute-start.34 = (f32[10,1,256]{2,1,0:T(1,128)}, f32[10,1,256]{2,1,0:T(1,128)}, u32[]{:S(2)}, u32[]{:S(2)}) collective-permute-start(f32[10,1,256]{2,1,0:T(1,128)} %get-tuple-element.56), channel_id=1, source_target_pairs={{1,0},{2,1},{3,2},{4,3},{5,4},{6,5},{7,6},{9,8},{10,9},{11,10},{12... | collective-permute-start | bytes 30728 | tf_op jit(solution)/shard_map/ppermute | solution.py:32
  264.7 64.1 %collective-permute-start.46 = (f32[5,1,512]{0,2,1:T(8,128)}, f32[5,1,512]{0,2,1:T(8,128)}, u32[]{:S(2)}, u32[]{:S(2)}) collective-permute-start(f32[5,1,512]{0,2,1:T(8,128)} %slice_bitcast_fusion.6), channel_id=1, source_target_pairs={{0,1},{1,2},{2,3},{3,4},{4,5},{5,6},{6,7},{8,9},{9,10},{10,11},{11... | collective-permute-start | bytes 30728 | tf_op jit(solution)/shard_map/ppermute | solution.py:40
  281.1 27.7 %collective-permute-start.36 = (f32[1,8,256]{2,1,0:T(8,128)S(1)}, f32[1,8,256]{2,1,0:T(8,128)S(1)}, u32[]{:S(2)}, u32[]{:S(2)}) collective-permute-start(f32[1,8,256]{2,1,0:T(8,128)S(1)} %get-tuple-element.74), channel_id=1, source_target_pairs={{8,0},{16,8},{24,16},{32,24},{40,32},{48,40},{56,48},{64,56},{72,6... | collective-permute-start | bytes 24584 | tf_op jit(solution)/shard_map/ppermute | solution.py:32
  287.6 21.2 %collective-permute-start.37 = (f32[1,8,256]{2,1,0:T(8,128)S(1)}, f32[1,8,256]{2,1,0:T(8,128)S(1)}, u32[]{:S(2)}, u32[]{:S(2)}) collective-permute-start(f32[1,8,256]{2,1,0:T(8,128)S(1)} %get-tuple-element.73), channel_id=1, source_target_pairs={{0,8},{8,16},{16,24},{24,32},{32,40},{40,48},{48,56},{56,64},{64,7... | collective-permute-start | bytes 24584 | tf_op jit(solution)/shard_map/ppermute | solution.py:31
  290.3 39.6 %collective-permute-start.45 = (f32[5,1,512]{0,2,1:T(8,128)}, f32[5,1,512]{0,2,1:T(8,128)}, u32[]{:S(2)}, u32[]{:S(2)}) collective-permute-start(f32[5,1,512]{0,2,1:T(8,128)} %slice_bitcast_fusion.7), channel_id=1, source_target_pairs={{8,0},{16,8},{24,16},{32,24},{40,32},{48,40},{56,48},{64,56},{72,6... | collective-permute-start | bytes 30728 | tf_op jit(solution)/shard_map/ppermute | solution.py:40
  314.7 16.2 %collective-permute-start.44 = (f32[5,1,512]{0,2,1:T(8,128)S(1)}, f32[5,1,512]{0,2,1:T(8,128)S(1)}, u32[]{:S(2)}, u32[]{:S(2)}) collective-permute-start(f32[5,1,512]{0,2,1:T(8,128)S(1)} %slice_bitcast_fusion.8), channel_id=1, source_target_pairs={{0,8},{8,16},{16,24},{24,32},{32,40},{40,48},{48,56},{56,64},{64,7... | collective-permute-start | bytes 30728 | tf_op jit(solution)/shard_map/ppermute | solution.py:40
  318.2 12.9 %collective-permute-start.41 = (f32[1,8,256]{2,1,0:T(8,128)S(1)}, f32[1,8,256]{2,1,0:T(8,128)S(1)}, u32[]{:S(2)}, u32[]{:S(2)}) collective-permute-start(f32[1,8,256]{2,1,0:T(8,128)S(1)} %get-tuple-element.71), channel_id=1, source_target_pairs={{0,8},{8,16},{16,24},{24,32},{32,40},{40,48},{48,56},{56,64},{64,7... | collective-permute-start | bytes 24584 | tf_op jit(solution)/shard_map/ppermute | solution.py:31
  320.1 11.0 %collective-permute-start.40 = (f32[1,8,256]{2,1,0:T(8,128)S(1)}, f32[1,8,256]{2,1,0:T(8,128)S(1)}, u32[]{:S(2)}, u32[]{:S(2)}) collective-permute-start(f32[1,8,256]{2,1,0:T(8,128)S(1)} %get-tuple-element.72), channel_id=1, source_target_pairs={{8,0},{16,8},{24,16},{32,24},{40,32},{48,40},{56,48},{64,56},{72,6... | collective-permute-start | bytes 24584 | tf_op jit(solution)/shard_map/ppermute | solution.py:32
  331.1 6.6 %collective-permute-start.43 = (f32[10,1,256]{2,1,0:T(1,128)S(1)}, f32[10,1,256]{2,1,0:T(1,128)S(1)}, u32[]{:S(2)}, u32[]{:S(2)}) collective-permute-start(f32[10,1,256]{2,1,0:T(1,128)S(1)} %get-tuple-element.53), channel_id=1, source_target_pairs={{0,1},{1,2},{2,3},{3,4},{4,5},{5,6},{6,7},{8,9},{9,10},{10,11},{11... | collective-permute-start | bytes 30728 | tf_op jit(solution)/shard_map/ppermute | solution.py:31
  334.0 6.5 %collective-permute-start.42 = (f32[10,1,256]{2,1,0:T(1,128)S(1)}, f32[10,1,256]{2,1,0:T(1,128)S(1)}, u32[]{:S(2)}, u32[]{:S(2)}) collective-permute-start(f32[10,1,256]{2,1,0:T(1,128)S(1)} %get-tuple-element.52), channel_id=1, source_target_pairs={{1,0},{2,1},{3,2},{4,3},{5,4},{6,5},{7,6},{9,8},{10,9},{11,10},{12... | collective-permute-start | bytes 30728 | tf_op jit(solution)/shard_map/ppermute | solution.py:32
  (26 other events, 237.3 us)
where the time goes:
time: 343 us; the launch traced here: 341 us
  starting transfers between devices  156 us (45%)
  local copies, waits for them, and re-layouts  77.4 us (23%)
  waiting for transfers between devices  58 us (17%)
  other arithmetic  48.1 us (14%)
    ppermute x22, starting transfers between devices, padded_2(): after = lax.ppermute(leading, axis, down)  76.1 us
    ppermute x22, starting transfers between devices, padded_2(): before = lax.ppermute(last, axis, up)  63.4 us
    scatter x4, local copies, waits for them, and re-layouts, body(): parcel = jnp.zeros((5, CAP + 1), jnp.float32).at[:, place].set(renewed)  42.7 us
    ppermute x22, waiting for transfers between devices, padded_2(): before = lax.ppermute(last, axis, up)  40.2 us
    scatter-add x1, other arithmetic, body(): sources = jnp.zeros((3, volume), jnp.float32).at[:, cells].add(drop_sources)  26.1 us
    ppermute x22, waiting for transfers between devices, padded_2(): after = lax.ppermute(leading, axis, down)  17.9 us
    ppermute x4, starting transfers between devices, shifted(): return lax.ppermute(shard, axis, pairs)  16.5 us
    gather x2, local copies, waits for them, and re-layouts, body(): local = flat[:, cells]  14.8 us
  transfers between devices with their start and end apart: 48, of which 13 were waited for; matrix products, arithmetic and copies ran while one was open for 36% of the time, Pallas kernels for 0%

commit v1 on v0

v1 whole, which is shorter than its diff:
```python
import functools

import jax
import jax.numpy as jnp
from jax import lax
from jax.experimental import pallas as pl
from jax.experimental.pallas import tpu as pltpu
from jax.sharding import PartitionSpec as P

B = 8
NZ = 256
PD = 4096
CAP = 512
CHUNK = 512
F32 = jnp.float32
BF16 = jnp.bfloat16
VMEM = pl.BlockSpec(memory_space=pltpu.VMEM)
SMEM = pl.BlockSpec(memory_space=pltpu.SMEM)

Y_LAYERS = [(1, 0), (1, 1), (1, 2), (0, 0), (0, 1), (2, 0), (2, 1), (3, 0), (3, 1), (4, 0), (4, 1), (5, 0)]
X_LAYERS = [(0, 0), (0, 1), (0, 2), (1, 0), (1, 1), (2, 0), (2, 1), (3, 0), (3, 1), (4, 0), (4, 1), (5, 0)]
NL = 12


def params(limit=16):
    return pltpu.CompilerParams(vmem_limit_bytes=limit * 1024 * 1024)


def tiles(n):
    return jax.ShapeDtypeStruct((n, B, NZ), F32)


def call(kernel, outs, n_in, cost, scratch=(), smem=(), limit=16):
    return pl.pallas_call(
        kernel,
        out_shape=outs,
        in_specs=[SMEM if i in smem else VMEM for i in range(n_in)],
        out_specs=[VMEM] * len(outs),
        scratch_shapes=list(scratch),
        compiler_params=params(limit),
        cost_estimate=pl.CostEstimate(flops=cost, bytes_accessed=cost // 8, transcendentals=0),
    )


def pack_y_kernel(gas, guess, low, high):
    for r, (field, depth) in enumerate(Y_LAYERS):
        for side, y in ((low, depth), (high, B - 1 - depth)):
            side[r] = guess[:, y, :] if field == 5 else gas[field, :, y, :]


def split(value):
    high = value.astype(BF16).astype(F32)
    return high, value - high


def droplet_kernel(gas, motion, size, cell, target, on, when, head, sources, kept, parcels):
    table = jnp.concatenate([gas[f].reshape(B * B, NZ) for f in range(4)], axis=0)
    high, low = split(table)
    table = jnp.concatenate([high.astype(BF16), low.astype(BF16)], axis=1)
    at_z = lax.broadcasted_iota(jnp.int32, (NZ, CHUNK), 0)
    at_xy = lax.broadcasted_iota(jnp.int32, (B * B, CHUNK), 0)
    at_high = lax.broadcasted_iota(jnp.int32, (B, CHUNK), 0)
    heading = lax.broadcasted_iota(jnp.int32, (B, CHUNK), 0)
    a = lax.broadcasted_iota(jnp.int32, (CHUNK, CHUNK), 0)
    b = lax.broadcasted_iota(jnp.int32, (CHUNK, CHUNK), 1)
    upper = jnp.where(a <= b, 1.0, 0.0).astype(BF16)
    before = jnp.zeros((B, 1), F32)
    total = jnp.zeros((4 * B * B, NZ), F32)
    moved = jnp.zeros((10 * B, NZ), F32)
    across = (((1,), (1,)), ((), ()))
    for n in range(PD // CHUNK):
        part = slice(n * CHUNK, (n + 1) * CHUNK)
        cells = cell[:, part]
        goal = target[:, part]
        in_z = jnp.where(at_z == (cells & (NZ - 1)), 1.0, 0.0).astype(BF16)
        in_xy = at_xy == (cells >> 8)
        found = jnp.dot(table, jnp.concatenate([in_z, in_z], axis=0), preferred_element_type=F32)
        local = [
            jnp.sum(jnp.where(in_xy, found[f * B * B : (f + 1) * B * B], 0.0), axis=0, keepdims=True)
            for f in range(4)
        ]
        u, v, w, temperature = (motion[f, :, part] for f in range(4))
        diameter = size[:, part]
        excess = local[3] - temperature
        vapour = 0.5 * diameter * jax.nn.sigmoid(excess)
        renewed = [
            u + 0.4 * (local[0] - u),
            v + 0.4 * (local[1] - v),
            w + 0.2 * ((local[2] - w) * 2.0 - 1.0),
            temperature + 0.2 * excess,
            diameter - 0.2 * vapour,
        ]
        drag = 0.5 * diameter * diameter * (w - local[2])
        alive = goal >= 0
        for f in range(5):
            kept[f, :, part] = jnp.where(goal == 4, renewed[f], 0.0)
        pieces = [*split(jnp.where(alive, drag, 0.0)), *split(jnp.where(alive, vapour, 0.0))]
        given = jnp.concatenate([jnp.where(in_xy, piece, 0.0).astype(BF16) for piece in pieces], axis=0)
        total = total + lax.dot_general(given, in_z, across, preferred_element_type=F32)
        chosen = heading == goal
        rank = jnp.dot(jnp.where(chosen, 1.0, 0.0).astype(BF16), upper, preferred_element_type=F32) + before
        before = rank[:, CHUNK - 1 :]
        place = (rank - 1.0).astype(jnp.int32) + heading * CAP
        leaves = chosen & (heading < 4)
        place = jnp.sum(jnp.where(leaves, place + 1, 0), axis=0, keepdims=True) - 1
        in_low = jnp.where(at_z == (place & (NZ - 1)), 1.0, 0.0).astype(BF16)
        in_high = at_high == (place >> 8)
        split_up = [split(value) for value in renewed]
        rows = [jnp.where(in_high, split_up[f][piece], 0.0) for piece in range(2) for f in range(5)]
        moved = moved + lax.dot_general(
            jnp.concatenate(rows, axis=0).astype(BF16), in_low, across, preferred_element_type=F32
        )
    q = B * B
    steam = total[2 * q : 3 * q] + total[3 * q :]
    sources[0] = total[:q] + total[q : 2 * q]
    sources[1] = -2.0 * steam
    sources[2] = steam
    lanes = lax.broadcasted_iota(jnp.int32, (1, NZ), 1)
    for s in range(B):
        ramp = jnp.clip((100.0 - when[0, s].astype(F32)) / 50.0, 0.0, 1.0)
        strength = 3.0 * ramp * on[0, s].astype(F32)
        where = head[0, s]
        row = pl.ds(where >> 8, 1)
        taken = jnp.where(lanes == (where & (NZ - 1)), strength, 0.0)
        for f in range(2):
            sources[f, row, :] = sources[f, row, :] - taken
    moved = moved[: 5 * B] + moved[5 * B :]
    for d in range(4):
        for f in range(5):
            for half in range(2):
                at = f * B + 2 * d + half
                r = 2 * f + half
                parcels[d, r // B, r % B : r % B + 1, :] = moved[at : at + 1]
        parcels[d, 1, 2:, :] = jnp.zeros((B - 2, NZ), F32)


def pack_x_kernel(gas, guess, below, above, parcels, low, high):
    for side, near, step, heading in ((low, 0, 1, 1), (high, B - 1, -1, 0)):
        for r, (field, depth) in enumerate(X_LAYERS):
            x = near + step * depth
            side[r] = guess[x] if field == 5 else gas[field, x]
        for h, halo in enumerate((below, above)):
            for r, (layer, x) in enumerate(((3, near), (4, near), (0, near), (0, near + step))):
                side[NL, 4 * h + r : 4 * h + r + 1, :] = halo[layer, x : x + 1, :]
        side[NL + 1] = parcels[heading, 0]
        side[NL + 2] = parcels[heading, 1]


def beside(value, by):
    lane = lax.broadcasted_iota(jnp.int32, value.shape, 1)
    turned = pltpu.roll(value, (-by) % NZ, axis=1)
    return jnp.where((lane < NZ - by) if by > 0 else (lane >= -by), turned, 0.0)


def advance(e, f, x, rows, first):
    def at(field, dx, dy):
        return e[field, x + dx, first + dy : first + dy + rows, :]

    centre = at(f, 0, 0)
    xs = {s: at(f, s, 0) for s in (-2, -1, 1, 2)}
    ys = {s: at(f, 0, s) for s in (-2, -1, 1, 2)}
    zs = {s: beside(centre, s) for s in (-2, -1, 1, 2)}
    laplace = xs[1] + xs[-1] + ys[1] + ys[-1] + zs[1] + zs[-1] - 6.0 * centre
    transport = 0.0
    for axis, shifted in enumerate((xs, ys, zs)):
        slope = 8.0 * (shifted[1] - shifted[-1]) - (shifted[2] - shifted[-2])
        transport = transport + at(axis, 0, 0) * slope
    return centre + (0.02 * laplace - (0.2 / 12.0) * transport)


def predict_kernel(gas, guess, below, above, left, right, sources, parcels, star, up, down, e, wide, tall, q):
    gx = lax.axis_index("gx")
    gy = lax.axis_index("gy")
    has_left, has_right = gx > 0, gx < lax.axis_size("gx") - 1
    has_below, has_above = gy > 0, gy < lax.axis_size("gy") - 1
    for f in range(5):
        e[f, 3 : 3 + B, B : 2 * B, :] = gas[f]
    q[1 : 1 + B, B : 2 * B, :] = guess[...]
    for r, (field, depth) in enumerate(Y_LAYERS):
        for halo, y in ((below, B - 1 - depth), (above, 2 * B + depth)):
            if field == 5:
                q[1 : 1 + B, y, :] = halo[r]
            else:
                e[field, 3 : 3 + B, y, :] = halo[r]
    for r, (field, depth) in enumerate(X_LAYERS):
        for halo, x in ((left, -1 - depth), (right, B + depth)):
            if field == 5:
                q[x + 1, B : 2 * B, :] = halo[r]
            else:
                e[field, x + 3, B : 2 * B, :] = halo[r]
    for halo, near, step in ((left, 2, -1), (right, 3 + B, 1)):
        for h, (y, onward) in enumerate(((B - 1, -1), (2 * B, 1))):
            spots = ((0, near, y), (0, near, y + onward), (1, near, y), (1, near + step, y))
            for r, (field, x, row) in enumerate(spots):
                e[field, x, row : row + 1, :] = halo[NL, 4 * h + r : 4 * h + r + 1, :]
    for x in range(-1, B + 1):
        value = advance(e, 0, x + 3, B, B)
        if x < 0:
            value = jnp.where(has_left, value, 0.0)
        if x == B:
            value = jnp.where(has_right, value, 0.0)
        wide[x + 1] = value
        if 0 <= x < B:
            star[0, x] = value
    for x in range(B):
        value = advance(e, 1, x + 3, B + 2, B - 1)
        row = lax.broadcasted_iota(jnp.int32, value.shape, 0)
        inside = ((row > 0) | has_below) & ((row < B + 1) | has_above)
        value = jnp.where(inside, value, 0.0)
        tall[x, : B + 2, :] = value
        star[1, x] = value[1 : 1 + B]
    for f in (3, 4):
        for x in range(B):
            star[f, x] = advance(e, f, x + 3, B, B) + 0.2 * sources[f - 2, x]
    for x in range(B):
        w = advance(e, 2, x + 3, B, B) + 0.2 * sources[0, x]
        star[2, x] = w
        spread = wide[x + 2] - wide[x] + (tall[x, 2 : 2 + B, :] - tall[x, :B, :])
        source = 2.5 * (spread + (beside(w, 1) - beside(w, -1)))
        centre = q[x + 1, B : 2 * B, :]
        around = q[x + 2, B : 2 * B, :] + q[x, B : 2 * B, :]
        around = around + q[x + 1, B + 1 : 2 * B + 1, :] + q[x + 1, B - 1 : 2 * B - 1, :]
        field = (around + beside(centre, 1) + beside(centre, -1) - source) * (1.0 / 6.0)
        for side in (up, down):
            side[x] = field
            side[B + x] = source
    for side, heading in ((up, 2), (down, 3)):
        side[2 * B] = parcels[heading, 0]
        side[2 * B + 1] = parcels[heading, 1]


NX2 = 28


def pack_x2_kernel(own, below, above, low, high):
    row = lax.broadcasted_iota(jnp.int32, (B, NZ), 0)
    for side, near, step in ((low, -1, 1), (high, B, -1)):
        for d in range(1, B + 1):
            side[d - 1] = own[near + step * d]
        for m in range(1, B):
            lower = below[near + step * m]
            upper = above[near + step * (B - m)]
            side[B - 1 + m] = jnp.where(row >= m, lower, upper)
        base = 2 * B - 1
        for d in range(1, B):
            side[base + d - 1] = own[B + near + step * d]
        for m in range(1, B - 1):
            lower = below[B + near + step * m]
            upper = above[B + near + step * (B - 1 - m)]
            side[base + B - 2 + m] = jnp.where(row >= m + 1, lower, upper)


def finish_kernel(star, own, below, above, left, right, early_left, early_right, gas_next, pressure, arrived, p0, p1, s, c):
    gx = lax.axis_index("gx")
    gy = lax.axis_index("gy")
    inside_x = [gx > 0, None, gx < lax.axis_size("gx") - 1]
    inside_y = [gy > 0, None, gy < lax.axis_size("gy") - 1]
    for i in range(3):
        for j in range(3):
            value = jnp.full((B, NZ), 1.0 / 6.0, F32)
            for flag in (inside_x[i], inside_y[j]):
                if flag is not None:
                    value = jnp.where(flag, value, 0.0)
            c[i, j * B : (j + 1) * B, :] = value
    for x in range(B):
        for k, halo in enumerate((below, own, above)):
            p0[B + x, k * B : (k + 1) * B, :] = halo[x]
            s[B + x, k * B : (k + 1) * B, :] = halo[B + x]
    base = 2 * B - 1
    for halo, near, step in ((left, B, -1), (right, 2 * B - 1, 1)):
        for d in range(1, B + 1):
            p0[near + step * d, B : 2 * B, :] = halo[d - 1]
            if d < B:
                s[near + step * d, B : 2 * B, :] = halo[base + d - 1]
        for m in range(1, B):
            piece = halo[B - 1 + m]
            p0[near + step * m, :B, :] = piece
            p0[near + step * (B - m), 2 * B :, :] = piece
        for m in range(1, B - 1):
            piece = halo[base + B - 2 + m]
            s[near + step * m, :B, :] = piece
            s[near + step * (B - 1 - m), 2 * B :, :] = piece
        p0[near + step * B, :B, :] = halo[0]
        p0[near + step * B, 2 * B :, :] = halo[0]
        s[near + step * (B - 1), :B, :] = halo[0]
        s[near + step * (B - 1), 2 * B :, :] = halo[0]
    now, later = p0, p1
    for turn in range(2, 9):
        reach = 9 - turn
        for x in range(B - reach, 2 * B + reach):
            centre = now[x]
            around = now[x - 1] + now[x + 1]
            around = around + pltpu.roll(centre, 1, axis=0) + pltpu.roll(centre, 3 * B - 1, axis=0)
            around = around + beside(centre, 1) + beside(centre, -1)
            later[x] = (around - s[x]) * c[0 if x < B else (1 if x < 2 * B else 2)]
        now, later = later, now
    for x in range(B):
        centre = now[B + x, B : 2 * B, :]
        pressure[x] = centre
        gas_next[0, x] = star[0, x] - 0.1 * (now[B + x + 1, B : 2 * B, :] - now[B + x - 1, B : 2 * B, :])
        gas_next[1, x] = star[1, x] - 0.1 * (now[B + x, B + 1 : 2 * B + 1, :] - now[B + x, B - 1 : 2 * B - 1, :])
        gas_next[2, x] = star[2, x] - 0.1 * (beside(centre, 1) - beside(centre, -1))
        gas_next[3, x] = star[3, x]
        gas_next[4, x] = star[4, x]
    for d, (halo, base) in enumerate(((early_left, NL + 1), (early_right, NL + 1), (below, 2 * B), (above, 2 * B))):
        for f in range(5):
            for half in range(2):
                r = 2 * f + half
                arrived[d, f, :, half * NZ : (half + 1) * NZ] = halo[base + r // B, r % B : r % B + 1, :]


def shifted(shard, axis, by):
    peers = lax.axis_size(axis)
    pairs = [(i, i + by) for i in range(peers) if 0 <= i + by < peers]
    return lax.ppermute(shard, axis, pairs)


def body(gas, guess, motion, size, cell, target, on, when, head):
    low, high = call(pack_y_kernel, [tiles(NL)] * 2, 2, 10**6)(gas, guess)
    below = shifted(high, "gy", 1)
    above = shifted(low, "gy", -1)
    sources, kept, parcels = call(
        droplet_kernel,
        [
            jax.ShapeDtypeStruct((3, B * B, NZ), F32),
            jax.ShapeDtypeStruct((5, 1, PD), F32),
            jax.ShapeDtypeStruct((4, 2, B, NZ), F32),
        ],
        8,
        10**9,
        smem=(5, 6, 7),
    )(gas, motion, size, cell, target, on, when, head)
    low, high = call(pack_x_kernel, [tiles(NL + 3)] * 2, 5, 10**6)(gas, guess, below, above, parcels)
    left = shifted(high, "gx", 1)
    right = shifted(low, "gx", -1)
    star, up, down = call(
        predict_kernel,
        [jax.ShapeDtypeStruct((5, B, B, NZ), F32), tiles(2 * B + 2), tiles(2 * B + 2)],
        8,
        10**7,
        scratch=[
            pltpu.VMEM((5, B + 6, 3 * B, NZ), F32),
            pltpu.VMEM((B + 2, B, NZ), F32),
            pltpu.VMEM((B, 2 * B, NZ), F32),
            pltpu.VMEM((B + 2, 3 * B, NZ), F32),
        ],
    )(gas, guess, below, above, left, right, sources.reshape(3, B, B, NZ), parcels)
    below = shifted(up, "gy", 1)
    above = shifted(down, "gy", -1)
    low, high = call(pack_x2_kernel, [tiles(NX2)] * 2, 3, 10**6)(up, below, above)
    far_left = shifted(high, "gx", 1)
    far_right = shifted(low, "gx", -1)
    gas_next, pressure, arrived = call(
        finish_kernel,
        [
            jax.ShapeDtypeStruct((5, B, B, NZ), F32),
            jax.ShapeDtypeStruct((B, B, NZ), F32),
            jax.ShapeDtypeStruct((4, 5, 1, CAP), F32),
        ],
        8,
        10**7,
        scratch=[
            pltpu.VMEM((3 * B, 3 * B, NZ), F32),
            pltpu.VMEM((3 * B, 3 * B, NZ), F32),
            pltpu.VMEM((3 * B, 3 * B, NZ), F32),
            pltpu.VMEM((3, 3 * B, NZ), F32),
        ],
    )(star, up, below, above, far_left, far_right, left, right)
    return gas_next, pressure, kept, arrived


def solution(mesh):
    in_specs = (
        P(None, "gx", "gy", None),
        P("gx", "gy", None),
        P(None, "gx", "gy"),
        P("gx", "gy"),
        P("gx", "gy"),
        P("gx", "gy"),
        P("gx", "gy"),
        P("gx", "gy"),
        P("gx", "gy"),
    )
    out_specs = (
        P(None, "gx", "gy", None),
        P("gx", "gy", None),
        P(None, "gx", "gy"),
        P(None, None, "gx", "gy"),
    )
    return jax.shard_map(body, mesh=mesh, in_specs=in_specs, out_specs=out_specs, check_vma=False)
```

time: 343 us -> 60.8 us (0.18)
  the two profiles are of different devices: /device:TPU:40 before, /device:TPU:50 now
where the time goes in v1:
time: 60.8 us; the launch traced here: 60.3 us
  starting transfers between devices  34.7 us (57%)
  waiting for transfers between devices  13.9 us (23%)
  Pallas kernels  9.04 us (15%)
  local copies, waits for them, and re-layouts  1.84 us (3%)
  between operations  0.83 us (1%)
    ppermute x8, starting transfers between devices, shifted(): return lax.ppermute(shard, axis, pairs)  34.7 us
    ppermute x8, waiting for transfers between devices, shifted(): return lax.ppermute(shard, axis, pairs)  13.9 us
    pallas_call x1, Pallas kernels, body(): call(droplet_kernel, [jax.ShapeDtypeStruct((3, B * B, NZ), F32), jax.Shap...  5.28 us
    pallas_call x1, Pallas kernels, body(): call(finish_kernel, [jax.ShapeDtypeStruct((5, B, B, NZ), F32), jax.ShapeD...  2.36 us
    unnamed x20, local copies, waits for them, and re-layouts  1.84 us
    pallas_call x1, Pallas kernels, body(): call(predict_kernel, [jax.ShapeDtypeStruct((5, B, B, NZ), F32), tiles(2 *...  1.27 us
  transfers between devices with their start and end apart: 8, of which 6 were waited for; matrix products, arithmetic and copies ran while one was open for 0% of the time, Pallas kernels for 9%

profile of v1, /device:TPU:50, one launch (start us, length us, event | category | flops | bytes accessed | tf_op | source)
XLA Modules:
  0.0 60.3 jit_solution(11751483746930130843)
XLA Ops:
  0.6 1.0 %copy-done = f32[5,8,8,256]{3,2,1,0:T(8,128)S(1)} copy-done((f32[5,8,8,256]{3,2,1,0:T(8,128)S(1)}, f32[5,8,8,256]{3,2,1,0:T(8,128)}, u32[]{:S(2)}) %copy-start) | copy-done | bytes 327704
  1.6 0.8 %copy-done.1 = f32[8,8,256]{2,1,0:T(8,128)S(1)} copy-done((f32[8,8,256]{2,1,0:T(8,128)S(1)}, f32[8,8,256]{2,1,0:T(8,128)}, u32[]{:S(2)}) %copy-start.1) | copy-done | bytes 65560
  2.5 0.1 shard_map.120
  2.5 0.0 copy-start.7
  2.5 0.0 copy-start.8
  2.6 0.0 copy-start.9
  2.6 2.7 %collective-permute-start = (f32[12,8,256]{2,1,0:T(8,128)S(1)}, f32[12,8,256]{2,1,0:T(8,128)S(1)}, u32[]{:S(2)}, u32[]{:S(2)}) collective-permute-start(f32[12,8,256]{2,1,0:T(8,128)S(1)} %get-tuple-element.19), channel_id=1, source_target_pairs={{0,1},{1,2},{2,3},{3,4},{4,5},{5,6},{6,7},{8,9},{9,10},{10,11},{11... | collective-permute-start | bytes 294920 | tf_op jit(solution)/shard_map/ppermute | solution.py:315
  5.3 0.0 copy-start.2
  5.3 4.3 %collective-permute-start.1 = (f32[12,8,256]{2,1,0:T(8,128)S(1)}, f32[12,8,256]{2,1,0:T(8,128)S(1)}, u32[]{:S(2)}, u32[]{:S(2)}) collective-permute-start(f32[12,8,256]{2,1,0:T(8,128)S(1)} %get-tuple-element.20), channel_id=1, source_target_pairs={{1,0},{2,1},{3,2},{4,3},{5,4},{6,5},{7,6},{9,8},{10,9},{11,10},{12... | collective-permute-start | bytes 294920 | tf_op jit(solution)/shard_map/ppermute | solution.py:315
  9.6 0.0 copy-done.3
  9.6 0.0 copy-done.4
  9.6 0.0 copy-done.5
  9.6 0.0 copy-done.6
  9.6 0.0 copy-done.7
  9.7 0.0 copy-done.8
  9.7 5.3 %shard_map.121 = (f32[3,64,256]{2,1,0:T(8,128)S(1)}, f32[5,1,4096]{2,1,0:T(1,128)}, f32[4,2,8,256]{3,2,1,0:T(8,128)S(1)}) custom-call(f32[5,8,8,256]{3,2,1,0:T(8,128)S(1)} %copy-done, f32[4,1,4096]{2,1,0:T(1,128)S(1)} %copy-done.3, f32[1,4096]{1,0:T(1,128)S(1)} %copy-done.4, s32[1,4096]{1,0:T(1,128)S(1)} %copy-done.5, s32[1,4096]{1,0:T(1,128)S(1)} %copy-done.6, ...), custom_call_target="tpu_custom_call" | custom-call | flops 1000000000 | bytes 125000000 | tf_op jit(solution)/shard_map/pallas_call | solution.py:322
  15.0 0.0 collective-permute-done.below
  15.0 0.0 collective-permute-done.1.above
  15.0 1.9 %collective-permute-start.2 = (f32[15,8,256]{2,1,0:T(8,128)S(1)}, f32[15,8,256]{2,1,0:T(8,128)S(1)}, u32[]{:S(2)}, u32[]{:S(2)}) collective-permute-start(f32[15,8,256]{2,1,0:T(8,128)S(1)} %get-tuple-element.22), channel_id=1, source_target_pairs={{0,8},{8,16},{16,24},{24,32},{32,40},{40,48},{48,56},{56,64},{64,7... | collective-permute-start | bytes 368648 | tf_op jit(solution)/shard_map/ppermute | solution.py:315
  16.9 11.4 %collective-permute-start.3 = (f32[15,8,256]{2,1,0:T(8,128)S(1)}, f32[15,8,256]{2,1,0:T(8,128)S(1)}, u32[]{:S(2)}, u32[]{:S(2)}) collective-permute-start(f32[15,8,256]{2,1,0:T(8,128)S(1)} %get-tuple-element.23), channel_id=1, source_target_pairs={{8,0},{16,8},{24,16},{32,24},{40,32},{48,40},{56,48},{64,56},{72,6... | collective-permute-start | bytes 368648 | tf_op jit(solution)/shard_map/ppermute | solution.py:315
  28.3 1.1 %collective-permute-done.2.left.early_left = f32[15,8,256]{2,1,0:T(8,128)S(1)} collective-permute-done((f32[15,8,256]{2,1,0:T(8,128)S(1)}, f32[15,8,256]{2,1,0:T(8,128)S(1)}, u32[]{:S(2)}, u32[]{:S(2)}) %collective-permute-start.2) | collective-permute-done | bytes 122912 | tf_op jit(solution)/shard_map/ppermute | solution.py:315
  29.4 2.4 %collective-permute-done.3.right.early_right = f32[15,8,256]{2,1,0:T(8,128)S(1)} collective-permute-done((f32[15,8,256]{2,1,0:T(8,128)S(1)}, f32[15,8,256]{2,1,0:T(8,128)S(1)}, u32[]{:S(2)}, u32[]{:S(2)}) %collective-permute-start.3) | collective-permute-done | bytes 122912 | tf_op jit(solution)/shard_map/ppermute | solution.py:315
  31.8 1.3 %shard_map.123 = (f32[5,8,8,256]{3,2,1,0:T(8,128)S(1)}, f32[18,8,256]{2,1,0:T(8,128)S(1)}, f32[18,8,256]{2,1,0:T(8,128)S(1)}) custom-call(f32[5,8,8,256]{3,2,1,0:T(8,128)S(1)} %copy-done, f32[8,8,256]{2,1,0:T(8,128)S(1)} %copy-done.2, f32[12,8,256]{2,1,0:T(8,128)S(1)} %collective-permute-done.below, f32[12,8,256]{2,1,0:T(8,128)S(1)} %collective-permute-done.1.above, ...), custom_call_target="tpu_custom_call" | custom-call | flops 10000000 | bytes 1250000 | tf_op jit(solution)/shard_map/pallas_call | solution.py:336
  33.1 2.3 %collective-permute-start.5 = (f32[18,8,256]{2,1,0:T(8,128)S(1)}, f32[18,8,256]{2,1,0:T(8,128)S(1)}, u32[]{:S(2)}, u32[]{:S(2)}) collective-permute-start(f32[18,8,256]{2,1,0:T(8,128)S(1)} %get-tuple-element.27), channel_id=1, source_target_pairs={{1,0},{2,1},{3,2},{4,3},{5,4},{6,5},{7,6},{9,8},{10,9},{11,10},{12... | collective-permute-start | bytes 442376 | tf_op jit(solution)/shard_map/ppermute | solution.py:315
  35.4 3.5 %collective-permute-start.4 = (f32[18,8,256]{2,1,0:T(8,128)S(1)}, f32[18,8,256]{2,1,0:T(8,128)S(1)}, u32[]{:S(2)}, u32[]{:S(2)}) collective-permute-start(f32[18,8,256]{2,1,0:T(8,128)S(1)} %get-tuple-element.26.own), channel_id=1, source_target_pairs={{0,1},{1,2},{2,3},{3,4},{4,5},{5,6},{6,7},{8,9},{9,10},{10,11},{11... | collective-permute-start | bytes 442376 | tf_op jit(solution)/shard_map/ppermute | solution.py:315
  39.0 1.2 %collective-permute-done.5.above = f32[18,8,256]{2,1,0:T(8,128)S(1)} collective-permute-done((f32[18,8,256]{2,1,0:T(8,128)S(1)}, f32[18,8,256]{2,1,0:T(8,128)S(1)}, u32[]{:S(2)}, u32[]{:S(2)}) %collective-permute-start.5) | collective-permute-done | bytes 147488 | tf_op jit(solution)/shard_map/ppermute | solution.py:315
  40.1 3.2 %collective-permute-done.4.below = f32[18,8,256]{2,1,0:T(8,128)S(1)} collective-permute-done((f32[18,8,256]{2,1,0:T(8,128)S(1)}, f32[18,8,256]{2,1,0:T(8,128)S(1)}, u32[]{:S(2)}, u32[]{:S(2)}) %collective-permute-start.4) | collective-permute-done | bytes 147488 | tf_op jit(solution)/shard_map/ppermute | solution.py:315
  43.4 1.9 %collective-permute-start.6 = (f32[28,8,256]{2,1,0:T(8,128)S(1)}, f32[28,8,256]{2,1,0:T(8,128)S(1)}, u32[]{:S(2)}, u32[]{:S(2)}) collective-permute-start(f32[28,8,256]{2,1,0:T(8,128)S(1)} %get-tuple-element.28), channel_id=1, source_target_pairs={{0,8},{8,16},{16,24},{24,32},{32,40},{40,48},{48,56},{56,64},{64,7... | collective-permute-start | bytes 688136 | tf_op jit(solution)/shard_map/ppermute | solution.py:315
  45.3 6.7 %collective-permute-start.7 = (f32[28,8,256]{2,1,0:T(8,128)S(1)}, f32[28,8,256]{2,1,0:T(8,128)S(1)}, u32[]{:S(2)}, u32[]{:S(2)}) collective-permute-start(f32[28,8,256]{2,1,0:T(8,128)S(1)} %get-tuple-element.29), channel_id=1, source_target_pairs={{8,0},{16,8},{24,16},{32,24},{40,32},{48,40},{56,48},{64,56},{72,6... | collective-permute-start | bytes 688136 | tf_op jit(solution)/shard_map/ppermute | solution.py:315
  52.0 4.2 %collective-permute-done.6.left = f32[28,8,256]{2,1,0:T(8,128)S(1)} collective-permute-done((f32[28,8,256]{2,1,0:T(8,128)S(1)}, f32[28,8,256]{2,1,0:T(8,128)S(1)}, u32[]{:S(2)}, u32[]{:S(2)}) %collective-permute-start.6) | collective-permute-done | bytes 229408 | tf_op jit(solution)/shard_map/ppermute | solution.py:315
  56.2 1.8 %collective-permute-done.7.right = f32[28,8,256]{2,1,0:T(8,128)S(1)} collective-permute-done((f32[28,8,256]{2,1,0:T(8,128)S(1)}, f32[28,8,256]{2,1,0:T(8,128)S(1)}, u32[]{:S(2)}, u32[]{:S(2)}) %collective-permute-start.7) | collective-permute-done | bytes 229408 | tf_op jit(solution)/shard_map/ppermute | solution.py:315
  58.0 2.4 %shard_map.125 = (f32[5,8,8,256]{3,2,1,0:T(8,128)}, f32[8,8,256]{2,1,0:T(8,128)}, f32[4,5,1,512]{3,2,1,0:T(1,128)}) custom-call(f32[5,8,8,256]{3,2,1,0:T(8,128)S(1)} %get-tuple-element.25.star, f32[18,8,256]{2,1,0:T(8,128)S(1)} %get-tuple-element.26.own, f32[18,8,256]{2,1,0:T(8,128)S(1)} %collective-permute-done.4.below, ...), custom_call_target="tpu_custom_call" | custom-call | flops 10000000 | bytes 1250000 | tf_op jit(solution)/shard_map/pallas_call | solution.py:353
  (10 shorter events, 0.1 us)
Async XLA Ops:
  0.6 1.0 %copy-start = (f32[5,8,8,256]{3,2,1,0:T(8,128)S(1)}, f32[5,8,8,256]{3,2,1,0:T(8,128)}, u32[]{:S(2)}) copy-start(f32[5,8,8,256]{3,2,1,0:T(8,128)} %gas.7) | copy-start | bytes 983044
  1.6 0.8 %copy-start.1 = (f32[8,8,256]{2,1,0:T(8,128)S(1)}, f32[8,8,256]{2,1,0:T(8,128)}, u32[]{:S(2)}) copy-start(f32[8,8,256]{2,1,0:T(8,128)} %guess.5) | copy-start | bytes 196612
  2.4 7.2 %copy-start.3 = (f32[4,1,4096]{2,1,0:T(1,128)S(1)}, f32[4,1,4096]{2,1,0:T(1,128)}, u32[]{:S(2)}) copy-start(f32[4,1,4096]{2,1,0:T(1,128)} %motion.1) | copy-start | bytes 196612
  2.4 7.2 %copy-start.4 = (f32[1,4096]{1,0:T(1,128)S(1)}, f32[1,4096]{1,0:T(1,128)}, u32[]{:S(2)}) copy-start(f32[1,4096]{1,0:T(1,128)} %size.1) | copy-start | bytes 49156
  2.5 7.2 %copy-start.5 = (s32[1,4096]{1,0:T(1,128)S(1)}, s32[1,4096]{1,0:T(1,128)}, u32[]{:S(2)}) copy-start(s32[1,4096]{1,0:T(1,128)} %cell.1) | copy-start | bytes 49156
  2.5 7.2 %copy-start.6 = (s32[1,4096]{1,0:T(1,128)S(1)}, s32[1,4096]{1,0:T(1,128)}, u32[]{:S(2)}) copy-start(s32[1,4096]{1,0:T(1,128)} %target.1) | copy-start | bytes 49156
  2.5 7.1 %copy-start.7 = (s32[1,8]{1,0:T(1,128)S(1)}, s32[1,8]{1,0:T(1,128)}, u32[]{:S(2)}) copy-start(s32[1,8]{1,0:T(1,128)} %on.1) | copy-start | bytes 100
  2.5 7.1 %copy-start.8 = (s32[1,8]{1,0:T(1,128)S(1)}, s32[1,8]{1,0:T(1,128)}, u32[]{:S(2)}) copy-start(s32[1,8]{1,0:T(1,128)} %when.1) | copy-start | bytes 100
  2.6 7.1 %copy-start.9 = (s32[1,8]{1,0:T(1,128)S(1)}, s32[1,8]{1,0:T(1,128)}, u32[]{:S(2)}) copy-start(s32[1,8]{1,0:T(1,128)} %head.1) | copy-start | bytes 100
  2.6 12.4 %collective-permute-start = (f32[12,8,256]{2,1,0:T(8,128)S(1)}, f32[12,8,256]{2,1,0:T(8,128)S(1)}, u32[]{:S(2)}, u32[]{:S(2)}) collective-permute-start(f32[12,8,256]{2,1,0:T(8,128)S(1)} %get-tuple-element.19), channel_id=1, source_target_pairs={{0,1},{1,2},{2,3},{3,4},{4,5},{5,6},{6,7},{8,9},{9,10},{10,11},{11... | collective-permute-start | bytes 294920 | tf_op jit(solution)/shard_map/ppermute | solution.py:315
  5.3 9.7 %copy-start.2 = (f32[8,8,256]{2,1,0:T(8,128)S(1)}, f32[8,8,256]{2,1,0:T(8,128)}, u32[]{:S(2)}) copy-start(f32[8,8,256]{2,1,0:T(8,128)} %guess.5) | copy-start | bytes 196612
  5.3 9.7 %collective-permute-start.1 = (f32[12,8,256]{2,1,0:T(8,128)S(1)}, f32[12,8,256]{2,1,0:T(8,128)S(1)}, u32[]{:S(2)}, u32[]{:S(2)}) collective-permute-start(f32[12,8,256]{2,1,0:T(8,128)S(1)} %get-tuple-element.20), channel_id=1, source_target_pairs={{1,0},{2,1},{3,2},{4,3},{5,4},{6,5},{7,6},{9,8},{10,9},{11,10},{12... | collective-permute-start | bytes 294920 | tf_op jit(solution)/shard_map/ppermute | solution.py:315
  15.0 14.4 %collective-permute-start.2 = (f32[15,8,256]{2,1,0:T(8,128)S(1)}, f32[15,8,256]{2,1,0:T(8,128)S(1)}, u32[]{:S(2)}, u32[]{:S(2)}) collective-permute-start(f32[15,8,256]{2,1,0:T(8,128)S(1)} %get-tuple-element.22), channel_id=1, source_target_pairs={{0,8},{8,16},{16,24},{24,32},{32,40},{40,48},{48,56},{56,64},{64,7... | collective-permute-start | bytes 368648 | tf_op jit(solution)/shard_map/ppermute | solution.py:315
  16.9 14.9 %collective-permute-start.3 = (f32[15,8,256]{2,1,0:T(8,128)S(1)}, f32[15,8,256]{2,1,0:T(8,128)S(1)}, u32[]{:S(2)}, u32[]{:S(2)}) collective-permute-start(f32[15,8,256]{2,1,0:T(8,128)S(1)} %get-tuple-element.23), channel_id=1, source_target_pairs={{8,0},{16,8},{24,16},{32,24},{40,32},{48,40},{56,48},{64,56},{72,6... | collective-permute-start | bytes 368648 | tf_op jit(solution)/shard_map/ppermute | solution.py:315
  33.1 7.0 %collective-permute-start.5 = (f32[18,8,256]{2,1,0:T(8,128)S(1)}, f32[18,8,256]{2,1,0:T(8,128)S(1)}, u32[]{:S(2)}, u32[]{:S(2)}) collective-permute-start(f32[18,8,256]{2,1,0:T(8,128)S(1)} %get-tuple-element.27), channel_id=1, source_target_pairs={{1,0},{2,1},{3,2},{4,3},{5,4},{6,5},{7,6},{9,8},{10,9},{11,10},{12... | collective-permute-start | bytes 442376 | tf_op jit(solution)/shard_map/ppermute | solution.py:315
  35.4 7.9 %collective-permute-start.4 = (f32[18,8,256]{2,1,0:T(8,128)S(1)}, f32[18,8,256]{2,1,0:T(8,128)S(1)}, u32[]{:S(2)}, u32[]{:S(2)}) collective-permute-start(f32[18,8,256]{2,1,0:T(8,128)S(1)} %get-tuple-element.26.own), channel_id=1, source_target_pairs={{0,1},{1,2},{2,3},{3,4},{4,5},{5,6},{6,7},{8,9},{9,10},{10,11},{11... | collective-permute-start | bytes 442376 | tf_op jit(solution)/shard_map/ppermute | solution.py:315
  43.4 12.8 %collective-permute-start.6 = (f32[28,8,256]{2,1,0:T(8,128)S(1)}, f32[28,8,256]{2,1,0:T(8,128)S(1)}, u32[]{:S(2)}, u32[]{:S(2)}) collective-permute-start(f32[28,8,256]{2,1,0:T(8,128)S(1)} %get-tuple-element.28), channel_id=1, source_target_pairs={{0,8},{8,16},{16,24},{24,32},{32,40},{40,48},{48,56},{56,64},{64,7... | collective-permute-start | bytes 688136 | tf_op jit(solution)/shard_map/ppermute | solution.py:315
  45.3 12.6 %collective-permute-start.7 = (f32[28,8,256]{2,1,0:T(8,128)S(1)}, f32[28,8,256]{2,1,0:T(8,128)S(1)}, u32[]{:S(2)}, u32[]{:S(2)}) collective-permute-start(f32[28,8,256]{2,1,0:T(8,128)S(1)} %get-tuple-element.29), channel_id=1, source_target_pairs={{8,0},{16,8},{24,16},{32,24},{40,32},{48,40},{56,48},{64,56},{72,6... | collective-permute-start | bytes 688136 | tf_op jit(solution)/shard_map/ppermute | solution.py:315

commit v2 on v1

v2 whole, which is shorter than its diff:
```python
import jax
import jax.numpy as jnp
from jax import lax
from jax.experimental import pallas as pl
from jax.experimental.pallas import tpu as pltpu
from jax.sharding import PartitionSpec as P

B = 8
NZ = 256
PD = 4096
CAP = 512
CHUNK = 512
F32 = jnp.float32
BF16 = jnp.bfloat16
VMEM = pl.BlockSpec(memory_space=pltpu.VMEM)
SMEM = pl.BlockSpec(memory_space=pltpu.SMEM)

Y_LAYERS = [(1, 0), (1, 1), (1, 2), (0, 0), (0, 1), (2, 0), (2, 1), (3, 0), (3, 1), (4, 0), (4, 1), (5, 0)]
X_LAYERS = [(0, 0), (0, 1), (0, 2), (1, 0), (1, 1), (2, 0), (2, 1), (3, 0), (3, 1), (4, 0), (4, 1), (5, 0)]
NL = 12


def params(limit=16):
    return pltpu.CompilerParams(vmem_limit_bytes=limit * 1024 * 1024)


def tiles(n):
    return jax.ShapeDtypeStruct((n, B, NZ), F32)


def call(kernel, outs, n_in, cost, scratch=(), smem=(), limit=16):
    return pl.pallas_call(
        kernel,
        out_shape=outs,
        in_specs=[SMEM if i in smem else VMEM for i in range(n_in)],
        out_specs=[VMEM] * len(outs),
        scratch_shapes=list(scratch),
        compiler_params=params(limit),
        cost_estimate=pl.CostEstimate(flops=cost, bytes_accessed=cost // 8, transcendentals=0),
    )


def by_parity(axis, act, even, odd):
    first = lax.rem(lax.axis_index(axis), 2) == 0

    @pl.when(first)
    def _():
        act(odd, even)

    @pl.when(jnp.logical_not(first))
    def _():
        act(even, odd)


def swap(shard, axis, start):
    peers = lax.axis_size(axis)
    pairs = [(i + a, i + 1 - a) for i in range(start, peers - 1, 2) for a in range(2)]
    return lax.ppermute(shard, axis, pairs)


def pack_y_kernel(gas, guess, even, odd):
    def act(low, high):
        for r, (field, depth) in enumerate(Y_LAYERS):
            for side, y in ((low, depth), (high, B - 1 - depth)):
                side[r] = guess[:, y, :] if field == 5 else gas[field, :, y, :]

    by_parity("gy", act, even, odd)


def split(value):
    high = value.astype(BF16).astype(F32)
    return high, value - high


def renew_kernel(gas, motion, size, cell, target, kept, rows):
    table = jnp.concatenate([gas[f].reshape(B * B, NZ) for f in range(4)], axis=0)
    high, low = split(table)
    table = jnp.concatenate([high.astype(BF16), low.astype(BF16)], axis=1)
    at_z = lax.broadcasted_iota(jnp.int32, (NZ, CHUNK), 0)
    at_xy = lax.broadcasted_iota(jnp.int32, (B * B, CHUNK), 0)
    heading = lax.broadcasted_iota(jnp.int32, (B, CHUNK), 0)
    a = lax.broadcasted_iota(jnp.int32, (CHUNK, CHUNK), 0)
    b = lax.broadcasted_iota(jnp.int32, (CHUNK, CHUNK), 1)
    upper = jnp.where(a <= b, 1.0, 0.0).astype(BF16)
    before = jnp.zeros((B, 1), F32)
    for n in range(PD // CHUNK):
        part = slice(n * CHUNK, (n + 1) * CHUNK)
        cells = cell[:, part]
        goal = target[:, part]
        in_z = jnp.where(at_z == (cells & (NZ - 1)), 1.0, 0.0).astype(BF16)
        in_xy = at_xy == (cells >> 8)
        found = jnp.dot(table, jnp.concatenate([in_z, in_z], axis=0), preferred_element_type=F32)
        local = [
            jnp.sum(jnp.where(in_xy, found[f * B * B : (f + 1) * B * B], 0.0), axis=0, keepdims=True)
            for f in range(4)
        ]
        u, v, w, temperature = (motion[f, :, part] for f in range(4))
        diameter = size[:, part]
        excess = local[3] - temperature
        vapour = 0.5 * diameter * jax.nn.sigmoid(excess)
        renewed = [
            u + 0.4 * (local[0] - u),
            v + 0.4 * (local[1] - v),
            w + 0.2 * ((local[2] - w) * 2.0 - 1.0),
            temperature + 0.2 * excess,
            diameter - 0.2 * vapour,
        ]
        drag = 0.5 * diameter * diameter * (w - local[2])
        alive = goal >= 0
        for f in range(5):
            kept[f, :, part] = jnp.where(goal == 4, renewed[f], 0.0)
            rows[f : f + 1, part] = renewed[f]
        rows[5:6, part] = jnp.where(alive, drag, 0.0)
        rows[6:7, part] = jnp.where(alive, vapour, 0.0)
        chosen = heading == goal
        rank = jnp.dot(jnp.where(chosen, 1.0, 0.0).astype(BF16), upper, preferred_element_type=F32) + before
        before = rank[:, CHUNK - 1 :]
        leaves = chosen & (heading < 4)
        place = jnp.where(leaves, rank + heading.astype(F32) * float(CAP), 0.0)
        rows[7:8, part] = jnp.sum(place, axis=0, keepdims=True) - 1.0


def spread_kernel(rows, cell, on, when, head, _, sources, parcels):
    at_z = lax.broadcasted_iota(jnp.int32, (NZ, CHUNK), 0)
    at_xy = lax.broadcasted_iota(jnp.int32, (B * B, CHUNK), 0)
    at_high = lax.broadcasted_iota(jnp.int32, (B, CHUNK), 0)
    total = jnp.zeros((4 * B * B, NZ), F32)
    moved = jnp.zeros((10 * B, NZ), F32)
    across = (((1,), (1,)), ((), ()))
    for n in range(PD // CHUNK):
        part = slice(n * CHUNK, (n + 1) * CHUNK)
        cells = cell[:, part]
        in_z = jnp.where(at_z == (cells & (NZ - 1)), 1.0, 0.0).astype(BF16)
        in_xy = at_xy == (cells >> 8)
        pieces = [*split(rows[5:6, part]), *split(rows[6:7, part])]
        given = jnp.concatenate([jnp.where(in_xy, piece, 0.0).astype(BF16) for piece in pieces], axis=0)
        total = total + lax.dot_general(given, in_z, across, preferred_element_type=F32)
        place = rows[7:8, part].astype(jnp.int32)
        in_low = jnp.where(at_z == (place & (NZ - 1)), 1.0, 0.0).astype(BF16)
        in_high = at_high == (place >> 8)
        split_up = [split(rows[f : f + 1, part]) for f in range(5)]
        leaving = [jnp.where(in_high, split_up[f][piece], 0.0) for piece in range(2) for f in range(5)]
        moved = moved + lax.dot_general(
            jnp.concatenate(leaving, axis=0).astype(BF16), in_low, across, preferred_element_type=F32
        )
    q = B * B
    steam = total[2 * q : 3 * q] + total[3 * q :]
    sources[0] = total[:q] + total[q : 2 * q]
    sources[1] = -2.0 * steam
    sources[2] = steam
    lanes = lax.broadcasted_iota(jnp.int32, (1, NZ), 1)
    for s in range(B):
        ramp = jnp.clip((100.0 - when[0, s].astype(F32)) / 50.0, 0.0, 1.0)
        strength = 3.0 * ramp * on[0, s].astype(F32)
        where = head[0, s]
        row = pl.ds(where >> 8, 1)
        taken = jnp.where(lanes == (where & (NZ - 1)), strength, 0.0)
        for f in range(2):
            sources[f, row, :] = sources[f, row, :] - taken
    moved = moved[: 5 * B] + moved[5 * B :]
    for d in range(4):
        for f in range(5):
            for half in range(2):
                at = f * B + 2 * d + half
                r = 2 * f + half
                parcels[d, r // B, r % B : r % B + 1, :] = moved[at : at + 1]
        parcels[d, 1, 2:, :] = jnp.zeros((B - 2, NZ), F32)


def pack_x_kernel(gas, guess, y_even, y_odd, _, even, odd):
    def planes(low, high):
        for side, near, step in ((low, 0, 1), (high, B - 1, -1)):
            for r, (field, depth) in enumerate(X_LAYERS):
                x = near + step * depth
                side[r] = guess[x] if field == 5 else gas[field, x]

            def corners(below, above, side=side, near=near, step=step):
                for h, halo in enumerate((below, above)):
                    for r, (layer, x) in enumerate(((3, near), (4, near), (0, near), (0, near + step))):
                        side[NL, 4 * h + r : 4 * h + r + 1, :] = halo[layer, x : x + 1, :]

            by_parity("gy", corners, y_even, y_odd)

    by_parity("gx", planes, even, odd)


def beside(value, by):
    lane = lax.broadcasted_iota(jnp.int32, value.shape, 1)
    turned = pltpu.roll(value, (-by) % NZ, axis=1)
    return jnp.where((lane < NZ - by) if by > 0 else (lane >= -by), turned, 0.0)


def advance(e, f, x, rows, first):
    def at(field, dx, dy):
        return e[field, x + dx, first + dy : first + dy + rows, :]

    centre = at(f, 0, 0)
    xs = {s: at(f, s, 0) for s in (-2, -1, 1, 2)}
    ys = {s: at(f, 0, s) for s in (-2, -1, 1, 2)}
    zs = {s: beside(centre, s) for s in (-2, -1, 1, 2)}
    laplace = xs[1] + xs[-1] + ys[1] + ys[-1] + zs[1] + zs[-1] - 6.0 * centre
    transport = 0.0
    for axis, shifted in enumerate((xs, ys, zs)):
        slope = 8.0 * (shifted[1] - shifted[-1]) - (shifted[2] - shifted[-2])
        transport = transport + at(axis, 0, 0) * slope
    return centre + (0.02 * laplace - (0.2 / 12.0) * transport)


def fill_own(gas, e, fields):
    for k, f in enumerate(fields):
        e[k, 3 : 3 + B, B : 2 * B, :] = gas[f]


def predict_kernel(gas, guess, y_even, y_odd, x_even, x_odd, sources, parcels, star, even, odd, e, wide, tall, q):
    gx = lax.axis_index("gx")
    gy = lax.axis_index("gy")
    has_left, has_right = gx > 0, gx < lax.axis_size("gx") - 1
    has_below, has_above = gy > 0, gy < lax.axis_size("gy") - 1
    fill_own(gas, e, range(3))
    q[1 : 1 + B, B : 2 * B, :] = guess[...]

    def fill_y(below, above):
        for r, (field, depth) in enumerate(Y_LAYERS):
            for halo, y in ((below, B - 1 - depth), (above, 2 * B + depth)):
                if field == 5:
                    q[1 : 1 + B, y, :] = halo[r]
                elif field < 3:
                    e[field, 3 : 3 + B, y, :] = halo[r]

    def fill_x(left, right):
        for r, (field, depth) in enumerate(X_LAYERS):
            for halo, x in ((left, -1 - depth), (right, B + depth)):
                if field == 5:
                    q[x + 1, B : 2 * B, :] = halo[r]
                elif field < 3:
                    e[field, x + 3, B : 2 * B, :] = halo[r]
        for halo, near, step in ((left, 2, -1), (right, 3 + B, 1)):
            for h, (y, onward) in enumerate(((B - 1, -1), (2 * B, 1))):
                spots = ((0, near, y), (0, near, y + onward), (1, near, y), (1, near + step, y))
                for r, (field, x, row) in enumerate(spots):
                    e[field, x, row : row + 1, :] = halo[NL, 4 * h + r : 4 * h + r + 1, :]

    by_parity("gy", fill_y, y_even, y_odd)
    by_parity("gx", fill_x, x_even, x_odd)
    for x in range(-1, B + 1):
        value = advance(e, 0, x + 3, B, B)
        if x < 0:
            value = jnp.where(has_left, value, 0.0)
        if x == B:
            value = jnp.where(has_right, value, 0.0)
        wide[x + 1] = value
        if 0 <= x < B:
            star[0, x] = value
    for x in range(B):
        value = advance(e, 1, x + 3, B + 2, B - 1)
        row = lax.broadcasted_iota(jnp.int32, value.shape, 0)
        inside = ((row > 0) | has_below) & ((row < B + 1) | has_above)
        value = jnp.where(inside, value, 0.0)
        tall[x, : B + 2, :] = value
        star[1, x] = value[1 : 1 + B]
    for x in range(B):
        w = advance(e, 2, x + 3, B, B) + 0.2 * sources[0, x]
        star[2, x] = w
        spread = wide[x + 2] - wide[x] + (tall[x, 2 : 2 + B, :] - tall[x, :B, :])
        source = 2.5 * (spread + (beside(w, 1) - beside(w, -1)))
        centre = q[x + 1, B : 2 * B, :]
        around = q[x + 2, B : 2 * B, :] + q[x, B : 2 * B, :]
        around = around + q[x + 1, B + 1 : 2 * B + 1, :] + q[x + 1, B - 1 : 2 * B - 1, :]
        field = (around + beside(centre, 1) + beside(centre, -1) - source) * (1.0 / 6.0)
        for side in (even, odd):
            side[x] = field
            side[B + x] = source

    def attach(low, high):
        for side, heading in ((high, 2), (low, 3)):
            side[2 * B] = parcels[heading, 0]
            side[2 * B + 1] = parcels[heading, 1]

    by_parity("gy", attach, even, odd)


def scalars_kernel(gas, y_even, y_odd, x_even, x_odd, sources, _, star, e):
    fill_own(gas, e, range(5))

    def fill_y(below, above):
        for r, (field, depth) in enumerate(Y_LAYERS):
            if field in (3, 4):
                e[field, 3 : 3 + B, B - 1 - depth, :] = below[r]
                e[field, 3 : 3 + B, 2 * B + depth, :] = above[r]

    def fill_x(left, right):
        for r, (field, depth) in enumerate(X_LAYERS):
            if field in (3, 4):
                e[field, 2 - depth, B : 2 * B, :] = left[r]
                e[field, B + 3 + depth, B : 2 * B, :] = right[r]

    by_parity("gy", fill_y, y_even, y_odd)
    by_parity("gx", fill_x, x_even, x_odd)
    for f in (3, 4):
        for x in range(B):
            star[f - 3, x] = advance(e, f, x + 3, B, B) + 0.2 * sources[f - 2, x]


NX2 = 28


def pack_x2_kernel(own, y_even, y_odd, parcels, even, odd):
    row = lax.broadcasted_iota(jnp.int32, (B, NZ), 0)
    base = 2 * B - 1

    def planes(low, high):
        for side, near, step, heading in ((low, -1, 1, 1), (high, B, -1, 0)):
            for d in range(1, B + 1):
                side[d - 1] = own[near + step * d]
            for d in range(1, B):
                side[base + d - 1] = own[B + near + step * d]
            side[NX2] = parcels[heading, 0]
            side[NX2 + 1] = parcels[heading, 1]

            def merged(below, above, side=side, near=near, step=step):
                for m in range(1, B):
                    lower = below[near + step * m]
                    upper = above[near + step * (B - m)]
                    side[B - 1 + m] = jnp.where(row >= m, lower, upper)
                for m in range(1, B - 1):
                    lower = below[B + near + step * m]
                    upper = above[B + near + step * (B - 1 - m)]
                    side[base + B - 2 + m] = jnp.where(row >= m + 1, lower, upper)

            by_parity("gy", merged, y_even, y_odd)

    by_parity("gx", planes, even, odd)


def finish_kernel(star, star_rest, own, y_even, y_odd, x_even, x_odd, gas_next, pressure, arrived, p0, p1, s, c):
    gx = lax.axis_index("gx")
    gy = lax.axis_index("gy")
    inside_x = [gx > 0, None, gx < lax.axis_size("gx") - 1]
    inside_y = [gy > 0, None, gy < lax.axis_size("gy") - 1]
    for i in range(3):
        for j in range(3):
            value = jnp.full((B, NZ), 1.0 / 6.0, F32)
            for flag in (inside_x[i], inside_y[j]):
                if flag is not None:
                    value = jnp.where(flag, value, 0.0)
            c[i, j * B : (j + 1) * B, :] = value
    for x in range(B):
        p0[B + x, B : 2 * B, :] = own[x]
        s[B + x, B : 2 * B, :] = own[B + x]
    base = 2 * B - 1

    def arrive(d, halo, at):
        for f in range(5):
            for half in range(2):
                r = 2 * f + half
                arrived[d, f, :, half * NZ : (half + 1) * NZ] = halo[at + r // B, r % B : r % B + 1, :]

    def fill_y(below, above):
        for x in range(B):
            for k, halo in ((0, below), (2, above)):
                p0[B + x, k * B : (k + 1) * B, :] = halo[x]
                s[B + x, k * B : (k + 1) * B, :] = halo[B + x]
        arrive(2, below, 2 * B)
        arrive(3, above, 2 * B)

    def fill_x(left, right):
        for halo, near, step in ((left, B, -1), (right, 2 * B - 1, 1)):
            for d in range(1, B + 1):
                p0[near + step * d, B : 2 * B, :] = halo[d - 1]
                if d < B:
                    s[near + step * d, B : 2 * B, :] = halo[base + d - 1]
            for m in range(1, B):
                piece = halo[B - 1 + m]
                p0[near + step * m, :B, :] = piece
                p0[near + step * (B - m), 2 * B :, :] = piece
            for m in range(1, B - 1):
                piece = halo[base + B - 2 + m]
                s[near + step * m, :B, :] = piece
                s[near + step * (B - 1 - m), 2 * B :, :] = piece
            p0[near + step * B, :B, :] = halo[0]
            p0[near + step * B, 2 * B :, :] = halo[0]
            s[near + step * (B - 1), :B, :] = halo[0]
            s[near + step * (B - 1), 2 * B :, :] = halo[0]
        arrive(0, left, NX2)
        arrive(1, right, NX2)

    by_parity("gy", fill_y, y_even, y_odd)
    by_parity("gx", fill_x, x_even, x_odd)
    now, later = p0, p1
    for turn in range(2, 9):
        reach = 9 - turn
        for x in range(B - reach, 2 * B + reach):
            centre = now[x]
            around = now[x - 1] + now[x + 1]
            around = around + pltpu.roll(centre, 1, axis=0) + pltpu.roll(centre, 3 * B - 1, axis=0)
            around = around + beside(centre, 1) + beside(centre, -1)
            later[x] = (around - s[x]) * c[0 if x < B else (1 if x < 2 * B else 2)]
        now, later = later, now
    for x in range(B):
        centre = now[B + x, B : 2 * B, :]
        pressure[x] = centre
        gas_next[0, x] = star[0, x] - 0.1 * (now[B + x + 1, B : 2 * B, :] - now[B + x - 1, B : 2 * B, :])
        gas_next[1, x] = star[1, x] - 0.1 * (now[B + x, B + 1 : 2 * B + 1, :] - now[B + x, B - 1 : 2 * B - 1, :])
        gas_next[2, x] = star[2, x] - 0.1 * (beside(centre, 1) - beside(centre, -1))
        gas_next[3, x] = star_rest[0, x]
        gas_next[4, x] = star_rest[1, x]


def body(gas, guess, motion, size, cell, target, on, when, head):
    shape = jax.ShapeDtypeStruct
    y_even, y_odd = call(pack_y_kernel, [tiles(NL)] * 2, 2, 10**6)(gas, guess)
    y_odd = swap(y_odd, "gy", 1)
    y_even = swap(y_even, "gy", 0)
    kept, rows = call(renew_kernel, [shape((5, 1, PD), F32), shape((8, PD), F32)], 5, 10**9)(
        gas, motion, size, cell, target
    )
    x_even, x_odd = call(pack_x_kernel, [tiles(NL + 1)] * 2, 5, 10**6)(gas, guess, y_even, y_odd, rows)
    sources, parcels = call(
        spread_kernel,
        [shape((3, B * B, NZ), F32), shape((4, 2, B, NZ), F32)],
        6,
        10**9,
        smem=(2, 3, 4),
    )(rows, cell, on, when, head, x_odd)
    sources = sources.reshape(3, B, B, NZ)
    x_even = swap(x_even, "gx", 0)
    x_odd = swap(x_odd, "gx", 1)
    wide = pltpu.VMEM((5, B + 6, 3 * B, NZ), F32)
    star, ps_even, ps_odd = call(
        predict_kernel,
        [shape((3, B, B, NZ), F32), tiles(2 * B + 2), tiles(2 * B + 2)],
        8,
        10**7,
        scratch=[
            wide,
            pltpu.VMEM((B + 2, B, NZ), F32),
            pltpu.VMEM((B, 2 * B, NZ), F32),
            pltpu.VMEM((B + 2, 3 * B, NZ), F32),
        ],
    )(gas, guess, y_even, y_odd, x_even, x_odd, sources, parcels)
    [star_rest] = call(scalars_kernel, [shape((2, B, B, NZ), F32)], 7, 10**8, scratch=[wide])(
        gas, y_even, y_odd, x_even, x_odd, sources, ps_odd
    )
    y_odd = swap(ps_odd, "gy", 1)
    y_even = swap(ps_even, "gy", 0)
    x_even, x_odd = call(pack_x2_kernel, [tiles(NX2 + 2)] * 2, 4, 10**6)(ps_even, y_even, y_odd, parcels)
    x_even = swap(x_even, "gx", 0)
    x_odd = swap(x_odd, "gx", 1)
    gas_next, pressure, arrived = call(
        finish_kernel,
        [shape((5, B, B, NZ), F32), shape((B, B, NZ), F32), shape((4, 5, 1, CAP), F32)],
        7,
        10**7,
        scratch=[
            pltpu.VMEM((3 * B, 3 * B, NZ), F32),
            pltpu.VMEM((3 * B, 3 * B, NZ), F32),
            pltpu.VMEM((3 * B, 3 * B, NZ), F32),
            pltpu.VMEM((3, 3 * B, NZ), F32),
        ],
    )(star, star_rest, ps_even, y_even, y_odd, x_even, x_odd)
    return gas_next, pressure, kept, arrived


def solution(mesh):
    in_specs = (
        P(None, "gx", "gy", None),
        P("gx", "gy", None),
        P(None, "gx", "gy"),
        P("gx", "gy"),
        P("gx", "gy"),
        P("gx", "gy"),
        P("gx", "gy"),
        P("gx", "gy"),
        P("gx", "gy"),
    )
    out_specs = (
        P(None, "gx", "gy", None),
        P("gx", "gy", None),
        P(None, "gx", "gy"),
        P(None, None, "gx", "gy"),
    )
    return jax.shard_map(body, mesh=mesh, in_specs=in_specs, out_specs=out_specs, check_vma=False)
```

time: 60.8 us -> 60.9 us (level)
  the two profiles are of different devices: /device:TPU:50 before, /device:TPU:58 now
where the time goes in v2:
time: 60.9 us; the launch traced here: 60.4 us
  starting transfers between devices  34.4 us (56%)
  waiting for transfers between devices  14.3 us (23%)
  Pallas kernels  8.99 us (15%)
  local copies, waits for them, and re-layouts  1.85 us (3%)
  between operations  0.87 us (1%)
    ppermute x8, starting transfers between devices, swap(): return lax.ppermute(shard, axis, pairs)  34.4 us
    ppermute x8, waiting for transfers between devices, swap(): return lax.ppermute(shard, axis, pairs)  14.3 us
    pallas_call x1, Pallas kernels, body(): call(renew_kernel, [shape((5, 1, PD), F32), shape((8, PD), F32)], 5, 10 *...  3.25 us
    pallas_call x1, Pallas kernels, body(): call(finish_kernel, [shape((5, B, B, NZ), F32), shape((B, B, NZ), F32), s...  2.39 us
    pallas_call x1, Pallas kernels, body(): call(spread_kernel, [shape((3, B * B, NZ), F32), shape((4, 2, B, NZ), F32...  1.92 us
    unnamed x22, local copies, waits for them, and re-layouts  1.85 us
  transfers between devices with their start and end apart: 8, of which 5 were waited for; matrix products, arithmetic and copies ran while one was open for 0% of the time, Pallas kernels for 9%

profile of v2, /device:TPU:58, one launch (start us, length us, event | category | flops | bytes accessed | tf_op | source)
XLA Modules:
  0.0 60.4 jit_solution(485922252358105773)
XLA Ops:
  0.6 0.0 copy-start
  0.6 1.0 %copy-done = f32[5,8,8,256]{3,2,1,0:T(8,128)S(1)} copy-done((f32[5,8,8,256]{3,2,1,0:T(8,128)S(1)}, f32[5,8,8,256]{3,2,1,0:T(8,128)}, u32[]{:S(2)}) %copy-start) | copy-done | bytes 327704
  1.6 0.8 %copy-done.2 = f32[8,8,256]{2,1,0:T(8,128)S(1)} copy-done((f32[8,8,256]{2,1,0:T(8,128)S(1)}, f32[8,8,256]{2,1,0:T(8,128)}, u32[]{:S(2)}) %copy-start.2) | copy-done | bytes 65560
  2.5 0.1 shard_map.120
  2.5 3.3 %collective-permute-start = (f32[12,8,256]{2,1,0:T(8,128)S(1)}, f32[12,8,256]{2,1,0:T(8,128)S(1)}, u32[]{:S(2)}, u32[]{:S(2)}) collective-permute-start(f32[12,8,256]{2,1,0:T(8,128)S(1)} %get-tuple-element.20), channel_id=1, source_target_pairs={{0,1},{1,0},{2,3},{3,2},{4,5},{5,4},{6,7},{7,6},{8,9},{9,8},{10,11... | collective-permute-start | bytes 294920 | tf_op jit(solution)/shard_map/ppermute | solution.py:58
  5.8 0.0 copy-start.3
  5.8 3.6 %collective-permute-start.1 = (f32[12,8,256]{2,1,0:T(8,128)S(1)}, f32[12,8,256]{2,1,0:T(8,128)S(1)}, u32[]{:S(2)}, u32[]{:S(2)}) collective-permute-start(f32[12,8,256]{2,1,0:T(8,128)S(1)} %get-tuple-element.21), channel_id=1, source_target_pairs={{1,2},{2,1},{3,4},{4,3},{5,6},{6,5},{9,10},{10,9},{11,12},{12,11},... | collective-permute-start | bytes 294920 | tf_op jit(solution)/shard_map/ppermute | solution.py:58
  9.5 0.0 copy-done.4
  9.5 3.2 %shard_map.121 = (f32[5,1,4096]{2,1,0:T(1,128)}, f32[8,4096]{1,0:T(8,128)S(1)}) custom-call(f32[5,8,8,256]{3,2,1,0:T(8,128)S(1)} %copy-done, f32[4,1,4096]{2,1,0:T(1,128)S(1)} %copy-done.4, f32[1,4096]{1,0:T(1,128)S(1)} %copy-done.5, s32[1,4096]{1,0:T(1,128)S(1)} %copy-done.7, s32[1,4096]{1,0:T(1,128)S(1)} %copy-done.6), custom_call_target="tpu_custom_call" | custom-call | flops 1000000000 | bytes 125000000 | tf_op jit(solution)/shard_map/pallas_call | solution.py:414
  12.8 0.0 collective-permute-done.y_even
  12.8 0.6 collective-permute-done.1.y_odd
  13.4 0.0 copy-done.3
  13.4 0.0 copy-start.8
  13.4 0.0 copy-start.9
  13.4 0.0 copy-start.10
  13.4 2.1 %collective-permute-start.2 = (f32[13,8,256]{2,1,0:T(8,128)S(1)}, f32[13,8,256]{2,1,0:T(8,128)S(1)}, u32[]{:S(2)}, u32[]{:S(2)}) collective-permute-start(f32[13,8,256]{2,1,0:T(8,128)S(1)} %get-tuple-element.23), channel_id=1, source_target_pairs={{0,8},{8,0},{16,24},{24,16},{32,40},{40,32},{48,56},{56,48},{64,72... | collective-permute-start | bytes 319496 | tf_op jit(solution)/shard_map/ppermute | solution.py:58
  15.5 0.0 copy-start.1
  15.5 12.8 %collective-permute-start.3 = (f32[13,8,256]{2,1,0:T(8,128)S(1)}, f32[13,8,256]{2,1,0:T(8,128)S(1)}, u32[]{:S(2)}, u32[]{:S(2)}) collective-permute-start(f32[13,8,256]{2,1,0:T(8,128)S(1)} %get-tuple-element.24._), channel_id=1, source_target_pairs={{8,16},{16,8},{24,32},{32,24},{40,48},{48,40},{56,64},{64,56},{72,... | collective-permute-start | bytes 319496 | tf_op jit(solution)/shard_map/ppermute | solution.py:58
  28.3 1.9 %shard_map.123 = (f32[3,64,256]{2,1,0:T(8,128)S(1)}, f32[4,2,8,256]{3,2,1,0:T(8,128)S(1)}) custom-call(f32[8,4096]{1,0:T(8,128)S(1)} %get-tuple-element.22._.rows, s32[1,4096]{1,0:T(1,128)S(1)} %copy-done.7, s32[1,8]{1,0:T(1,128)S(1)} %copy-done.8, s32[1,8]{1,0:T(1,128)S(1)} %copy-done.9, s32[1,8]{1,0:T(1,128)S(1)} %copy-done.10, ...), custom_call_target="tpu_custom_call" | custom-call | flops 1000000000 | bytes 125000000 | tf_op jit(solution)/shard_map/pallas_call | solution.py:418
  30.2 0.0 collective-permute-done.2.x_even
  30.2 1.6 %collective-permute-done.3.x_odd = f32[13,8,256]{2,1,0:T(8,128)S(1)} collective-permute-done((f32[13,8,256]{2,1,0:T(8,128)S(1)}, f32[13,8,256]{2,1,0:T(8,128)S(1)}, u32[]{:S(2)}, u32[]{:S(2)}) %collective-permute-start.3) | collective-permute-done | bytes 106528 | tf_op jit(solution)/shard_map/ppermute | solution.py:58
  31.8 0.9 %shard_map.124 = (f32[3,8,8,256]{3,2,1,0:T(8,128)S(1)}, f32[18,8,256]{2,1,0:T(8,128)S(1)}, f32[18,8,256]{2,1,0:T(8,128)S(1)}) custom-call(f32[5,8,8,256]{3,2,1,0:T(8,128)S(1)} %copy-done.1, f32[8,8,256]{2,1,0:T(8,128)S(1)} %copy-done.3, f32[12,8,256]{2,1,0:T(8,128)S(1)} %collective-permute-done.y_even, f32[12,8,256]{2,1,0:T(8,128)S(1)} %collective-permute-done.1.y_odd, ...), custom_call_target="tpu_custom_call" | custom-call | flops 10000000 | bytes 1250000 | tf_op jit(solution)/shard_map/pallas_call | solution.py:429
  32.8 3.2 %collective-permute-start.5 = (f32[18,8,256]{2,1,0:T(8,128)S(1)}, f32[18,8,256]{2,1,0:T(8,128)S(1)}, u32[]{:S(2)}, u32[]{:S(2)}) collective-permute-start(f32[18,8,256]{2,1,0:T(8,128)S(1)} %get-tuple-element.28._), channel_id=1, source_target_pairs={{1,2},{2,1},{3,4},{4,3},{5,6},{6,5},{9,10},{10,9},{11,12},{12,11},... | collective-permute-start | bytes 442376 | tf_op jit(solution)/shard_map/ppermute | solution.py:58
  36.0 2.3 %collective-permute-start.4 = (f32[18,8,256]{2,1,0:T(8,128)S(1)}, f32[18,8,256]{2,1,0:T(8,128)S(1)}, u32[]{:S(2)}, u32[]{:S(2)}) collective-permute-start(f32[18,8,256]{2,1,0:T(8,128)S(1)} %get-tuple-element.29.own), channel_id=1, source_target_pairs={{0,1},{1,0},{2,3},{3,2},{4,5},{5,4},{6,7},{7,6},{8,9},{9,8},{10,11... | collective-permute-start | bytes 442376 | tf_op jit(solution)/shard_map/ppermute | solution.py:58
  38.3 2.4 %collective-permute-done.5.y_odd = f32[18,8,256]{2,1,0:T(8,128)S(1)} collective-permute-done((f32[18,8,256]{2,1,0:T(8,128)S(1)}, f32[18,8,256]{2,1,0:T(8,128)S(1)}, u32[]{:S(2)}, u32[]{:S(2)}) %collective-permute-start.5) | collective-permute-done | bytes 147488 | tf_op jit(solution)/shard_map/ppermute | solution.py:58
  40.7 2.4 %collective-permute-done.4.y_even = f32[18,8,256]{2,1,0:T(8,128)S(1)} collective-permute-done((f32[18,8,256]{2,1,0:T(8,128)S(1)}, f32[18,8,256]{2,1,0:T(8,128)S(1)}, u32[]{:S(2)}, u32[]{:S(2)}) %collective-permute-start.4) | collective-permute-done | bytes 147488 | tf_op jit(solution)/shard_map/ppermute | solution.py:58
  43.1 1.9 %collective-permute-start.6 = (f32[30,8,256]{2,1,0:T(8,128)S(1)}, f32[30,8,256]{2,1,0:T(8,128)S(1)}, u32[]{:S(2)}, u32[]{:S(2)}) collective-permute-start(f32[30,8,256]{2,1,0:T(8,128)S(1)} %get-tuple-element.30), channel_id=1, source_target_pairs={{0,8},{8,0},{16,24},{24,16},{32,40},{40,32},{48,56},{56,48},{64,72... | collective-permute-start | bytes 737288 | tf_op jit(solution)/shard_map/ppermute | solution.py:58
  45.0 5.2 %collective-permute-start.7 = (f32[30,8,256]{2,1,0:T(8,128)S(1)}, f32[30,8,256]{2,1,0:T(8,128)S(1)}, u32[]{:S(2)}, u32[]{:S(2)}) collective-permute-start(f32[30,8,256]{2,1,0:T(8,128)S(1)} %get-tuple-element.31), channel_id=1, source_target_pairs={{8,16},{16,8},{24,32},{32,24},{40,48},{48,40},{56,64},{64,56},{72,... | collective-permute-start | bytes 737288 | tf_op jit(solution)/shard_map/ppermute | solution.py:58
  50.3 0.3 shard_map.125.star_rest
  50.6 0.0 collective-permute-done.6.x_even
  50.6 7.4 %collective-permute-done.7.x_odd = f32[30,8,256]{2,1,0:T(8,128)S(1)} collective-permute-done((f32[30,8,256]{2,1,0:T(8,128)S(1)}, f32[30,8,256]{2,1,0:T(8,128)S(1)}, u32[]{:S(2)}, u32[]{:S(2)}) %collective-permute-start.7) | collective-permute-done | bytes 245792 | tf_op jit(solution)/shard_map/ppermute | solution.py:58
  58.0 2.4 %shard_map.127 = (f32[5,8,8,256]{3,2,1,0:T(8,128)}, f32[8,8,256]{2,1,0:T(8,128)}, f32[4,5,1,512]{3,2,1,0:T(1,128)}) custom-call(f32[3,8,8,256]{3,2,1,0:T(8,128)S(1)} %get-tuple-element.27.star, f32[2,8,8,256]{3,2,1,0:T(8,128)S(1)} %shard_map.125.star_rest, f32[18,8,256]{2,1,0:T(8,128)S(1)} %get-tuple-element.29.own, ...), custom_call_target="tpu_custom_call" | custom-call | flops 10000000 | bytes 1250000 | tf_op jit(solution)/shard_map/pallas_call | solution.py:449
  (14 shorter events, 0.1 us)
Async XLA Ops:
  0.6 1.0 %copy-start = (f32[5,8,8,256]{3,2,1,0:T(8,128)S(1)}, f32[5,8,8,256]{3,2,1,0:T(8,128)}, u32[]{:S(2)}) copy-start(f32[5,8,8,256]{3,2,1,0:T(8,128)} %gas.9) | copy-start | bytes 983044
  1.6 0.8 %copy-start.2 = (f32[8,8,256]{2,1,0:T(8,128)S(1)}, f32[8,8,256]{2,1,0:T(8,128)}, u32[]{:S(2)}) copy-start(f32[8,8,256]{2,1,0:T(8,128)} %guess.5) | copy-start | bytes 196612
  2.4 7.0 %copy-start.4 = (f32[4,1,4096]{2,1,0:T(1,128)S(1)}, f32[4,1,4096]{2,1,0:T(1,128)}, u32[]{:S(2)}) copy-start(f32[4,1,4096]{2,1,0:T(1,128)} %motion.1) | copy-start | bytes 196612
  2.5 7.0 %copy-start.5 = (f32[1,4096]{1,0:T(1,128)S(1)}, f32[1,4096]{1,0:T(1,128)}, u32[]{:S(2)}) copy-start(f32[1,4096]{1,0:T(1,128)} %size.1) | copy-start | bytes 49156
  2.5 7.0 %copy-start.6 = (s32[1,4096]{1,0:T(1,128)S(1)}, s32[1,4096]{1,0:T(1,128)}, u32[]{:S(2)}) copy-start(s32[1,4096]{1,0:T(1,128)} %target.1) | copy-start | bytes 49156
  2.5 7.1 %copy-start.7 = (s32[1,4096]{1,0:T(1,128)S(1)}, s32[1,4096]{1,0:T(1,128)}, u32[]{:S(2)}) copy-start(s32[1,4096]{1,0:T(1,128)} %cell.3) | copy-start | bytes 49156
  2.5 10.2 %collective-permute-start = (f32[12,8,256]{2,1,0:T(8,128)S(1)}, f32[12,8,256]{2,1,0:T(8,128)S(1)}, u32[]{:S(2)}, u32[]{:S(2)}) collective-permute-start(f32[12,8,256]{2,1,0:T(8,128)S(1)} %get-tuple-element.20), channel_id=1, source_target_pairs={{0,1},{1,0},{2,3},{3,2},{4,5},{5,4},{6,7},{7,6},{8,9},{9,8},{10,11... | collective-permute-start | bytes 294920 | tf_op jit(solution)/shard_map/ppermute | solution.py:58
  5.8 7.6 %copy-start.3 = (f32[8,8,256]{2,1,0:T(8,128)S(1)}, f32[8,8,256]{2,1,0:T(8,128)}, u32[]{:S(2)}) copy-start(f32[8,8,256]{2,1,0:T(8,128)} %guess.5) | copy-start | bytes 196612
  5.8 7.5 %collective-permute-start.1 = (f32[12,8,256]{2,1,0:T(8,128)S(1)}, f32[12,8,256]{2,1,0:T(8,128)S(1)}, u32[]{:S(2)}, u32[]{:S(2)}) collective-permute-start(f32[12,8,256]{2,1,0:T(8,128)S(1)} %get-tuple-element.21), channel_id=1, source_target_pairs={{1,2},{2,1},{3,4},{4,3},{5,6},{6,5},{9,10},{10,9},{11,12},{12,11},... | collective-permute-start | bytes 294920 | tf_op jit(solution)/shard_map/ppermute | solution.py:58
  13.4 14.9 %copy-start.8 = (s32[1,8]{1,0:T(1,128)S(1)}, s32[1,8]{1,0:T(1,128)}, u32[]{:S(2)}) copy-start(s32[1,8]{1,0:T(1,128)} %on.1) | copy-start | bytes 100
  13.4 14.9 %copy-start.9 = (s32[1,8]{1,0:T(1,128)S(1)}, s32[1,8]{1,0:T(1,128)}, u32[]{:S(2)}) copy-start(s32[1,8]{1,0:T(1,128)} %when.1) | copy-start | bytes 100
  13.4 14.9 %copy-start.10 = (s32[1,8]{1,0:T(1,128)S(1)}, s32[1,8]{1,0:T(1,128)}, u32[]{:S(2)}) copy-start(s32[1,8]{1,0:T(1,128)} %head.1) | copy-start | bytes 100
  13.4 16.8 %collective-permute-start.2 = (f32[13,8,256]{2,1,0:T(8,128)S(1)}, f32[13,8,256]{2,1,0:T(8,128)S(1)}, u32[]{:S(2)}, u32[]{:S(2)}) collective-permute-start(f32[13,8,256]{2,1,0:T(8,128)S(1)} %get-tuple-element.23), channel_id=1, source_target_pairs={{0,8},{8,0},{16,24},{24,16},{32,40},{40,32},{48,56},{56,48},{64,72... | collective-permute-start | bytes 319496 | tf_op jit(solution)/shard_map/ppermute | solution.py:58
  15.5 16.3 %copy-start.1 = (f32[5,8,8,256]{3,2,1,0:T(8,128)S(1)}, f32[5,8,8,256]{3,2,1,0:T(8,128)}, u32[]{:S(2)}) copy-start(f32[5,8,8,256]{3,2,1,0:T(8,128)} %gas.9) | copy-start | bytes 983044
  15.5 16.3 %collective-permute-start.3 = (f32[13,8,256]{2,1,0:T(8,128)S(1)}, f32[13,8,256]{2,1,0:T(8,128)S(1)}, u32[]{:S(2)}, u32[]{:S(2)}) collective-permute-start(f32[13,8,256]{2,1,0:T(8,128)S(1)} %get-tuple-element.24._), channel_id=1, source_target_pairs={{8,16},{16,8},{24,32},{32,24},{40,48},{48,40},{56,64},{64,56},{72,... | collective-permute-start | bytes 319496 | tf_op jit(solution)/shard_map/ppermute | solution.py:58
  32.8 7.9 %collective-permute-start.5 = (f32[18,8,256]{2,1,0:T(8,128)S(1)}, f32[18,8,256]{2,1,0:T(8,128)S(1)}, u32[]{:S(2)}, u32[]{:S(2)}) collective-permute-start(f32[18,8,256]{2,1,0:T(8,128)S(1)} %get-tuple-element.28._), channel_id=1, source_target_pairs={{1,2},{2,1},{3,4},{4,3},{5,6},{6,5},{9,10},{10,9},{11,12},{12,11},... | collective-permute-start | bytes 442376 | tf_op jit(solution)/shard_map/ppermute | solution.py:58
  36.0 7.0 %collective-permute-start.4 = (f32[18,8,256]{2,1,0:T(8,128)S(1)}, f32[18,8,256]{2,1,0:T(8,128)S(1)}, u32[]{:S(2)}, u32[]{:S(2)}) collective-permute-start(f32[18,8,256]{2,1,0:T(8,128)S(1)} %get-tuple-element.29.own), channel_id=1, source_target_pairs={{0,1},{1,0},{2,3},{3,2},{4,5},{5,4},{6,7},{7,6},{8,9},{9,8},{10,11... | collective-permute-start | bytes 442376 | tf_op jit(solution)/shard_map/ppermute | solution.py:58
  43.1 7.5 %collective-permute-start.6 = (f32[30,8,256]{2,1,0:T(8,128)S(1)}, f32[30,8,256]{2,1,0:T(8,128)S(1)}, u32[]{:S(2)}, u32[]{:S(2)}) collective-permute-start(f32[30,8,256]{2,1,0:T(8,128)S(1)} %get-tuple-element.30), channel_id=1, source_target_pairs={{0,8},{8,0},{16,24},{24,16},{32,40},{40,32},{48,56},{56,48},{64,72... | collective-permute-start | bytes 737288 | tf_op jit(solution)/shard_map/ppermute | solution.py:58
  45.0 13.0 %collective-permute-start.7 = (f32[30,8,256]{2,1,0:T(8,128)S(1)}, f32[30,8,256]{2,1,0:T(8,128)S(1)}, u32[]{:S(2)}, u32[]{:S(2)}) collective-permute-start(f32[30,8,256]{2,1,0:T(8,128)S(1)} %get-tuple-element.31), channel_id=1, source_target_pairs={{8,16},{16,8},{24,32},{32,24},{40,48},{48,40},{56,64},{64,56},{72,... | collective-permute-start | bytes 737288 | tf_op jit(solution)/shard_map/ppermute | solution.py:58

commit v3 on v2

--- a/solution.py
+++ b/solution.py
@@ -58,11 +58,11 @@
     return lax.ppermute(shard, axis, pairs)
 
 
-def pack_y_kernel(gas, guess, even, odd):
+def pack_y_kernel(gas, edges, even, odd):
     def act(low, high):
         for r, (field, depth) in enumerate(Y_LAYERS):
-            for side, y in ((low, depth), (high, B - 1 - depth)):
-                side[r] = guess[:, y, :] if field == 5 else gas[field, :, y, :]
+            for side, y, edge in ((low, depth, 0), (high, B - 1 - depth, 1)):
+                side[r] = edges[edge] if field == 5 else gas[field, :, y, :]
 
     by_parity("gy", act, even, odd)
 
@@ -72,17 +72,32 @@
     return high, value - high
 
 
-def renew_kernel(gas, motion, size, cell, target, kept, rows):
+def place_kernel(target, place):
+    heading = lax.broadcasted_iota(jnp.int32, (B, CHUNK), 0)
+    a = lax.broadcasted_iota(jnp.int32, (CHUNK, CHUNK), 0)
+    b = lax.broadcasted_iota(jnp.int32, (CHUNK, CHUNK), 1)
+    upper = jnp.where(a <= b, 1.0, 0.0).astype(BF16)
+    before = jnp.zeros((B, 1), F32)
+    for n in range(PD // CHUNK):
+        part = slice(n * CHUNK, (n + 1) * CHUNK)
+        chosen = heading == target[:, part]
+        rank = jnp.dot(jnp.where(chosen, 1.0, 0.0).astype(BF16), upper, preferred_element_type=F32) + before
+        before = rank[:, CHUNK - 1 :]
+        leaves = chosen & (heading < 4)
+        value = jnp.where(leaves, rank + heading.astype(F32) * float(CAP), 0.0)
+        place[:, part] = jnp.sum(value, axis=0, keepdims=True).astype(jnp.int32) - 1
+
+
+def droplet_kernel(gas, motion, size, cell, target, place, on, when, head, _, sources, parcels, kept):
     table = jnp.concatenate([gas[f].reshape(B * B, NZ) for f in range(4)], axis=0)
     high, low = split(table)
     table = jnp.concatenate([high.astype(BF16), low.astype(BF16)], axis=1)
     at_z = lax.broadcasted_iota(jnp.int32, (NZ, CHUNK), 0)
     at_xy = lax.broadcasted_iota(jnp.int32, (B * B, CHUNK), 0)
-    heading = lax.broadcasted_iota(jnp.int32, (B, CHUNK), 0)
-    a = lax.broadcasted_iota(jnp.int32, (CHUNK, CHUNK), 0)
-    b = lax.broadcasted_iota(jnp.int32, (CHUNK, CHUNK), 1)
-    upper = jnp.where(a <= b, 1.0, 0.0).astype(BF16)
-    before = jnp.zeros((B, 1), F32)
+    at_high = lax.broadcasted_iota(jnp.int32, (B, CHUNK), 0)
+    total = jnp.zeros((4 * B * B, NZ), F32)
+    moved = jnp.zeros((10 * B, NZ), F32)
+    across = (((1,), (1,)), ((), ()))
     for n in range(PD // CHUNK):
         part = slice(n * CHUNK, (n + 1) * CHUNK)
         cells = cell[:, part]
@@ -109,36 +124,13 @@
         alive = goal >= 0
         for f in range(5):
             kept[f, :, part] = jnp.where(goal == 4, renewed[f], 0.0)
-            rows[f : f + 1, part] = renewed[f]
-        rows[5:6, part] = jnp.where(alive, drag, 0.0)
-        rows[6:7, part] = jnp.where(alive, vapour, 0.0)
-        chosen = heading == goal
-        rank = jnp.dot(jnp.where(chosen, 1.0, 0.0).astype(BF16), upper, preferred_element_type=F32) + before
-        before = rank[:, CHUNK - 1 :]
-        leaves = chosen & (heading < 4)
-        place = jnp.where(leaves, rank + heading.astype(F32) * float(CAP), 0.0)
-        rows[7:8, part] = jnp.sum(place, axis=0, keepdims=True) - 1.0
-
-
-def spread_kernel(rows, cell, on, when, head, _, sources, parcels):
-    at_z = lax.broadcasted_iota(jnp.int32, (NZ, CHUNK), 0)
-    at_xy = lax.broadcasted_iota(jnp.int32, (B * B, CHUNK), 0)
-    at_high = lax.broadcasted_iota(jnp.int32, (B, CHUNK), 0)
-    total = jnp.zeros((4 * B * B, NZ), F32)
-    moved = jnp.zeros((10 * B, NZ), F32)
-    across = (((1,), (1,)), ((), ()))
-    for n in range(PD // CHUNK):
-        part = slice(n * CHUNK, (n + 1) * CHUNK)
-        cells = cell[:, part]
-        in_z = jnp.where(at_z == (cells & (NZ - 1)), 1.0, 0.0).astype(BF16)
-        in_xy = at_xy == (cells >> 8)
-        pieces = [*split(rows[5:6, part]), *split(rows[6:7, part])]
+        pieces = [*split(jnp.where(alive, drag, 0.0)), *split(jnp.where(alive, vapour, 0.0))]
         given = jnp.concatenate([jnp.where(in_xy, piece, 0.0).astype(BF16) for piece in pieces], axis=0)
         total = total + lax.dot_general(given, in_z, across, preferred_element_type=F32)
-        place = rows[7:8, part].astype(jnp.int32)
-        in_low = jnp.where(at_z == (place & (NZ - 1)), 1.0, 0.0).astype(BF16)
-        in_high = at_high == (place >> 8)
-        split_up = [split(rows[f : f + 1, part]) for f in range(5)]
+        spot = place[:, part]
+        in_low = jnp.where(at_z == (spot & (NZ - 1)), 1.0, 0.0).astype(BF16)
+        in_high = at_high == (spot >> 8)
+        split_up = [split(value) for value in renewed]
         leaving = [jnp.where(in_high, split_up[f][piece], 0.0) for piece in range(2) for f in range(5)]
         moved = moved + lax.dot_general(
             jnp.concatenate(leaving, axis=0).astype(BF16), in_low, across, preferred_element_type=F32
@@ -167,7 +159,7 @@
         parcels[d, 1, 2:, :] = jnp.zeros((B - 2, NZ), F32)
 
 
-def pack_x_kernel(gas, guess, y_even, y_odd, _, even, odd):
+def pack_x_kernel(gas, guess, y_odd, y_even, _, even, odd):
     def planes(low, high):
         for side, near, step in ((low, 0, 1), (high, B - 1, -1)):
             for r, (field, depth) in enumerate(X_LAYERS):
@@ -211,7 +203,7 @@
         e[k, 3 : 3 + B, B : 2 * B, :] = gas[f]
 
 
-def predict_kernel(gas, guess, y_even, y_odd, x_even, x_odd, sources, parcels, star, even, odd, e, wide, tall, q):
+def predict_kernel(gas, guess, y_odd, y_even, x_odd, x_even, sources, parcels, star, even, odd, e, wide, tall, q):
     gx = lax.axis_index("gx")
     gy = lax.axis_index("gy")
     has_left, has_right = gx > 0, gx < lax.axis_size("gx") - 1
@@ -279,7 +271,7 @@
     by_parity("gy", attach, even, odd)
 
 
-def scalars_kernel(gas, y_even, y_odd, x_even, x_odd, sources, _, star, e):
+def scalars_kernel(gas, y_odd, y_even, x_odd, x_even, sources, _, star, e):
     fill_own(gas, e, range(5))
 
     def fill_y(below, above):
@@ -332,7 +324,7 @@
     by_parity("gx", planes, even, odd)
 
 
-def finish_kernel(star, star_rest, own, y_even, y_odd, x_even, x_odd, gas_next, pressure, arrived, p0, p1, s, c):
+def finish_kernel(star, star_rest, own, y_even, y_odd, x_odd, x_even, gas_next, pressure, arrived, p0, p1, s, c):
     gx = lax.axis_index("gx")
     gy = lax.axis_index("gy")
     inside_x = [gx > 0, None, gx < lax.axis_size("gx") - 1]
@@ -408,23 +400,23 @@
 
 def body(gas, guess, motion, size, cell, target, on, when, head):
     shape = jax.ShapeDtypeStruct
-    y_even, y_odd = call(pack_y_kernel, [tiles(NL)] * 2, 2, 10**6)(gas, guess)
+    y_even, y_odd = call(pack_y_kernel, [tiles(NL)] * 2, 2, 10**6)(
+        gas, jnp.stack([guess[:, 0], guess[:, B - 1]])
+    )
     y_odd = swap(y_odd, "gy", 1)
     y_even = swap(y_even, "gy", 0)
-    kept, rows = call(renew_kernel, [shape((5, 1, PD), F32), shape((8, PD), F32)], 5, 10**9)(
-        gas, motion, size, cell, target
-    )
-    x_even, x_odd = call(pack_x_kernel, [tiles(NL + 1)] * 2, 5, 10**6)(gas, guess, y_even, y_odd, rows)
-    sources, parcels = call(
-        spread_kernel,
-        [shape((3, B * B, NZ), F32), shape((4, 2, B, NZ), F32)],
-        6,
-        10**9,
-        smem=(2, 3, 4),
-    )(rows, cell, on, when, head, x_odd)
+    [place] = call(place_kernel, [shape((1, PD), jnp.int32)], 1, 10**9)(target)
+    x_even, x_odd = call(pack_x_kernel, [tiles(NL + 1)] * 2, 5, 10**6)(gas, guess, y_odd, y_even, place)
+    sources, parcels, kept = call(
+        droplet_kernel,
+        [shape((3, B * B, NZ), F32), shape((4, 2, B, NZ), F32), shape((5, 1, PD), F32)],
+        10,
+        2 * 10**9,
+        smem=(6, 7, 8),
+    )(gas, motion, size, cell, target, place, on, when, head, x_even)
     sources = sources.reshape(3, B, B, NZ)
+    x_odd = swap(x_odd, "gx", 1)
     x_even = swap(x_even, "gx", 0)
-    x_odd = swap(x_odd, "gx", 1)
     wide = pltpu.VMEM((5, B + 6, 3 * B, NZ), F32)
     star, ps_even, ps_odd = call(
         predict_kernel,
@@ -437,15 +429,15 @@
             pltpu.VMEM((B, 2 * B, NZ), F32),
             pltpu.VMEM((B + 2, 3 * B, NZ), F32),
         ],
-    )(gas, guess, y_even, y_odd, x_even, x_odd, sources, parcels)
+    )(gas, guess, y_odd, y_even, x_odd, x_even, sources, parcels)
     [star_rest] = call(scalars_kernel, [shape((2, B, B, NZ), F32)], 7, 10**8, scratch=[wide])(
-        gas, y_even, y_odd, x_even, x_odd, sources, ps_odd
+        gas, y_odd, y_even, x_odd, x_even, sources, ps_odd
     )
     y_odd = swap(ps_odd, "gy", 1)
     y_even = swap(ps_even, "gy", 0)
     x_even, x_odd = call(pack_x2_kernel, [tiles(NX2 + 2)] * 2, 4, 10**6)(ps_even, y_even, y_odd, parcels)
+    x_odd = swap(x_odd, "gx", 1)
     x_even = swap(x_even, "gx", 0)
-    x_odd = swap(x_odd, "gx", 1)
     gas_next, pressure, arrived = call(
         finish_kernel,
         [shape((5, B, B, NZ), F32), shape((B, B, NZ), F32), shape((4, 5, 1, CAP), F32)],
@@ -457,7 +449,7 @@
             pltpu.VMEM((3 * B, 3 * B, NZ), F32),
             pltpu.VMEM((3, 3 * B, NZ), F32),
         ],
-    )(star, star_rest, ps_even, y_even, y_odd, x_even, x_odd)
+    )(star, star_rest, ps_even, y_even, y_odd, x_odd, x_even)
     return gas_next, pressure, kept, arrived
 
 

time: 60.9 us -> 59.2 us (0.972)
  the two profiles are of different devices: /device:TPU:58 before, /device:TPU:48 now
where the time goes in v3:
time: 59.2 us; the launch traced here: 58.8 us
  starting transfers between devices  32.1 us (54%)
  waiting for transfers between devices  14.9 us (25%)
  Pallas kernels  8.94 us (15%)
  local copies, waits for them, and re-layouts  1.96 us (3%)
  between operations  0.91 us (2%)
    ppermute x8, starting transfers between devices, swap(): return lax.ppermute(shard, axis, pairs)  32.1 us
    ppermute x8, waiting for transfers between devices, swap(): return lax.ppermute(shard, axis, pairs)  14.9 us
    pallas_call x1, Pallas kernels, body(): call(droplet_kernel, [shape((3, B * B, NZ), F32), shape((4, 2, B, NZ), F3...  4.44 us
    pallas_call x1, Pallas kernels, body(): call(finish_kernel, [shape((5, B, B, NZ), F32), shape((B, B, NZ), F32), s...  2.4 us
  transfers between devices with their start and end apart: 8, of which 3 were waited for; matrix products, arithmetic and copies ran while one was open for 0% of the time, Pallas kernels for 9%

profile of v3, /device:TPU:48, one launch (start us, length us, event | category | flops | bytes accessed | tf_op | source)
XLA Modules:
  0.0 58.8 jit_solution(5800210777051548346)
XLA Ops:
  0.6 0.9 %fusion = (f32[8,1,256]{2,1,0:T(1,128)S(1)}, f32[8,1,256]{2,1,0:T(1,128)S(1)}) fusion(f32[8,8,256]{2,1,0:T(8,128)} %guess.3), kind=kLoop, calls=%fused_computation.3 | loop fusion | bytes 32768 | tf_op jit(solution)/shard_map/slice | solution.py:404
  1.6 0.0 copy-start
  1.6 1.0 %copy-done = f32[5,8,8,256]{3,2,1,0:T(8,128)S(1)} copy-done((f32[5,8,8,256]{3,2,1,0:T(8,128)S(1)}, f32[5,8,8,256]{3,2,1,0:T(8,128)}, u32[]{:S(2)}) %copy-start) | copy-done | bytes 327704
  2.6 0.1 shard_map.120
  2.6 0.7 %collective-permute-start = (f32[12,8,256]{2,1,0:T(8,128)S(1)}, f32[12,8,256]{2,1,0:T(8,128)S(1)}, u32[]{:S(2)}, u32[]{:S(2)}) collective-permute-start(f32[12,8,256]{2,1,0:T(8,128)S(1)} %get-tuple-element.19), channel_id=1, source_target_pairs={{1,2},{2,1},{3,4},{4,3},{5,6},{6,5},{9,10},{10,9},{11,12},{12,11},... | collective-permute-start | bytes 294920 | tf_op jit(solution)/shard_map/ppermute | solution.py:58
  3.3 0.0 copy-start.1
  3.3 0.0 copy-start.2
  3.3 6.2 %collective-permute-start.1 = (f32[12,8,256]{2,1,0:T(8,128)S(1)}, f32[12,8,256]{2,1,0:T(8,128)S(1)}, u32[]{:S(2)}, u32[]{:S(2)}) collective-permute-start(f32[12,8,256]{2,1,0:T(8,128)S(1)} %get-tuple-element.20), channel_id=1, source_target_pairs={{0,1},{1,0},{2,3},{3,2},{4,5},{5,4},{6,7},{7,6},{8,9},{9,8},{10,11... | collective-permute-start | bytes 294920 | tf_op jit(solution)/shard_map/ppermute | solution.py:58
  9.6 0.7 %shard_map.121._.place = s32[1,4096]{1,0:T(1,128)S(1)} custom-call(s32[1,4096]{1,0:T(1,128)S(1)} %copy-done.4), custom_call_target="tpu_custom_call" | custom-call | flops 1000000000 | bytes 125000000 | tf_op jit(solution)/shard_map/pallas_call | solution.py:408
  10.3 0.0 copy-start.3
  10.3 0.0 copy-start.5
  10.3 0.0 copy-start.6
  10.3 0.0 collective-permute-done.y_odd
  10.3 1.9 %collective-permute-done.1.y_even = f32[12,8,256]{2,1,0:T(8,128)S(1)} collective-permute-done((f32[12,8,256]{2,1,0:T(8,128)S(1)}, f32[12,8,256]{2,1,0:T(8,128)S(1)}, u32[]{:S(2)}, u32[]{:S(2)}) %collective-permute-start.1) | collective-permute-done | bytes 98336 | tf_op jit(solution)/shard_map/ppermute | solution.py:58
  12.2 0.0 copy-start.7
  12.2 0.0 copy-start.8
  12.2 0.0 copy-start.9
  12.3 11.3 %collective-permute-start.2 = (f32[13,8,256]{2,1,0:T(8,128)S(1)}, f32[13,8,256]{2,1,0:T(8,128)S(1)}, u32[]{:S(2)}, u32[]{:S(2)}) collective-permute-start(f32[13,8,256]{2,1,0:T(8,128)S(1)} %get-tuple-element.21), channel_id=1, source_target_pairs={{8,16},{16,8},{24,32},{32,24},{40,48},{48,40},{56,64},{64,56},{72,... | collective-permute-start | bytes 319496 | tf_op jit(solution)/shard_map/ppermute | solution.py:58
  23.6 1.9 %collective-permute-start.3 = (f32[13,8,256]{2,1,0:T(8,128)S(1)}, f32[13,8,256]{2,1,0:T(8,128)S(1)}, u32[]{:S(2)}, u32[]{:S(2)}) collective-permute-start(f32[13,8,256]{2,1,0:T(8,128)S(1)} %get-tuple-element.22._), channel_id=1, source_target_pairs={{0,8},{8,0},{16,24},{24,16},{32,40},{40,32},{48,56},{56,48},{64,72... | collective-permute-start | bytes 319496 | tf_op jit(solution)/shard_map/ppermute | solution.py:58
  25.6 4.4 %shard_map.123 = (f32[3,64,256]{2,1,0:T(8,128)S(1)}, f32[4,2,8,256]{3,2,1,0:T(8,128)S(1)}, f32[5,1,4096]{2,1,0:T(1,128)}) custom-call(f32[5,8,8,256]{3,2,1,0:T(8,128)S(1)} %copy-done.1, f32[4,1,4096]{2,1,0:T(1,128)S(1)} %copy-done.3, f32[1,4096]{1,0:T(1,128)S(1)} %copy-done.5, s32[1,4096]{1,0:T(1,128)S(1)} %copy-done.6, s32[1,4096]{1,0:T(1,128)S(1)} %copy-done.4, ...), custom_call_target="tpu_custom_call" | custom-call | flops 2000000000 | bytes 250000000 | tf_op jit(solution)/shard_map/pallas_call | solution.py:410
  30.0 0.0 collective-permute-done.2.x_odd
  30.0 0.0 collective-permute-done.3.x_even
  30.0 1.0 %shard_map.124 = (f32[3,8,8,256]{3,2,1,0:T(8,128)S(1)}, f32[18,8,256]{2,1,0:T(8,128)S(1)}, f32[18,8,256]{2,1,0:T(8,128)S(1)}) custom-call(f32[5,8,8,256]{3,2,1,0:T(8,128)S(1)} %copy-done.1, f32[8,8,256]{2,1,0:T(8,128)S(1)} %copy-done.2, f32[12,8,256]{2,1,0:T(8,128)S(1)} %collective-permute-done.y_odd, f32[12,8,256]{2,1,0:T(8,128)S(1)} %collective-permute-done.1.y_even, ...), custom_call_target="tpu_custom_call" | custom-call | flops 10000000 | bytes 1250000 | tf_op jit(solution)/shard_map/pallas_call | solution.py:421
  31.0 0.7 %collective-permute-start.5 = (f32[18,8,256]{2,1,0:T(8,128)S(1)}, f32[18,8,256]{2,1,0:T(8,128)S(1)}, u32[]{:S(2)}, u32[]{:S(2)}) collective-permute-start(f32[18,8,256]{2,1,0:T(8,128)S(1)} %get-tuple-element.26._), channel_id=1, source_target_pairs={{1,2},{2,1},{3,4},{4,3},{5,6},{6,5},{9,10},{10,9},{11,12},{12,11},... | collective-permute-start | bytes 442376 | tf_op jit(solution)/shard_map/ppermute | solution.py:58
  31.7 6.1 %collective-permute-start.4 = (f32[18,8,256]{2,1,0:T(8,128)S(1)}, f32[18,8,256]{2,1,0:T(8,128)S(1)}, u32[]{:S(2)}, u32[]{:S(2)}) collective-permute-start(f32[18,8,256]{2,1,0:T(8,128)S(1)} %get-tuple-element.27.own), channel_id=1, source_target_pairs={{0,1},{1,0},{2,3},{3,2},{4,5},{5,4},{6,7},{7,6},{8,9},{9,8},{10,11... | collective-permute-start | bytes 442376 | tf_op jit(solution)/shard_map/ppermute | solution.py:58
  37.8 5.4 %collective-permute-done.4.y_even = f32[18,8,256]{2,1,0:T(8,128)S(1)} collective-permute-done((f32[18,8,256]{2,1,0:T(8,128)S(1)}, f32[18,8,256]{2,1,0:T(8,128)S(1)}, u32[]{:S(2)}, u32[]{:S(2)}) %collective-permute-start.4) | collective-permute-done | bytes 147488 | tf_op jit(solution)/shard_map/ppermute | solution.py:58
  43.2 0.1 shard_map.126
  43.3 3.2 %collective-permute-start.6 = (f32[30,8,256]{2,1,0:T(8,128)S(1)}, f32[30,8,256]{2,1,0:T(8,128)S(1)}, u32[]{:S(2)}, u32[]{:S(2)}) collective-permute-start(f32[30,8,256]{2,1,0:T(8,128)S(1)} %get-tuple-element.28), channel_id=1, source_target_pairs={{8,16},{16,8},{24,32},{32,24},{40,48},{48,40},{56,64},{64,56},{72,... | collective-permute-start | bytes 737288 | tf_op jit(solution)/shard_map/ppermute | solution.py:58
  46.5 1.9 %collective-permute-start.7 = (f32[30,8,256]{2,1,0:T(8,128)S(1)}, f32[30,8,256]{2,1,0:T(8,128)S(1)}, u32[]{:S(2)}, u32[]{:S(2)}) collective-permute-start(f32[30,8,256]{2,1,0:T(8,128)S(1)} %get-tuple-element.29), channel_id=1, source_target_pairs={{0,8},{8,0},{16,24},{24,16},{32,40},{40,32},{48,56},{56,48},{64,72... | collective-permute-start | bytes 737288 | tf_op jit(solution)/shard_map/ppermute | solution.py:58
  48.5 0.3 shard_map.125.star_rest
  48.8 7.6 %collective-permute-done.6.x_odd = f32[30,8,256]{2,1,0:T(8,128)S(1)} collective-permute-done((f32[30,8,256]{2,1,0:T(8,128)S(1)}, f32[30,8,256]{2,1,0:T(8,128)S(1)}, u32[]{:S(2)}, u32[]{:S(2)}) %collective-permute-start.6) | collective-permute-done | bytes 245792 | tf_op jit(solution)/shard_map/ppermute | solution.py:58
  56.4 2.4 %shard_map.127 = (f32[5,8,8,256]{3,2,1,0:T(8,128)}, f32[8,8,256]{2,1,0:T(8,128)}, f32[4,5,1,512]{3,2,1,0:T(1,128)}) custom-call(f32[3,8,8,256]{3,2,1,0:T(8,128)S(1)} %get-tuple-element.25.star, f32[2,8,8,256]{3,2,1,0:T(8,128)S(1)} %shard_map.125.star_rest, f32[18,8,256]{2,1,0:T(8,128)S(1)} %get-tuple-element.27.own, ...), custom_call_target="tpu_custom_call" | custom-call | flops 10000000 | bytes 1250000 | tf_op jit(solution)/shard_map/pallas_call | solution.py:441
  (15 shorter events, 0.1 us)
Async XLA Ops:
  1.6 1.0 %copy-start = (f32[5,8,8,256]{3,2,1,0:T(8,128)S(1)}, f32[5,8,8,256]{3,2,1,0:T(8,128)}, u32[]{:S(2)}) copy-start(f32[5,8,8,256]{3,2,1,0:T(8,128)} %gas.9) | copy-start | bytes 983044
  2.6 7.0 %copy-start.4 = (s32[1,4096]{1,0:T(1,128)S(1)}, s32[1,4096]{1,0:T(1,128)}, u32[]{:S(2)}) copy-start(s32[1,4096]{1,0:T(1,128)} %target.3) | copy-start | bytes 49156
  2.6 7.7 %collective-permute-start = (f32[12,8,256]{2,1,0:T(8,128)S(1)}, f32[12,8,256]{2,1,0:T(8,128)S(1)}, u32[]{:S(2)}, u32[]{:S(2)}) collective-permute-start(f32[12,8,256]{2,1,0:T(8,128)S(1)} %get-tuple-element.19), channel_id=1, source_target_pairs={{1,2},{2,1},{3,4},{4,3},{5,6},{6,5},{9,10},{10,9},{11,12},{12,11},... | collective-permute-start | bytes 294920 | tf_op jit(solution)/shard_map/ppermute | solution.py:58
  3.3 8.9 %copy-start.1 = (f32[5,8,8,256]{3,2,1,0:T(8,128)S(1)}, f32[5,8,8,256]{3,2,1,0:T(8,128)}, u32[]{:S(2)}) copy-start(f32[5,8,8,256]{3,2,1,0:T(8,128)} %gas.9) | copy-start | bytes 983044
  3.3 8.9 %copy-start.2 = (f32[8,8,256]{2,1,0:T(8,128)S(1)}, f32[8,8,256]{2,1,0:T(8,128)}, u32[]{:S(2)}) copy-start(f32[8,8,256]{2,1,0:T(8,128)} %guess.3) | copy-start | bytes 196612
  3.3 8.8 %collective-permute-start.1 = (f32[12,8,256]{2,1,0:T(8,128)S(1)}, f32[12,8,256]{2,1,0:T(8,128)S(1)}, u32[]{:S(2)}, u32[]{:S(2)}) collective-permute-start(f32[12,8,256]{2,1,0:T(8,128)S(1)} %get-tuple-element.20), channel_id=1, source_target_pairs={{0,1},{1,0},{2,3},{3,2},{4,5},{5,4},{6,7},{7,6},{8,9},{9,8},{10,11... | collective-permute-start | bytes 294920 | tf_op jit(solution)/shard_map/ppermute | solution.py:58
  10.3 15.2 %copy-start.3 = (f32[4,1,4096]{2,1,0:T(1,128)S(1)}, f32[4,1,4096]{2,1,0:T(1,128)}, u32[]{:S(2)}) copy-start(f32[4,1,4096]{2,1,0:T(1,128)} %motion.1) | copy-start | bytes 196612
  10.3 15.2 %copy-start.5 = (f32[1,4096]{1,0:T(1,128)S(1)}, f32[1,4096]{1,0:T(1,128)}, u32[]{:S(2)}) copy-start(f32[1,4096]{1,0:T(1,128)} %size.1) | copy-start | bytes 49156
  10.3 15.2 %copy-start.6 = (s32[1,4096]{1,0:T(1,128)S(1)}, s32[1,4096]{1,0:T(1,128)}, u32[]{:S(2)}) copy-start(s32[1,4096]{1,0:T(1,128)} %cell.1) | copy-start | bytes 49156
  12.2 13.3 %copy-start.7 = (s32[1,8]{1,0:T(1,128)S(1)}, s32[1,8]{1,0:T(1,128)}, u32[]{:S(2)}) copy-start(s32[1,8]{1,0:T(1,128)} %on.1) | copy-start | bytes 100
  12.2 13.3 %copy-start.8 = (s32[1,8]{1,0:T(1,128)S(1)}, s32[1,8]{1,0:T(1,128)}, u32[]{:S(2)}) copy-start(s32[1,8]{1,0:T(1,128)} %when.1) | copy-start | bytes 100
  12.2 13.3 %copy-start.9 = (s32[1,8]{1,0:T(1,128)S(1)}, s32[1,8]{1,0:T(1,128)}, u32[]{:S(2)}) copy-start(s32[1,8]{1,0:T(1,128)} %head.1) | copy-start | bytes 100
  12.3 17.8 %collective-permute-start.2 = (f32[13,8,256]{2,1,0:T(8,128)S(1)}, f32[13,8,256]{2,1,0:T(8,128)S(1)}, u32[]{:S(2)}, u32[]{:S(2)}) collective-permute-start(f32[13,8,256]{2,1,0:T(8,128)S(1)} %get-tuple-element.21), channel_id=1, source_target_pairs={{8,16},{16,8},{24,32},{32,24},{40,48},{48,40},{56,64},{64,56},{72,... | collective-permute-start | bytes 319496 | tf_op jit(solution)/shard_map/ppermute | solution.py:58
  23.6 6.4 %collective-permute-start.3 = (f32[13,8,256]{2,1,0:T(8,128)S(1)}, f32[13,8,256]{2,1,0:T(8,128)S(1)}, u32[]{:S(2)}, u32[]{:S(2)}) collective-permute-start(f32[13,8,256]{2,1,0:T(8,128)S(1)} %get-tuple-element.22._), channel_id=1, source_target_pairs={{0,8},{8,0},{16,24},{24,16},{32,40},{40,32},{48,56},{56,48},{64,72... | collective-permute-start | bytes 319496 | tf_op jit(solution)/shard_map/ppermute | solution.py:58
  31.0 6.8 %collective-permute-start.5 = (f32[18,8,256]{2,1,0:T(8,128)S(1)}, f32[18,8,256]{2,1,0:T(8,128)S(1)}, u32[]{:S(2)}, u32[]{:S(2)}) collective-permute-start(f32[18,8,256]{2,1,0:T(8,128)S(1)} %get-tuple-element.26._), channel_id=1, source_target_pairs={{1,2},{2,1},{3,4},{4,3},{5,6},{6,5},{9,10},{10,9},{11,12},{12,11},... | collective-permute-start | bytes 442376 | tf_op jit(solution)/shard_map/ppermute | solution.py:58
  31.7 11.6 %collective-permute-start.4 = (f32[18,8,256]{2,1,0:T(8,128)S(1)}, f32[18,8,256]{2,1,0:T(8,128)S(1)}, u32[]{:S(2)}, u32[]{:S(2)}) collective-permute-start(f32[18,8,256]{2,1,0:T(8,128)S(1)} %get-tuple-element.27.own), channel_id=1, source_target_pairs={{0,1},{1,0},{2,3},{3,2},{4,5},{5,4},{6,7},{7,6},{8,9},{9,8},{10,11... | collective-permute-start | bytes 442376 | tf_op jit(solution)/shard_map/ppermute | solution.py:58
  43.3 13.1 %collective-permute-start.6 = (f32[30,8,256]{2,1,0:T(8,128)S(1)}, f32[30,8,256]{2,1,0:T(8,128)S(1)}, u32[]{:S(2)}, u32[]{:S(2)}) collective-permute-start(f32[30,8,256]{2,1,0:T(8,128)S(1)} %get-tuple-element.28), channel_id=1, source_target_pairs={{8,16},{16,8},{24,32},{32,24},{40,48},{48,40},{56,64},{64,56},{72,... | collective-permute-start | bytes 737288 | tf_op jit(solution)/shard_map/ppermute | solution.py:58
  46.5 9.9 %collective-permute-start.7 = (f32[30,8,256]{2,1,0:T(8,128)S(1)}, f32[30,8,256]{2,1,0:T(8,128)S(1)}, u32[]{:S(2)}, u32[]{:S(2)}) collective-permute-start(f32[30,8,256]{2,1,0:T(8,128)S(1)} %get-tuple-element.29), channel_id=1, source_target_pairs={{0,8},{8,0},{16,24},{24,16},{32,40},{40,32},{48,56},{56,48},{64,72... | collective-permute-start | bytes 737288 | tf_op jit(solution)/shard_map/ppermute | solution.py:58

commit v4 on v3

--- a/solution.py
+++ b/solution.py
@@ -58,11 +58,15 @@
     return lax.ppermute(shard, axis, pairs)
 
 
-def pack_y_kernel(gas, edges, even, odd):
+def first_kernel(out):
+    out[...] = jnp.zeros_like(out)
+
+
+def pack_y_kernel(_, gas, guess, even, odd):
     def act(low, high):
         for r, (field, depth) in enumerate(Y_LAYERS):
-            for side, y, edge in ((low, depth, 0), (high, B - 1 - depth, 1)):
-                side[r] = edges[edge] if field == 5 else gas[field, :, y, :]
+            for side, y in ((low, depth), (high, B - 1 - depth)):
+                side[r] = guess[:, y, :] if field == 5 else gas[field, :, y, :]
 
     by_parity("gy", act, even, odd)
 
@@ -293,53 +297,125 @@
             star[f - 3, x] = advance(e, f, x + 3, B, B) + 0.2 * sources[f - 2, x]
 
 
-NX2 = 28
-
-
-def pack_x2_kernel(own, y_even, y_odd, parcels, even, odd):
-    row = lax.broadcasted_iota(jnp.int32, (B, NZ), 0)
-    base = 2 * B - 1
-
-    def planes(low, high):
-        for side, near, step, heading in ((low, -1, 1, 1), (high, B, -1, 0)):
-            for d in range(1, B + 1):
-                side[d - 1] = own[near + step * d]
-            for d in range(1, B):
-                side[base + d - 1] = own[B + near + step * d]
-            side[NX2] = parcels[heading, 0]
-            side[NX2 + 1] = parcels[heading, 1]
-
-            def merged(below, above, side=side, near=near, step=step):
-                for m in range(1, B):
-                    lower = below[near + step * m]
-                    upper = above[near + step * (B - m)]
-                    side[B - 1 + m] = jnp.where(row >= m, lower, upper)
-                for m in range(1, B - 1):
-                    lower = below[B + near + step * m]
-                    upper = above[B + near + step * (B - 1 - m)]
-                    side[base + B - 2 + m] = jnp.where(row >= m + 1, lower, upper)
-
-            by_parity("gy", merged, y_even, y_odd)
-
-    by_parity("gx", planes, even, odd)
-
-
-def finish_kernel(star, star_rest, own, y_even, y_odd, x_odd, x_even, gas_next, pressure, arrived, p0, p1, s, c):
+NH = 15
+HALF = NZ // 2
+
+
+def load(ref, *lead):
+    return [[ref[(*lead, slice(B * t, B * t + B), slice(HALF * h, HALF * h + HALF))] for h in range(2)] for t in range(3)]
+
+
+def store(ref, plane, *lead):
+    for t in range(3):
+        for h in range(2):
+            ref[(*lead, slice(B * t, B * t + B), slice(HALF * h, HALF * h + HALF))] = plane[t][h]
+
+
+def add(*planes):
+    planes = [p for p in planes if p is not None]
+    return [[sum((p[t][h] for p in planes[1:]), planes[0][t][h]) for h in range(2)] for t in range(3)]
+
+
+def beside_plane(c):
+    row = lax.broadcasted_iota(jnp.int32, (B, HALF), 0)
+    lane = lax.broadcasted_iota(jnp.int32, (B, HALF), 1)
+    top, bottom, start, end = row == 0, row == B - 1, lane == 0, lane == HALF - 1
+    out = []
+    for t in range(3):
+        after = [pltpu.roll(c[t][h], 1, axis=1) for h in range(2)]
+        ahead = [pltpu.roll(c[t][h], HALF - 1, axis=1) for h in range(2)]
+        along_z = [
+            jnp.where(start, 0.0, after[0]) + jnp.where(end, ahead[1], ahead[0]),
+            jnp.where(start, after[0], after[1]) + jnp.where(end, 0.0, ahead[1]),
+        ]
+        tile = []
+        for h in range(2):
+            down = pltpu.roll(c[t][h], 1, axis=0)
+            if t > 0:
+                down = jnp.where(top, pltpu.roll(c[t - 1][h], 1, axis=0), down)
+            up = pltpu.roll(c[t][h], B - 1, axis=0)
+            if t < 2:
+                up = jnp.where(bottom, pltpu.roll(c[t + 1][h], B - 1, axis=0), up)
+            tile.append(along_z[h] + (down + up))
+        out.append(tile)
+    return out
+
+
+def relax(centre, others, source, scale):
+    total = add(*others, None if centre is None else beside_plane(centre))
+    if source is not None:
+        total = [[total[t][h] - source[t][h] for h in range(2)] for t in range(3)]
+    return [[total[t][h] * scale[t] for h in range(2)] for t in range(3)]
+
+
+def weights(flags_x, flags_y):
+    out = []
+    for flag_y in flags_y:
+        value = jnp.full((B, HALF), 1.0 / 6.0, F32)
+        for flag in (*flags_x, flag_y):
+            if flag is not None:
+                value = jnp.where(flag, value, 0.0)
+        out.append(value)
+    return out
+
+
+def slab_kernel(own, y_odd, y_even, parcels, even, odd, first, source, f0, f1, low, high):
+    gy = lax.axis_index("gy")
+    scale = weights((), (gy > 0, None, gy < lax.axis_size("gy") - 1))
+    row = lax.broadcasted_iota(jnp.int32, (B, HALF), 0)
+    for x in range(B):
+        first[x, B : 2 * B, :] = own[x]
+        source[x, B : 2 * B, :] = own[B + x]
+
+    def fill(below, above):
+        for x in range(B):
+            for k, halo in ((0, below), (2, above)):
+                first[x, k * B : (k + 1) * B, :] = halo[x]
+                source[x, k * B : (k + 1) * B, :] = halo[B + x]
+
+    by_parity("gy", fill, y_even, y_odd)
+
+    def keep(side, k, plane):
+        for h in range(2):
+            part = slice(HALF * h, HALF * h + HALF)
+            side[k - 1, :, part] = plane[1][h]
+            if k < B:
+                side[B - 1 + k, k:, part] = plane[0][h][k:]
+                side[2 * B - 1 - k, : B - k, part] = plane[2][h][: B - k]
+
+    for side, x in ((low, 0), (high, B - 1)):
+        keep(side, 1, load(first, x))
+    now, later = first, f0
+    for k in range(2, 9):
+        depth = 9 - k
+        for x in range(B):
+            if depth <= x < B - depth:
+                continue
+            others = [load(now, y) for y in (x - 1, x + 1) if 0 <= y < B]
+            plane = relax(load(now, x), others, load(source, x), scale)
+            if k < 8:
+                store(later, plane, x)
+            for side, face in ((low, 0), (high, B - 1)):
+                if x == face:
+                    keep(side, k, plane)
+        now, later = (f0, f1) if k == 2 else (later, now)
+    for side, heading in ((low, 1), (high, 0)):
+        side[NH] = parcels[heading, 0]
+        side[NH + 1] = parcels[heading, 1]
+
+    def send(low_out, high_out):
+        low_out[...] = low[...]
+        high_out[...] = high[...]
+
+    by_parity("gx", send, even, odd)
+
+
+def finish_kernel(star, star_rest, first, source, y_even, y_odd, x_odd, x_even, gas_next, pressure, arrived, o0, o1, r0, r1, hist):
     gx = lax.axis_index("gx")
     gy = lax.axis_index("gy")
-    inside_x = [gx > 0, None, gx < lax.axis_size("gx") - 1]
-    inside_y = [gy > 0, None, gy < lax.axis_size("gy") - 1]
-    for i in range(3):
-        for j in range(3):
-            value = jnp.full((B, NZ), 1.0 / 6.0, F32)
-            for flag in (inside_x[i], inside_y[j]):
-                if flag is not None:
-                    value = jnp.where(flag, value, 0.0)
-            c[i, j * B : (j + 1) * B, :] = value
-    for x in range(B):
-        p0[B + x, B : 2 * B, :] = own[x]
-        s[B + x, B : 2 * B, :] = own[B + x]
-    base = 2 * B - 1
+    flags_y = (gy > 0, None, gy < lax.axis_size("gy") - 1)
+    inner = weights((), flags_y)
+    outer = [weights((gx > 0,), flags_y), weights((gx < lax.axis_size("gx") - 1,), flags_y)]
 
     def arrive(d, halo, at):
         for f in range(5):
@@ -347,52 +423,59 @@
                 r = 2 * f + half
                 arrived[d, f, :, half * NZ : (half + 1) * NZ] = halo[at + r // B, r % B : r % B + 1, :]
 
-    def fill_y(below, above):
-        for x in range(B):
-            for k, halo in ((0, below), (2, above)):
-                p0[B + x, k * B : (k + 1) * B, :] = halo[x]
-                s[B + x, k * B : (k + 1) * B, :] = halo[B + x]
+    def take_y(below, above):
         arrive(2, below, 2 * B)
         arrive(3, above, 2 * B)
 
-    def fill_x(left, right):
-        for halo, near, step in ((left, B, -1), (right, 2 * B - 1, 1)):
-            for d in range(1, B + 1):
-                p0[near + step * d, B : 2 * B, :] = halo[d - 1]
-                if d < B:
-                    s[near + step * d, B : 2 * B, :] = halo[base + d - 1]
-            for m in range(1, B):
-                piece = halo[B - 1 + m]
-                p0[near + step * m, :B, :] = piece
-                p0[near + step * (B - m), 2 * B :, :] = piece
-            for m in range(1, B - 1):
-                piece = halo[base + B - 2 + m]
-                s[near + step * m, :B, :] = piece
-                s[near + step * (B - 1 - m), 2 * B :, :] = piece
-            p0[near + step * B, :B, :] = halo[0]
-            p0[near + step * B, 2 * B :, :] = halo[0]
-            s[near + step * (B - 1), :B, :] = halo[0]
-            s[near + step * (B - 1), 2 * B :, :] = halo[0]
-        arrive(0, left, NX2)
-        arrive(1, right, NX2)
-
-    by_parity("gy", fill_y, y_even, y_odd)
-    by_parity("gx", fill_x, x_even, x_odd)
-    now, later = p0, p1
-    for turn in range(2, 9):
-        reach = 9 - turn
-        for x in range(B - reach, 2 * B + reach):
-            centre = now[x]
-            around = now[x - 1] + now[x + 1]
-            around = around + pltpu.roll(centre, 1, axis=0) + pltpu.roll(centre, 3 * B - 1, axis=0)
-            around = around + beside(centre, 1) + beside(centre, -1)
-            later[x] = (around - s[x]) * c[0 if x < B else (1 if x < 2 * B else 2)]
-        now, later = later, now
+    def take_x(left, right):
+        hist[0] = left[...]
+        hist[1] = right[...]
+
+    by_parity("gy", take_y, y_even, y_odd)
+    by_parity("gx", take_x, x_even, x_odd)
+    arrive(0, hist.at[0], NH)
+    arrive(1, hist.at[1], NH)
+
+    def history(side, k):
+        at = (B - 1 + k, k - 1, 2 * B - 1 - k)
+        return [[hist[side, at[t], :, slice(HALF * h, HALF * h + HALF)] for h in range(2)] for t in range(3)]
+
+    owns = {1: first, **{k: (o0, o1)[k % 2] for k in range(2, 9)}}
+    responses = {k: (r0, r1)[k % 2] for k in range(2, 9)}
+
+    def at(k, x):
+        if 0 <= x < B:
+            return load(owns[k], x)
+        side, depth = (0, -x) if x < 0 else (1, x - B + 1)
+        return load(responses[k], side, depth - 1) if depth < k else None
+
+    for k in range(2, 9):
+        depth = min(k - 1, 9 - k)
+        for x in range(-depth, B + depth):
+            others = [at(k - 1, x - 1), at(k - 1, x + 1)]
+            if 0 <= x < B:
+                if x == 0:
+                    others.append(history(0, k - 1))
+                if x == B - 1:
+                    others.append(history(1, k - 1))
+                store(owns[k], relax(at(k - 1, x), others, load(source, x), inner), x)
+            else:
+                side, far = (0, -x) if x < 0 else (1, x - B + 1)
+                store(responses[k], relax(at(k - 1, x), others, None, outer[side]), side, far - 1)
+    last, edge = owns[8], responses[8]
+
+    def level(x):
+        if x < 0:
+            return edge[0, 0, B : 2 * B, :] + hist[0, B - 1]
+        if x >= B:
+            return edge[1, 0, B : 2 * B, :] + hist[1, B - 1]
+        return last[x, B : 2 * B, :]
+
     for x in range(B):
-        centre = now[B + x, B : 2 * B, :]
+        centre = level(x)
         pressure[x] = centre
-        gas_next[0, x] = star[0, x] - 0.1 * (now[B + x + 1, B : 2 * B, :] - now[B + x - 1, B : 2 * B, :])
-        gas_next[1, x] = star[1, x] - 0.1 * (now[B + x, B + 1 : 2 * B + 1, :] - now[B + x, B - 1 : 2 * B - 1, :])
+        gas_next[0, x] = star[0, x] - 0.1 * (level(x + 1) - level(x - 1))
+        gas_next[1, x] = star[1, x] - 0.1 * (last[x, B + 1 : 2 * B + 1, :] - last[x, B - 1 : 2 * B - 1, :])
         gas_next[2, x] = star[2, x] - 0.1 * (beside(centre, 1) - beside(centre, -1))
         gas_next[3, x] = star_rest[0, x]
         gas_next[4, x] = star_rest[1, x]
@@ -400,9 +483,8 @@
 
 def body(gas, guess, motion, size, cell, target, on, when, head):
     shape = jax.ShapeDtypeStruct
-    y_even, y_odd = call(pack_y_kernel, [tiles(NL)] * 2, 2, 10**6)(
-        gas, jnp.stack([guess[:, 0], guess[:, B - 1]])
-    )
+    [first] = call(first_kernel, [shape((B, 128), F32)], 0, 10**10)()
+    y_even, y_odd = call(pack_y_kernel, [tiles(NL)] * 2, 3, 10**6)(first, gas, guess)
     y_odd = swap(y_odd, "gy", 1)
     y_even = swap(y_even, "gy", 0)
     [place] = call(place_kernel, [shape((1, PD), jnp.int32)], 1, 10**9)(target)
@@ -435,21 +517,25 @@
     )
     y_odd = swap(ps_odd, "gy", 1)
     y_even = swap(ps_even, "gy", 0)
-    x_even, x_odd = call(pack_x2_kernel, [tiles(NX2 + 2)] * 2, 4, 10**6)(ps_even, y_even, y_odd, parcels)
+    slab = shape((B, 3 * B, NZ), F32)
+    scratch = pltpu.VMEM((B, 3 * B, NZ), F32)
+    x_even, x_odd, first, source = call(
+        slab_kernel,
+        [tiles(NH + 2), tiles(NH + 2), slab, slab],
+        4,
+        10**7,
+        scratch=[scratch, scratch, pltpu.VMEM((NH + 2, B, NZ), F32), pltpu.VMEM((NH + 2, B, NZ), F32)],
+    )(ps_even, y_odd, y_even, parcels)
     x_odd = swap(x_odd, "gx", 1)
     x_even = swap(x_even, "gx", 0)
+    response = pltpu.VMEM((2, 4, 3 * B, NZ), F32)
     gas_next, pressure, arrived = call(
         finish_kernel,
         [shape((5, B, B, NZ), F32), shape((B, B, NZ), F32), shape((4, 5, 1, CAP), F32)],
-        7,
+        8,
         10**7,
-        scratch=[
-            pltpu.VMEM((3 * B, 3 * B, NZ), F32),
-            pltpu.VMEM((3 * B, 3 * B, NZ), F32),
-            pltpu.VMEM((3 * B, 3 * B, NZ), F32),
-            pltpu.VMEM((3, 3 * B, NZ), F32),
-        ],
-    )(star, star_rest, ps_even, y_even, y_odd, x_odd, x_even)
+        scratch=[scratch, scratch, response, response, pltpu.VMEM((2, NH + 2, B, NZ), F32)],
+    )(star, star_rest, first, source, y_even, y_odd, x_odd, x_even)
     return gas_next, pressure, kept, arrived
 
 

time: 59.2 us -> 55.8 us (0.943)
  waiting for transfers between devices: 14.9 us -> 12.4 us
  local copies, waits for them, and re-layouts: 1.96 us -> 0.99 us
    ppermute x8, waiting for transfers between devices: 14.9 us -> 12.4 us  [swap(): return lax.ppermute(shard, axis, pairs)]
    slice x1 -> x0, local copies, waits for them, and re-layouts: 0.93 us -> none  [body(): guess[:, 0]]
    pallas_call x2 -> x3, Pallas kernels: 0.11 us -> 0.78 us  [the longest x1 0.71 us: body(): call(slab_kernel, [tiles(NH + 2), tiles(NH + 2), slab, slab], 4, 10 ** 7,...]
  transfers between devices with their start and end apart: 8 -> 8, of which waited for: 3 -> 3; matrix products, arithmetic and copies ran while one was open for 0% -> 0% of each run, Pallas kernels for 9% -> 10%
where the time goes in v4:
time: 55.8 us; the launch traced here: 55.4 us
  starting transfers between devices  32.1 us (58%)
  waiting for transfers between devices  12.4 us (22%)
  Pallas kernels  9.1 us (16%)
  local copies, waits for them, and re-layouts  0.99 us (2%)
  between operations  0.89 us (2%)
    ppermute x8, starting transfers between devices, swap(): return lax.ppermute(shard, axis, pairs)  32.1 us
    ppermute x8, waiting for transfers between devices, swap(): return lax.ppermute(shard, axis, pairs)  12.4 us
    pallas_call x1, Pallas kernels, body(): call(droplet_kernel, [shape((3, B * B, NZ), F32), shape((4, 2, B, NZ), F3...  4.44 us
    pallas_call x1, Pallas kernels, body(): call(finish_kernel, [shape((5, B, B, NZ), F32), shape((B, B, NZ), F32), s...  1.89 us
  transfers between devices with their start and end apart: 8, of which 3 were waited for; matrix products, arithmetic and copies ran while one was open for 0% of the time, Pallas kernels for 10%

profile of v4, /device:TPU:48, one launch (start us, length us, event | category | flops | bytes accessed | tf_op | source)
XLA Modules:
  0.0 55.4 jit_solution(13380475816048256599)
XLA Ops:
  0.7 0.9 %copy-done = f32[5,8,8,256]{3,2,1,0:T(8,128)S(1)} copy-done((f32[5,8,8,256]{3,2,1,0:T(8,128)S(1)}, f32[5,8,8,256]{3,2,1,0:T(8,128)}, u32[]{:S(2)}) %copy-start) | copy-done | bytes 327704
  1.6 0.0 copy-done.1
  1.6 0.1 shard_map.121
  1.7 0.7 %collective-permute-start = (f32[12,8,256]{2,1,0:T(8,128)S(1)}, f32[12,8,256]{2,1,0:T(8,128)S(1)}, u32[]{:S(2)}, u32[]{:S(2)}) collective-permute-start(f32[12,8,256]{2,1,0:T(8,128)S(1)} %get-tuple-element.21), channel_id=1, source_target_pairs={{1,2},{2,1},{3,4},{4,3},{5,6},{6,5},{9,10},{10,9},{11,12},{12,11},... | collective-permute-start | bytes 294920 | tf_op jit(solution)/shard_map/ppermute | solution.py:58
  2.4 6.1 %collective-permute-start.1 = (f32[12,8,256]{2,1,0:T(8,128)S(1)}, f32[12,8,256]{2,1,0:T(8,128)S(1)}, u32[]{:S(2)}, u32[]{:S(2)}) collective-permute-start(f32[12,8,256]{2,1,0:T(8,128)S(1)} %get-tuple-element.22), channel_id=1, source_target_pairs={{0,1},{1,0},{2,3},{3,2},{4,5},{5,4},{6,7},{7,6},{8,9},{9,8},{10,11... | collective-permute-start | bytes 294920 | tf_op jit(solution)/shard_map/ppermute | solution.py:58
  8.5 0.0 copy-done.3
  8.5 0.7 %shard_map.122._.place = s32[1,4096]{1,0:T(1,128)S(1)} custom-call(s32[1,4096]{1,0:T(1,128)S(1)} %copy-done.3), custom_call_target="tpu_custom_call" | custom-call | flops 1000000000 | bytes 125000000 | tf_op jit(solution)/shard_map/pallas_call | solution.py:490
  9.2 0.0 copy-start.2
  9.2 0.0 copy-start.4
  9.2 0.0 copy-start.5
  9.2 0.0 collective-permute-done.y_odd
  9.2 2.0 %collective-permute-done.1.y_even = f32[12,8,256]{2,1,0:T(8,128)S(1)} collective-permute-done((f32[12,8,256]{2,1,0:T(8,128)S(1)}, f32[12,8,256]{2,1,0:T(8,128)S(1)}, u32[]{:S(2)}, u32[]{:S(2)}) %collective-permute-start.1) | collective-permute-done | bytes 98336 | tf_op jit(solution)/shard_map/ppermute | solution.py:58
  11.3 0.0 copy-start.6
  11.3 0.0 copy-start.7
  11.3 0.0 copy-start.8
  11.3 11.5 %collective-permute-start.2 = (f32[13,8,256]{2,1,0:T(8,128)S(1)}, f32[13,8,256]{2,1,0:T(8,128)S(1)}, u32[]{:S(2)}, u32[]{:S(2)}) collective-permute-start(f32[13,8,256]{2,1,0:T(8,128)S(1)} %get-tuple-element.23), channel_id=1, source_target_pairs={{8,16},{16,8},{24,32},{32,24},{40,48},{48,40},{56,64},{64,56},{72,... | collective-permute-start | bytes 319496 | tf_op jit(solution)/shard_map/ppermute | solution.py:58
  22.8 1.9 %collective-permute-start.3 = (f32[13,8,256]{2,1,0:T(8,128)S(1)}, f32[13,8,256]{2,1,0:T(8,128)S(1)}, u32[]{:S(2)}, u32[]{:S(2)}) collective-permute-start(f32[13,8,256]{2,1,0:T(8,128)S(1)} %get-tuple-element.24._), channel_id=1, source_target_pairs={{0,8},{8,0},{16,24},{24,16},{32,40},{40,32},{48,56},{56,48},{64,72... | collective-permute-start | bytes 319496 | tf_op jit(solution)/shard_map/ppermute | solution.py:58
  24.8 4.4 %shard_map.124 = (f32[3,64,256]{2,1,0:T(8,128)S(1)}, f32[4,2,8,256]{3,2,1,0:T(8,128)S(1)}, f32[5,1,4096]{2,1,0:T(1,128)}) custom-call(f32[5,8,8,256]{3,2,1,0:T(8,128)S(1)} %copy-done, f32[4,1,4096]{2,1,0:T(1,128)S(1)} %copy-done.2, f32[1,4096]{1,0:T(1,128)S(1)} %copy-done.4, s32[1,4096]{1,0:T(1,128)S(1)} %copy-done.5, s32[1,4096]{1,0:T(1,128)S(1)} %copy-done.3, ...), custom_call_target="tpu_custom_call" | custom-call | flops 2000000000 | bytes 250000000 | tf_op jit(solution)/shard_map/pallas_call | solution.py:492
  29.2 0.0 collective-permute-done.2.x_odd
  29.2 0.0 collective-permute-done.3.x_even
  29.2 0.9 %shard_map.125 = (f32[3,8,8,256]{3,2,1,0:T(8,128)S(1)}, f32[18,8,256]{2,1,0:T(8,128)S(1)}, f32[18,8,256]{2,1,0:T(8,128)S(1)}) custom-call(f32[5,8,8,256]{3,2,1,0:T(8,128)S(1)} %copy-done, f32[8,8,256]{2,1,0:T(8,128)S(1)} %copy-done.1, f32[12,8,256]{2,1,0:T(8,128)S(1)} %collective-permute-done.y_odd, f32[12,8,256]{2,1,0:T(8,128)S(1)} %collective-permute-done.1.y_even, ...), custom_call_target="tpu_custom_call" | custom-call | flops 10000000 | bytes 1250000 | tf_op jit(solution)/shard_map/pallas_call | solution.py:503
  30.2 0.7 %collective-permute-start.4 = (f32[18,8,256]{2,1,0:T(8,128)S(1)}, f32[18,8,256]{2,1,0:T(8,128)S(1)}, u32[]{:S(2)}, u32[]{:S(2)}) collective-permute-start(f32[18,8,256]{2,1,0:T(8,128)S(1)} %get-tuple-element.28._), channel_id=1, source_target_pairs={{1,2},{2,1},{3,4},{4,3},{5,6},{6,5},{9,10},{10,9},{11,12},{12,11},... | collective-permute-start | bytes 442376 | tf_op jit(solution)/shard_map/ppermute | solution.py:58
  30.9 6.1 %collective-permute-start.5 = (f32[18,8,256]{2,1,0:T(8,128)S(1)}, f32[18,8,256]{2,1,0:T(8,128)S(1)}, u32[]{:S(2)}, u32[]{:S(2)}) collective-permute-start(f32[18,8,256]{2,1,0:T(8,128)S(1)} %get-tuple-element.29.own), channel_id=1, source_target_pairs={{0,1},{1,0},{2,3},{3,2},{4,5},{5,4},{6,7},{7,6},{8,9},{9,8},{10,11... | collective-permute-start | bytes 442376 | tf_op jit(solution)/shard_map/ppermute | solution.py:58
  37.0 0.0 collective-permute-done.4.y_odd
  37.0 5.4 %collective-permute-done.5.y_even = f32[18,8,256]{2,1,0:T(8,128)S(1)} collective-permute-done((f32[18,8,256]{2,1,0:T(8,128)S(1)}, f32[18,8,256]{2,1,0:T(8,128)S(1)}, u32[]{:S(2)}, u32[]{:S(2)}) %collective-permute-start.5) | collective-permute-done | bytes 147488 | tf_op jit(solution)/shard_map/ppermute | solution.py:58
  42.4 0.7 %shard_map.127 = (f32[17,8,256]{2,1,0:T(8,128)S(1)}, f32[17,8,256]{2,1,0:T(8,128)S(1)}, f32[8,24,256]{2,1,0:T(8,128)S(1)}, f32[8,24,256]{2,1,0:T(8,128)S(1)}) custom-call(f32[18,8,256]{2,1,0:T(8,128)S(1)} %get-tuple-element.29.own, f32[18,8,256]{2,1,0:T(8,128)S(1)} %collective-permute-done.4.y_odd, f32[18,8,256]{2,1,0:T(8,128)S(1)} %collective-permute-done.5.y_even, ...), custom_call_target="tpu_custom_call" | custom-call | flops 10000000 | bytes 1250000 | tf_op jit(solution)/shard_map/pallas_call | solution.py:522
  43.1 3.2 %collective-permute-start.6 = (f32[17,8,256]{2,1,0:T(8,128)S(1)}, f32[17,8,256]{2,1,0:T(8,128)S(1)}, u32[]{:S(2)}, u32[]{:S(2)}) collective-permute-start(f32[17,8,256]{2,1,0:T(8,128)S(1)} %get-tuple-element.32), channel_id=1, source_target_pairs={{8,16},{16,8},{24,32},{32,24},{40,48},{48,40},{56,64},{64,56},{72,... | collective-permute-start | bytes 417800 | tf_op jit(solution)/shard_map/ppermute | solution.py:58
  46.4 1.9 %collective-permute-start.7 = (f32[17,8,256]{2,1,0:T(8,128)S(1)}, f32[17,8,256]{2,1,0:T(8,128)S(1)}, u32[]{:S(2)}, u32[]{:S(2)}) collective-permute-start(f32[17,8,256]{2,1,0:T(8,128)S(1)} %get-tuple-element.33), channel_id=1, source_target_pairs={{0,8},{8,0},{16,24},{24,16},{32,40},{40,32},{48,56},{56,48},{64,72... | collective-permute-start | bytes 417800 | tf_op jit(solution)/shard_map/ppermute | solution.py:58
  48.3 0.3 shard_map.126.star_rest
  48.6 4.9 %collective-permute-done.6.x_odd = f32[17,8,256]{2,1,0:T(8,128)S(1)} collective-permute-done((f32[17,8,256]{2,1,0:T(8,128)S(1)}, f32[17,8,256]{2,1,0:T(8,128)S(1)}, u32[]{:S(2)}, u32[]{:S(2)}) %collective-permute-start.6) | collective-permute-done | bytes 139296 | tf_op jit(solution)/shard_map/ppermute | solution.py:58
  53.5 0.0 collective-permute-done.7.x_even
  53.5 1.9 %shard_map.128 = (f32[5,8,8,256]{3,2,1,0:T(8,128)}, f32[8,8,256]{2,1,0:T(8,128)}, f32[4,5,1,512]{3,2,1,0:T(1,128)}) custom-call(f32[3,8,8,256]{3,2,1,0:T(8,128)S(1)} %get-tuple-element.27.star, f32[2,8,8,256]{3,2,1,0:T(8,128)S(1)} %shard_map.126.star_rest, f32[8,24,256]{2,1,0:T(8,128)S(1)} %get-tuple-element.30.first, ...), custom_call_target="tpu_custom_call" | custom-call | flops 10000000 | bytes 1250000 | tf_op jit(solution)/shard_map/pallas_call | solution.py:532
  (11 shorter events, 0.1 us)
Async XLA Ops:
  0.6 1.0 %copy-start = (f32[5,8,8,256]{3,2,1,0:T(8,128)S(1)}, f32[5,8,8,256]{3,2,1,0:T(8,128)}, u32[]{:S(2)}) copy-start(f32[5,8,8,256]{3,2,1,0:T(8,128)} %gas.9) | copy-start | bytes 983044
  0.6 1.0 %copy-start.1 = (f32[8,8,256]{2,1,0:T(8,128)S(1)}, f32[8,8,256]{2,1,0:T(8,128)}, u32[]{:S(2)}) copy-start(f32[8,8,256]{2,1,0:T(8,128)} %guess.5) | copy-start | bytes 196612
  1.6 6.9 %copy-start.3 = (s32[1,4096]{1,0:T(1,128)S(1)}, s32[1,4096]{1,0:T(1,128)}, u32[]{:S(2)}) copy-start(s32[1,4096]{1,0:T(1,128)} %target.3) | copy-start | bytes 49156
  1.7 7.5 %collective-permute-start = (f32[12,8,256]{2,1,0:T(8,128)S(1)}, f32[12,8,256]{2,1,0:T(8,128)S(1)}, u32[]{:S(2)}, u32[]{:S(2)}) collective-permute-start(f32[12,8,256]{2,1,0:T(8,128)S(1)} %get-tuple-element.21), channel_id=1, source_target_pairs={{1,2},{2,1},{3,4},{4,3},{5,6},{6,5},{9,10},{10,9},{11,12},{12,11},... | collective-permute-start | bytes 294920 | tf_op jit(solution)/shard_map/ppermute | solution.py:58
  2.4 8.9 %collective-permute-start.1 = (f32[12,8,256]{2,1,0:T(8,128)S(1)}, f32[12,8,256]{2,1,0:T(8,128)S(1)}, u32[]{:S(2)}, u32[]{:S(2)}) collective-permute-start(f32[12,8,256]{2,1,0:T(8,128)S(1)} %get-tuple-element.22), channel_id=1, source_target_pairs={{0,1},{1,0},{2,3},{3,2},{4,5},{5,4},{6,7},{7,6},{8,9},{9,8},{10,11... | collective-permute-start | bytes 294920 | tf_op jit(solution)/shard_map/ppermute | solution.py:58
  9.2 15.5 %copy-start.2 = (f32[4,1,4096]{2,1,0:T(1,128)S(1)}, f32[4,1,4096]{2,1,0:T(1,128)}, u32[]{:S(2)}) copy-start(f32[4,1,4096]{2,1,0:T(1,128)} %motion.1) | copy-start | bytes 196612
  9.2 15.5 %copy-start.4 = (f32[1,4096]{1,0:T(1,128)S(1)}, f32[1,4096]{1,0:T(1,128)}, u32[]{:S(2)}) copy-start(f32[1,4096]{1,0:T(1,128)} %size.1) | copy-start | bytes 49156
  9.2 15.5 %copy-start.5 = (s32[1,4096]{1,0:T(1,128)S(1)}, s32[1,4096]{1,0:T(1,128)}, u32[]{:S(2)}) copy-start(s32[1,4096]{1,0:T(1,128)} %cell.1) | copy-start | bytes 49156
  11.3 13.5 %copy-start.6 = (s32[1,8]{1,0:T(1,128)S(1)}, s32[1,8]{1,0:T(1,128)}, u32[]{:S(2)}) copy-start(s32[1,8]{1,0:T(1,128)} %on.1) | copy-start | bytes 100
  11.3 13.5 %copy-start.7 = (s32[1,8]{1,0:T(1,128)S(1)}, s32[1,8]{1,0:T(1,128)}, u32[]{:S(2)}) copy-start(s32[1,8]{1,0:T(1,128)} %when.1) | copy-start | bytes 100
  11.3 13.5 %copy-start.8 = (s32[1,8]{1,0:T(1,128)S(1)}, s32[1,8]{1,0:T(1,128)}, u32[]{:S(2)}) copy-start(s32[1,8]{1,0:T(1,128)} %head.1) | copy-start | bytes 100
  11.3 17.9 %collective-permute-start.2 = (f32[13,8,256]{2,1,0:T(8,128)S(1)}, f32[13,8,256]{2,1,0:T(8,128)S(1)}, u32[]{:S(2)}, u32[]{:S(2)}) collective-permute-start(f32[13,8,256]{2,1,0:T(8,128)S(1)} %get-tuple-element.23), channel_id=1, source_target_pairs={{8,16},{16,8},{24,32},{32,24},{40,48},{48,40},{56,64},{64,56},{72,... | collective-permute-start | bytes 319496 | tf_op jit(solution)/shard_map/ppermute | solution.py:58
  22.8 6.4 %collective-permute-start.3 = (f32[13,8,256]{2,1,0:T(8,128)S(1)}, f32[13,8,256]{2,1,0:T(8,128)S(1)}, u32[]{:S(2)}, u32[]{:S(2)}) collective-permute-start(f32[13,8,256]{2,1,0:T(8,128)S(1)} %get-tuple-element.24._), channel_id=1, source_target_pairs={{0,8},{8,0},{16,24},{24,16},{32,40},{40,32},{48,56},{56,48},{64,72... | collective-permute-start | bytes 319496 | tf_op jit(solution)/shard_map/ppermute | solution.py:58
  30.2 6.8 %collective-permute-start.4 = (f32[18,8,256]{2,1,0:T(8,128)S(1)}, f32[18,8,256]{2,1,0:T(8,128)S(1)}, u32[]{:S(2)}, u32[]{:S(2)}) collective-permute-start(f32[18,8,256]{2,1,0:T(8,128)S(1)} %get-tuple-element.28._), channel_id=1, source_target_pairs={{1,2},{2,1},{3,4},{4,3},{5,6},{6,5},{9,10},{10,9},{11,12},{12,11},... | collective-permute-start | bytes 442376 | tf_op jit(solution)/shard_map/ppermute | solution.py:58
  30.9 11.5 %collective-permute-start.5 = (f32[18,8,256]{2,1,0:T(8,128)S(1)}, f32[18,8,256]{2,1,0:T(8,128)S(1)}, u32[]{:S(2)}, u32[]{:S(2)}) collective-permute-start(f32[18,8,256]{2,1,0:T(8,128)S(1)} %get-tuple-element.29.own), channel_id=1, source_target_pairs={{0,1},{1,0},{2,3},{3,2},{4,5},{5,4},{6,7},{7,6},{8,9},{9,8},{10,11... | collective-permute-start | bytes 442376 | tf_op jit(solution)/shard_map/ppermute | solution.py:58
  43.1 10.4 %collective-permute-start.6 = (f32[17,8,256]{2,1,0:T(8,128)S(1)}, f32[17,8,256]{2,1,0:T(8,128)S(1)}, u32[]{:S(2)}, u32[]{:S(2)}) collective-permute-start(f32[17,8,256]{2,1,0:T(8,128)S(1)} %get-tuple-element.32), channel_id=1, source_target_pairs={{8,16},{16,8},{24,32},{32,24},{40,48},{48,40},{56,64},{64,56},{72,... | collective-permute-start | bytes 417800 | tf_op jit(solution)/shard_map/ppermute | solution.py:58
  46.4 7.2 %collective-permute-start.7 = (f32[17,8,256]{2,1,0:T(8,128)S(1)}, f32[17,8,256]{2,1,0:T(8,128)S(1)}, u32[]{:S(2)}, u32[]{:S(2)}) collective-permute-start(f32[17,8,256]{2,1,0:T(8,128)S(1)} %get-tuple-element.33), channel_id=1, source_target_pairs={{0,8},{8,0},{16,24},{24,16},{32,40},{40,32},{48,56},{56,48},{64,72... | collective-permute-start | bytes 417800 | tf_op jit(solution)/shard_map/ppermute | solution.py:58

commit v5 on v4

--- a/solution.py
+++ b/solution.py
@@ -76,32 +76,17 @@
     return high, value - high
 
 
-def place_kernel(target, place):
+def renew_kernel(gas, motion, size, cell, target, kept, rows):
+    table = jnp.concatenate([gas[f].reshape(B * B, NZ) for f in range(4)], axis=0)
+    high, low = split(table)
+    table = jnp.concatenate([high.astype(BF16), low.astype(BF16)], axis=1)
+    at_z = lax.broadcasted_iota(jnp.int32, (NZ, CHUNK), 0)
+    at_xy = lax.broadcasted_iota(jnp.int32, (B * B, CHUNK), 0)
     heading = lax.broadcasted_iota(jnp.int32, (B, CHUNK), 0)
     a = lax.broadcasted_iota(jnp.int32, (CHUNK, CHUNK), 0)
     b = lax.broadcasted_iota(jnp.int32, (CHUNK, CHUNK), 1)
     upper = jnp.where(a <= b, 1.0, 0.0).astype(BF16)
     before = jnp.zeros((B, 1), F32)
-    for n in range(PD // CHUNK):
-        part = slice(n * CHUNK, (n + 1) * CHUNK)
-        chosen = heading == target[:, part]
-        rank = jnp.dot(jnp.where(chosen, 1.0, 0.0).astype(BF16), upper, preferred_element_type=F32) + before
-        before = rank[:, CHUNK - 1 :]
-        leaves = chosen & (heading < 4)
-        value = jnp.where(leaves, rank + heading.astype(F32) * float(CAP), 0.0)
-        place[:, part] = jnp.sum(value, axis=0, keepdims=True).astype(jnp.int32) - 1
-
-
-def droplet_kernel(gas, motion, size, cell, target, place, on, when, head, _, sources, parcels, kept):
-    table = jnp.concatenate([gas[f].reshape(B * B, NZ) for f in range(4)], axis=0)
-    high, low = split(table)
-    table = jnp.concatenate([high.astype(BF16), low.astype(BF16)], axis=1)
-    at_z = lax.broadcasted_iota(jnp.int32, (NZ, CHUNK), 0)
-    at_xy = lax.broadcasted_iota(jnp.int32, (B * B, CHUNK), 0)
-    at_high = lax.broadcasted_iota(jnp.int32, (B, CHUNK), 0)
-    total = jnp.zeros((4 * B * B, NZ), F32)
-    moved = jnp.zeros((10 * B, NZ), F32)
-    across = (((1,), (1,)), ((), ()))
     for n in range(PD // CHUNK):
         part = slice(n * CHUNK, (n + 1) * CHUNK)
         cells = cell[:, part]
@@ -128,13 +113,36 @@
         alive = goal >= 0
         for f in range(5):
             kept[f, :, part] = jnp.where(goal == 4, renewed[f], 0.0)
-        pieces = [*split(jnp.where(alive, drag, 0.0)), *split(jnp.where(alive, vapour, 0.0))]
+            rows[f : f + 1, part] = renewed[f]
+        rows[5:6, part] = jnp.where(alive, drag, 0.0)
+        rows[6:7, part] = jnp.where(alive, vapour, 0.0)
+        chosen = heading == goal
+        rank = jnp.dot(jnp.where(chosen, 1.0, 0.0).astype(BF16), upper, preferred_element_type=F32) + before
+        before = rank[:, CHUNK - 1 :]
+        leaves = chosen & (heading < 4)
+        place = jnp.where(leaves, rank + heading.astype(F32) * float(CAP), 0.0)
+        rows[7:8, part] = jnp.sum(place, axis=0, keepdims=True) - 1.0
+
+
+def spread_kernel(rows, cell, on, when, head, _, sources, parcels):
+    at_z = lax.broadcasted_iota(jnp.int32, (NZ, CHUNK), 0)
+    at_xy = lax.broadcasted_iota(jnp.int32, (B * B, CHUNK), 0)
+    at_high = lax.broadcasted_iota(jnp.int32, (B, CHUNK), 0)
+    total = jnp.zeros((4 * B * B, NZ), F32)
+    moved = jnp.zeros((10 * B, NZ), F32)
+    across = (((1,), (1,)), ((), ()))
+    for n in range(PD // CHUNK):
+        part = slice(n * CHUNK, (n + 1) * CHUNK)
+        cells = cell[:, part]
+        in_z = jnp.where(at_z == (cells & (NZ - 1)), 1.0, 0.0).astype(BF16)
+        in_xy = at_xy == (cells >> 8)
+        pieces = [*split(rows[5:6, part]), *split(rows[6:7, part])]
         given = jnp.concatenate([jnp.where(in_xy, piece, 0.0).astype(BF16) for piece in pieces], axis=0)
         total = total + lax.dot_general(given, in_z, across, preferred_element_type=F32)
-        spot = place[:, part]
-        in_low = jnp.where(at_z == (spot & (NZ - 1)), 1.0, 0.0).astype(BF16)
-        in_high = at_high == (spot >> 8)
-        split_up = [split(value) for value in renewed]
+        place = rows[7:8, part].astype(jnp.int32)
+        in_low = jnp.where(at_z == (place & (NZ - 1)), 1.0, 0.0).astype(BF16)
+        in_high = at_high == (place >> 8)
+        split_up = [split(rows[f : f + 1, part]) for f in range(5)]
         leaving = [jnp.where(in_high, split_up[f][piece], 0.0) for piece in range(2) for f in range(5)]
         moved = moved + lax.dot_general(
             jnp.concatenate(leaving, axis=0).astype(BF16), in_low, across, preferred_element_type=F32
@@ -487,15 +495,17 @@
     y_even, y_odd = call(pack_y_kernel, [tiles(NL)] * 2, 3, 10**6)(first, gas, guess)
     y_odd = swap(y_odd, "gy", 1)
     y_even = swap(y_even, "gy", 0)
-    [place] = call(place_kernel, [shape((1, PD), jnp.int32)], 1, 10**9)(target)
-    x_even, x_odd = call(pack_x_kernel, [tiles(NL + 1)] * 2, 5, 10**6)(gas, guess, y_odd, y_even, place)
-    sources, parcels, kept = call(
-        droplet_kernel,
-        [shape((3, B * B, NZ), F32), shape((4, 2, B, NZ), F32), shape((5, 1, PD), F32)],
-        10,
-        2 * 10**9,
-        smem=(6, 7, 8),
-    )(gas, motion, size, cell, target, place, on, when, head, x_even)
+    kept, rows = call(renew_kernel, [shape((5, 1, PD), F32), shape((8, PD), F32)], 5, 10**9)(
+        gas, motion, size, cell, target
+    )
+    x_even, x_odd = call(pack_x_kernel, [tiles(NL + 1)] * 2, 5, 10**6)(gas, guess, y_odd, y_even, rows)
+    sources, parcels = call(
+        spread_kernel,
+        [shape((3, B * B, NZ), F32), shape((4, 2, B, NZ), F32)],
+        6,
+        10**9,
+        smem=(2, 3, 4),
+    )(rows, cell, on, when, head, x_even)
     sources = sources.reshape(3, B, B, NZ)
     x_odd = swap(x_odd, "gx", 1)
     x_even = swap(x_even, "gx", 0)

time: 55.8 us -> 54.3 us (0.973)
  waiting for transfers between devices: 12.4 us -> 10.5 us
    ppermute x8, waiting for transfers between devices: 12.4 us -> 10.5 us  [swap(): return lax.ppermute(shard, axis, pairs)]
  transfers between devices with their start and end apart: 8 -> 8, of which waited for: 3 -> 2; matrix products, arithmetic and copies ran while one was open for 0% -> 0% of each run, Pallas kernels for 10% -> 10%
where the time goes in v5:
time: 54.3 us; the launch traced here: 53.9 us
  starting transfers between devices  32.4 us (60%)
  waiting for transfers between devices  10.5 us (19%)
  Pallas kernels  9.21 us (17%)
  local copies, waits for them, and re-layouts  0.99 us (2%)
  between operations  0.88 us (2%)
    ppermute x8, starting transfers between devices, swap(): return lax.ppermute(shard, axis, pairs)  32.4 us
    ppermute x8, waiting for transfers between devices, swap(): return lax.ppermute(shard, axis, pairs)  10.5 us
    pallas_call x1, Pallas kernels, body(): call(renew_kernel, [shape((5, 1, PD), F32), shape((8, PD), F32)], 5, 10 *...  3.25 us
    pallas_call x1, Pallas kernels, body(): call(finish_kernel, [shape((5, B, B, NZ), F32), shape((B, B, NZ), F32), s...  1.93 us
    pallas_call x1, Pallas kernels, body(): call(spread_kernel, [shape((3, B * B, NZ), F32), shape((4, 2, B, NZ), F32...  1.92 us
  transfers between devices with their start and end apart: 8, of which 2 were waited for; matrix products, arithmetic and copies ran while one was open for 0% of the time, Pallas kernels for 10%

profile of v5, /device:TPU:48, one launch (start us, length us, event | category | flops | bytes accessed | tf_op | source)
XLA Modules:
  0.0 53.9 jit_solution(7288105517661028367)
XLA Ops:
  0.7 0.9 %copy-done = f32[5,8,8,256]{3,2,1,0:T(8,128)S(1)} copy-done((f32[5,8,8,256]{3,2,1,0:T(8,128)S(1)}, f32[5,8,8,256]{3,2,1,0:T(8,128)}, u32[]{:S(2)}) %copy-start) | copy-done | bytes 327704
  1.6 0.0 copy-done.1
  1.6 0.0 copy-start.5
  1.6 0.1 shard_map.121
  1.7 0.7 %collective-permute-start = (f32[12,8,256]{2,1,0:T(8,128)S(1)}, f32[12,8,256]{2,1,0:T(8,128)S(1)}, u32[]{:S(2)}, u32[]{:S(2)}) collective-permute-start(f32[12,8,256]{2,1,0:T(8,128)S(1)} %get-tuple-element.22), channel_id=1, source_target_pairs={{1,2},{2,1},{3,4},{4,3},{5,6},{6,5},{9,10},{10,9},{11,12},{12,11},... | collective-permute-start | bytes 294920 | tf_op jit(solution)/shard_map/ppermute | solution.py:58
  2.4 6.1 %collective-permute-start.1 = (f32[12,8,256]{2,1,0:T(8,128)S(1)}, f32[12,8,256]{2,1,0:T(8,128)S(1)}, u32[]{:S(2)}, u32[]{:S(2)}) collective-permute-start(f32[12,8,256]{2,1,0:T(8,128)S(1)} %get-tuple-element.23), channel_id=1, source_target_pairs={{0,1},{1,0},{2,3},{3,2},{4,5},{5,4},{6,7},{7,6},{8,9},{9,8},{10,11... | collective-permute-start | bytes 294920 | tf_op jit(solution)/shard_map/ppermute | solution.py:58
  8.5 3.2 %shard_map.122 = (f32[5,1,4096]{2,1,0:T(1,128)}, f32[8,4096]{1,0:T(8,128)S(1)}) custom-call(f32[5,8,8,256]{3,2,1,0:T(8,128)S(1)} %copy-done, f32[4,1,4096]{2,1,0:T(1,128)S(1)} %copy-done.2, f32[1,4096]{1,0:T(1,128)S(1)} %copy-done.3, s32[1,4096]{1,0:T(1,128)S(1)} %copy-done.5, s32[1,4096]{1,0:T(1,128)S(1)} %copy-done.4), custom_call_target="tpu_custom_call" | custom-call | flops 1000000000 | bytes 125000000 | tf_op jit(solution)/shard_map/pallas_call | solution.py:498
  11.8 0.0 collective-permute-done.y_odd
  11.8 0.0 collective-permute-done.1.y_even
  11.8 0.0 copy-start.6
  11.9 0.0 copy-start.7
  11.9 0.0 copy-start.8
  11.9 11.5 %collective-permute-start.2 = (f32[13,8,256]{2,1,0:T(8,128)S(1)}, f32[13,8,256]{2,1,0:T(8,128)S(1)}, u32[]{:S(2)}, u32[]{:S(2)}) collective-permute-start(f32[13,8,256]{2,1,0:T(8,128)S(1)} %get-tuple-element.25), channel_id=1, source_target_pairs={{8,16},{16,8},{24,32},{32,24},{40,48},{48,40},{56,64},{64,56},{72,... | collective-permute-start | bytes 319496 | tf_op jit(solution)/shard_map/ppermute | solution.py:58
  23.4 1.9 %collective-permute-start.3 = (f32[13,8,256]{2,1,0:T(8,128)S(1)}, f32[13,8,256]{2,1,0:T(8,128)S(1)}, u32[]{:S(2)}, u32[]{:S(2)}) collective-permute-start(f32[13,8,256]{2,1,0:T(8,128)S(1)} %get-tuple-element.26._), channel_id=1, source_target_pairs={{0,8},{8,0},{16,24},{24,16},{32,40},{40,32},{48,56},{56,48},{64,72... | collective-permute-start | bytes 319496 | tf_op jit(solution)/shard_map/ppermute | solution.py:58
  25.3 0.0 copy-done.6
  25.4 0.0 copy-done.7
  25.4 0.0 copy-done.8
  25.4 1.9 %shard_map.124 = (f32[3,64,256]{2,1,0:T(8,128)S(1)}, f32[4,2,8,256]{3,2,1,0:T(8,128)S(1)}) custom-call(f32[8,4096]{1,0:T(8,128)S(1)} %get-tuple-element.24._.rows, s32[1,4096]{1,0:T(1,128)S(1)} %copy-done.5, s32[1,8]{1,0:T(1,128)S(1)} %copy-done.6, s32[1,8]{1,0:T(1,128)S(1)} %copy-done.7, s32[1,8]{1,0:T(1,128)S(1)} %copy-done.8, ...), custom_call_target="tpu_custom_call" | custom-call | flops 1000000000 | bytes 125000000 | tf_op jit(solution)/shard_map/pallas_call | solution.py:502
  27.3 0.0 collective-permute-done.2.x_odd
  27.3 0.0 collective-permute-done.3.x_even
  27.3 1.0 %shard_map.125 = (f32[3,8,8,256]{3,2,1,0:T(8,128)S(1)}, f32[18,8,256]{2,1,0:T(8,128)S(1)}, f32[18,8,256]{2,1,0:T(8,128)S(1)}) custom-call(f32[5,8,8,256]{3,2,1,0:T(8,128)S(1)} %copy-done, f32[8,8,256]{2,1,0:T(8,128)S(1)} %copy-done.1, f32[12,8,256]{2,1,0:T(8,128)S(1)} %collective-permute-done.y_odd, f32[12,8,256]{2,1,0:T(8,128)S(1)} %collective-permute-done.1.y_even, ...), custom_call_target="tpu_custom_call" | custom-call | flops 10000000 | bytes 1250000 | tf_op jit(solution)/shard_map/pallas_call | solution.py:513
  28.3 0.7 %collective-permute-start.4 = (f32[18,8,256]{2,1,0:T(8,128)S(1)}, f32[18,8,256]{2,1,0:T(8,128)S(1)}, u32[]{:S(2)}, u32[]{:S(2)}) collective-permute-start(f32[18,8,256]{2,1,0:T(8,128)S(1)} %get-tuple-element.30._), channel_id=1, source_target_pairs={{1,2},{2,1},{3,4},{4,3},{5,6},{6,5},{9,10},{10,9},{11,12},{12,11},... | collective-permute-start | bytes 442376 | tf_op jit(solution)/shard_map/ppermute | solution.py:58
  29.0 6.1 %collective-permute-start.5 = (f32[18,8,256]{2,1,0:T(8,128)S(1)}, f32[18,8,256]{2,1,0:T(8,128)S(1)}, u32[]{:S(2)}, u32[]{:S(2)}) collective-permute-start(f32[18,8,256]{2,1,0:T(8,128)S(1)} %get-tuple-element.31.own), channel_id=1, source_target_pairs={{0,1},{1,0},{2,3},{3,2},{4,5},{5,4},{6,7},{7,6},{8,9},{9,8},{10,11... | collective-permute-start | bytes 442376 | tf_op jit(solution)/shard_map/ppermute | solution.py:58
  35.1 0.0 collective-permute-done.4.y_odd
  35.1 5.4 %collective-permute-done.5.y_even = f32[18,8,256]{2,1,0:T(8,128)S(1)} collective-permute-done((f32[18,8,256]{2,1,0:T(8,128)S(1)}, f32[18,8,256]{2,1,0:T(8,128)S(1)}, u32[]{:S(2)}, u32[]{:S(2)}) %collective-permute-start.5) | collective-permute-done | bytes 147488 | tf_op jit(solution)/shard_map/ppermute | solution.py:58
  40.5 0.7 %shard_map.127 = (f32[17,8,256]{2,1,0:T(8,128)S(1)}, f32[17,8,256]{2,1,0:T(8,128)S(1)}, f32[8,24,256]{2,1,0:T(8,128)S(1)}, f32[8,24,256]{2,1,0:T(8,128)S(1)}) custom-call(f32[18,8,256]{2,1,0:T(8,128)S(1)} %get-tuple-element.31.own, f32[18,8,256]{2,1,0:T(8,128)S(1)} %collective-permute-done.4.y_odd, f32[18,8,256]{2,1,0:T(8,128)S(1)} %collective-permute-done.5.y_even, ...), custom_call_target="tpu_custom_call" | custom-call | flops 10000000 | bytes 1250000 | tf_op jit(solution)/shard_map/pallas_call | solution.py:532
  41.2 3.5 %collective-permute-start.6 = (f32[17,8,256]{2,1,0:T(8,128)S(1)}, f32[17,8,256]{2,1,0:T(8,128)S(1)}, u32[]{:S(2)}, u32[]{:S(2)}) collective-permute-start(f32[17,8,256]{2,1,0:T(8,128)S(1)} %get-tuple-element.34), channel_id=1, source_target_pairs={{8,16},{16,8},{24,32},{32,24},{40,48},{48,40},{56,64},{64,56},{72,... | collective-permute-start | bytes 417800 | tf_op jit(solution)/shard_map/ppermute | solution.py:58
  44.7 1.9 %collective-permute-start.7 = (f32[17,8,256]{2,1,0:T(8,128)S(1)}, f32[17,8,256]{2,1,0:T(8,128)S(1)}, u32[]{:S(2)}, u32[]{:S(2)}) collective-permute-start(f32[17,8,256]{2,1,0:T(8,128)S(1)} %get-tuple-element.35), channel_id=1, source_target_pairs={{0,8},{8,0},{16,24},{24,16},{32,40},{40,32},{48,56},{56,48},{64,72... | collective-permute-start | bytes 417800 | tf_op jit(solution)/shard_map/ppermute | solution.py:58
  46.7 0.3 shard_map.126.star_rest
  47.0 5.0 %collective-permute-done.6.x_odd = f32[17,8,256]{2,1,0:T(8,128)S(1)} collective-permute-done((f32[17,8,256]{2,1,0:T(8,128)S(1)}, f32[17,8,256]{2,1,0:T(8,128)S(1)}, u32[]{:S(2)}, u32[]{:S(2)}) %collective-permute-start.6) | collective-permute-done | bytes 139296 | tf_op jit(solution)/shard_map/ppermute | solution.py:58
  52.0 0.0 collective-permute-done.7.x_even
  52.0 1.9 %shard_map.128 = (f32[5,8,8,256]{3,2,1,0:T(8,128)}, f32[8,8,256]{2,1,0:T(8,128)}, f32[4,5,1,512]{3,2,1,0:T(1,128)}) custom-call(f32[3,8,8,256]{3,2,1,0:T(8,128)S(1)} %get-tuple-element.29.star, f32[2,8,8,256]{3,2,1,0:T(8,128)S(1)} %shard_map.126.star_rest, f32[8,24,256]{2,1,0:T(8,128)S(1)} %get-tuple-element.32.first, ...), custom_call_target="tpu_custom_call" | custom-call | flops 10000000 | bytes 1250000 | tf_op jit(solution)/shard_map/pallas_call | solution.py:542
  (11 shorter events, 0.1 us)
Async XLA Ops:
  0.6 1.0 %copy-start = (f32[5,8,8,256]{3,2,1,0:T(8,128)S(1)}, f32[5,8,8,256]{3,2,1,0:T(8,128)}, u32[]{:S(2)}) copy-start(f32[5,8,8,256]{3,2,1,0:T(8,128)} %gas.9) | copy-start | bytes 983044
  0.6 1.0 %copy-start.1 = (f32[8,8,256]{2,1,0:T(8,128)S(1)}, f32[8,8,256]{2,1,0:T(8,128)}, u32[]{:S(2)}) copy-start(f32[8,8,256]{2,1,0:T(8,128)} %guess.5) | copy-start | bytes 196612
  1.6 6.9 %copy-start.2 = (f32[4,1,4096]{2,1,0:T(1,128)S(1)}, f32[4,1,4096]{2,1,0:T(1,128)}, u32[]{:S(2)}) copy-start(f32[4,1,4096]{2,1,0:T(1,128)} %motion.1) | copy-start | bytes 196612
  1.6 6.9 %copy-start.3 = (f32[1,4096]{1,0:T(1,128)S(1)}, f32[1,4096]{1,0:T(1,128)}, u32[]{:S(2)}) copy-start(f32[1,4096]{1,0:T(1,128)} %size.1) | copy-start | bytes 49156
  1.6 6.9 %copy-start.4 = (s32[1,4096]{1,0:T(1,128)S(1)}, s32[1,4096]{1,0:T(1,128)}, u32[]{:S(2)}) copy-start(s32[1,4096]{1,0:T(1,128)} %target.1) | copy-start | bytes 49156
  1.6 6.9 %copy-start.5 = (s32[1,4096]{1,0:T(1,128)S(1)}, s32[1,4096]{1,0:T(1,128)}, u32[]{:S(2)}) copy-start(s32[1,4096]{1,0:T(1,128)} %cell.3) | copy-start | bytes 49156
  1.7 10.1 %collective-permute-start = (f32[12,8,256]{2,1,0:T(8,128)S(1)}, f32[12,8,256]{2,1,0:T(8,128)S(1)}, u32[]{:S(2)}, u32[]{:S(2)}) collective-permute-start(f32[12,8,256]{2,1,0:T(8,128)S(1)} %get-tuple-element.22), channel_id=1, source_target_pairs={{1,2},{2,1},{3,4},{4,3},{5,6},{6,5},{9,10},{10,9},{11,12},{12,11},... | collective-permute-start | bytes 294920 | tf_op jit(solution)/shard_map/ppermute | solution.py:58
  2.4 9.4 %collective-permute-start.1 = (f32[12,8,256]{2,1,0:T(8,128)S(1)}, f32[12,8,256]{2,1,0:T(8,128)S(1)}, u32[]{:S(2)}, u32[]{:S(2)}) collective-permute-start(f32[12,8,256]{2,1,0:T(8,128)S(1)} %get-tuple-element.23), channel_id=1, source_target_pairs={{0,1},{1,0},{2,3},{3,2},{4,5},{5,4},{6,7},{7,6},{8,9},{9,8},{10,11... | collective-permute-start | bytes 294920 | tf_op jit(solution)/shard_map/ppermute | solution.py:58
  11.8 13.5 %copy-start.6 = (s32[1,8]{1,0:T(1,128)S(1)}, s32[1,8]{1,0:T(1,128)}, u32[]{:S(2)}) copy-start(s32[1,8]{1,0:T(1,128)} %on.1) | copy-start | bytes 100
  11.9 13.5 %copy-start.7 = (s32[1,8]{1,0:T(1,128)S(1)}, s32[1,8]{1,0:T(1,128)}, u32[]{:S(2)}) copy-start(s32[1,8]{1,0:T(1,128)} %when.1) | copy-start | bytes 100
  11.9 13.5 %copy-start.8 = (s32[1,8]{1,0:T(1,128)S(1)}, s32[1,8]{1,0:T(1,128)}, u32[]{:S(2)}) copy-start(s32[1,8]{1,0:T(1,128)} %head.1) | copy-start | bytes 100
  11.9 15.4 %collective-permute-start.2 = (f32[13,8,256]{2,1,0:T(8,128)S(1)}, f32[13,8,256]{2,1,0:T(8,128)S(1)}, u32[]{:S(2)}, u32[]{:S(2)}) collective-permute-start(f32[13,8,256]{2,1,0:T(8,128)S(1)} %get-tuple-element.25), channel_id=1, source_target_pairs={{8,16},{16,8},{24,32},{32,24},{40,48},{48,40},{56,64},{64,56},{72,... | collective-permute-start | bytes 319496 | tf_op jit(solution)/shard_map/ppermute | solution.py:58
  23.4 3.9 %collective-permute-start.3 = (f32[13,8,256]{2,1,0:T(8,128)S(1)}, f32[13,8,256]{2,1,0:T(8,128)S(1)}, u32[]{:S(2)}, u32[]{:S(2)}) collective-permute-start(f32[13,8,256]{2,1,0:T(8,128)S(1)} %get-tuple-element.26._), channel_id=1, source_target_pairs={{0,8},{8,0},{16,24},{24,16},{32,40},{40,32},{48,56},{56,48},{64,72... | collective-permute-start | bytes 319496 | tf_op jit(solution)/shard_map/ppermute | solution.py:58
  28.3 6.8 %collective-permute-start.4 = (f32[18,8,256]{2,1,0:T(8,128)S(1)}, f32[18,8,256]{2,1,0:T(8,128)S(1)}, u32[]{:S(2)}, u32[]{:S(2)}) collective-permute-start(f32[18,8,256]{2,1,0:T(8,128)S(1)} %get-tuple-element.30._), channel_id=1, source_target_pairs={{1,2},{2,1},{3,4},{4,3},{5,6},{6,5},{9,10},{10,9},{11,12},{12,11},... | collective-permute-start | bytes 442376 | tf_op jit(solution)/shard_map/ppermute | solution.py:58
  29.0 11.5 %collective-permute-start.5 = (f32[18,8,256]{2,1,0:T(8,128)S(1)}, f32[18,8,256]{2,1,0:T(8,128)S(1)}, u32[]{:S(2)}, u32[]{:S(2)}) collective-permute-start(f32[18,8,256]{2,1,0:T(8,128)S(1)} %get-tuple-element.31.own), channel_id=1, source_target_pairs={{0,1},{1,0},{2,3},{3,2},{4,5},{5,4},{6,7},{7,6},{8,9},{9,8},{10,11... | collective-permute-start | bytes 442376 | tf_op jit(solution)/shard_map/ppermute | solution.py:58
  41.2 10.8 %collective-permute-start.6 = (f32[17,8,256]{2,1,0:T(8,128)S(1)}, f32[17,8,256]{2,1,0:T(8,128)S(1)}, u32[]{:S(2)}, u32[]{:S(2)}) collective-permute-start(f32[17,8,256]{2,1,0:T(8,128)S(1)} %get-tuple-element.34), channel_id=1, source_target_pairs={{8,16},{16,8},{24,32},{32,24},{40,48},{48,40},{56,64},{64,56},{72,... | collective-permute-start | bytes 417800 | tf_op jit(solution)/shard_map/ppermute | solution.py:58
  44.7 7.3 %collective-permute-start.7 = (f32[17,8,256]{2,1,0:T(8,128)S(1)}, f32[17,8,256]{2,1,0:T(8,128)S(1)}, u32[]{:S(2)}, u32[]{:S(2)}) collective-permute-start(f32[17,8,256]{2,1,0:T(8,128)S(1)} %get-tuple-element.35), channel_id=1, source_target_pairs={{0,8},{8,0},{16,24},{24,16},{32,40},{40,32},{48,56},{56,48},{64,72... | collective-permute-start | bytes 417800 | tf_op jit(solution)/shard_map/ppermute | solution.py:58

commit v6 on v4

--- a/solution.py
+++ b/solution.py
@@ -76,37 +76,45 @@
     return high, value - high
 
 
-def place_kernel(target, place):
-    heading = lax.broadcasted_iota(jnp.int32, (B, CHUNK), 0)
-    a = lax.broadcasted_iota(jnp.int32, (CHUNK, CHUNK), 0)
-    b = lax.broadcasted_iota(jnp.int32, (CHUNK, CHUNK), 1)
-    upper = jnp.where(a <= b, 1.0, 0.0).astype(BF16)
-    before = jnp.zeros((B, 1), F32)
-    for n in range(PD // CHUNK):
-        part = slice(n * CHUNK, (n + 1) * CHUNK)
-        chosen = heading == target[:, part]
-        rank = jnp.dot(jnp.where(chosen, 1.0, 0.0).astype(BF16), upper, preferred_element_type=F32) + before
-        before = rank[:, CHUNK - 1 :]
-        leaves = chosen & (heading < 4)
-        value = jnp.where(leaves, rank + heading.astype(F32) * float(CAP), 0.0)
-        place[:, part] = jnp.sum(value, axis=0, keepdims=True).astype(jnp.int32) - 1
-
-
-def droplet_kernel(gas, motion, size, cell, target, place, on, when, head, _, sources, parcels, kept):
+def counting(rows):
+    return lax.broadcasted_iota(jnp.int32, (rows, CHUNK), 0).astype(F32).astype(BF16)
+
+
+def exact(numbers):
+    return numbers.astype(F32).astype(BF16)
+
+
+def one_hot(counted, numbers):
+    return jnp.where(counted == exact(numbers), jnp.ones((), BF16), jnp.zeros((), BF16))
+
+
+def renew_kernel(gas, motion, size, cell, target, kept, rows, parcels, places):
     table = jnp.concatenate([gas[f].reshape(B * B, NZ) for f in range(4)], axis=0)
     high, low = split(table)
     table = jnp.concatenate([high.astype(BF16), low.astype(BF16)], axis=1)
-    at_z = lax.broadcasted_iota(jnp.int32, (NZ, CHUNK), 0)
+    at_z = counting(NZ)
     at_xy = lax.broadcasted_iota(jnp.int32, (B * B, CHUNK), 0)
+    heading = lax.broadcasted_iota(jnp.int32, (B, NZ), 0)
+    blocks = [heading == target[:, n * NZ : (n + 1) * NZ] for n in range(PD // NZ)]
+    a = lax.broadcasted_iota(jnp.int32, (NZ, NZ), 0)
+    b = lax.broadcasted_iota(jnp.int32, (NZ, NZ), 1)
+    upper = jnp.where(a <= b, 1.0, 0.0).astype(BF16)
+    marks = jnp.concatenate([jnp.where(chosen, 1.0, 0.0) for chosen in blocks], axis=0).astype(BF16)
+    ranks = jnp.dot(marks, upper, preferred_element_type=F32)
+    before = jnp.zeros((B, 1), F32)
+    for n, chosen in enumerate(blocks):
+        rank = ranks[B * n : B * n + B] + before
+        before = rank[:, NZ - 1 :]
+        place = jnp.where(chosen & (heading < 4), rank + heading.astype(F32) * float(CAP), 0.0)
+        places[:, n * NZ : (n + 1) * NZ] = jnp.sum(place, axis=0, keepdims=True).astype(jnp.int32) - 1
+    moved = jnp.zeros((10 * B, NZ), F32)
     at_high = lax.broadcasted_iota(jnp.int32, (B, CHUNK), 0)
-    total = jnp.zeros((4 * B * B, NZ), F32)
-    moved = jnp.zeros((10 * B, NZ), F32)
     across = (((1,), (1,)), ((), ()))
     for n in range(PD // CHUNK):
         part = slice(n * CHUNK, (n + 1) * CHUNK)
         cells = cell[:, part]
         goal = target[:, part]
-        in_z = jnp.where(at_z == (cells & (NZ - 1)), 1.0, 0.0).astype(BF16)
+        in_z = one_hot(at_z, cells & (NZ - 1))
         in_xy = at_xy == (cells >> 8)
         found = jnp.dot(table, jnp.concatenate([in_z, in_z], axis=0), preferred_element_type=F32)
         local = [
@@ -128,17 +136,39 @@
         alive = goal >= 0
         for f in range(5):
             kept[f, :, part] = jnp.where(goal == 4, renewed[f], 0.0)
-        pieces = [*split(jnp.where(alive, drag, 0.0)), *split(jnp.where(alive, vapour, 0.0))]
-        given = jnp.concatenate([jnp.where(in_xy, piece, 0.0).astype(BF16) for piece in pieces], axis=0)
-        total = total + lax.dot_general(given, in_z, across, preferred_element_type=F32)
-        spot = place[:, part]
-        in_low = jnp.where(at_z == (spot & (NZ - 1)), 1.0, 0.0).astype(BF16)
-        in_high = at_high == (spot >> 8)
+        rows[0:1, part] = jnp.where(alive, drag, 0.0)
+        rows[1:2, part] = jnp.where(alive, vapour, 0.0)
+        place = places[:, part]
+        in_low = one_hot(at_z, place & (NZ - 1))
+        in_high = at_high == (place >> 8)
         split_up = [split(value) for value in renewed]
         leaving = [jnp.where(in_high, split_up[f][piece], 0.0) for piece in range(2) for f in range(5)]
         moved = moved + lax.dot_general(
             jnp.concatenate(leaving, axis=0).astype(BF16), in_low, across, preferred_element_type=F32
         )
+    moved = moved[: 5 * B] + moved[5 * B :]
+    for d in range(4):
+        for f in range(5):
+            for half in range(2):
+                at = f * B + 2 * d + half
+                r = 2 * f + half
+                parcels[d, r // B, r % B : r % B + 1, :] = moved[at : at + 1]
+        parcels[d, 1, 2:, :] = jnp.zeros((B - 2, NZ), F32)
+
+
+def spread_kernel(rows, cell, on, when, head, _, sources):
+    at_z = counting(NZ)
+    at_xy = counting(B * B)
+    total = jnp.zeros((4 * B * B, NZ), F32)
+    across = (((1,), (1,)), ((), ()))
+    for n in range(PD // CHUNK):
+        part = slice(n * CHUNK, (n + 1) * CHUNK)
+        cells = cell[:, part]
+        in_z = one_hot(at_z, cells & (NZ - 1))
+        in_xy = at_xy == exact(cells >> 8)
+        pieces = [*split(rows[0:1, part]), *split(rows[1:2, part])]
+        given = jnp.concatenate([jnp.where(in_xy, piece.astype(BF16), jnp.zeros((), BF16)) for piece in pieces], axis=0)
+        total = total + lax.dot_general(given, in_z, across, preferred_element_type=F32)
     q = B * B
     steam = total[2 * q : 3 * q] + total[3 * q :]
     sources[0] = total[:q] + total[q : 2 * q]
@@ -153,14 +183,6 @@
         taken = jnp.where(lanes == (where & (NZ - 1)), strength, 0.0)
         for f in range(2):
             sources[f, row, :] = sources[f, row, :] - taken
-    moved = moved[: 5 * B] + moved[5 * B :]
-    for d in range(4):
-        for f in range(5):
-            for half in range(2):
-                at = f * B + 2 * d + half
-                r = 2 * f + half
-                parcels[d, r // B, r % B : r % B + 1, :] = moved[at : at + 1]
-        parcels[d, 1, 2:, :] = jnp.zeros((B - 2, NZ), F32)
 
 
 def pack_x_kernel(gas, guess, y_odd, y_even, _, even, odd):
@@ -487,15 +509,17 @@
     y_even, y_odd = call(pack_y_kernel, [tiles(NL)] * 2, 3, 10**6)(first, gas, guess)
     y_odd = swap(y_odd, "gy", 1)
     y_even = swap(y_even, "gy", 0)
-    [place] = call(place_kernel, [shape((1, PD), jnp.int32)], 1, 10**9)(target)
-    x_even, x_odd = call(pack_x_kernel, [tiles(NL + 1)] * 2, 5, 10**6)(gas, guess, y_odd, y_even, place)
-    sources, parcels, kept = call(
-        droplet_kernel,
-        [shape((3, B * B, NZ), F32), shape((4, 2, B, NZ), F32), shape((5, 1, PD), F32)],
-        10,
-        2 * 10**9,
-        smem=(6, 7, 8),
-    )(gas, motion, size, cell, target, place, on, when, head, x_even)
+    kept, rows, parcels = call(
+        renew_kernel,
+        [shape((5, 1, PD), F32), shape((2, PD), F32), shape((4, 2, B, NZ), F32)],
+        5,
+        10**9,
+        scratch=[pltpu.VMEM((1, PD), jnp.int32)],
+    )(gas, motion, size, cell, target)
+    x_even, x_odd = call(pack_x_kernel, [tiles(NL + 1)] * 2, 5, 10**6)(gas, guess, y_odd, y_even, rows)
+    [sources] = call(spread_kernel, [shape((3, B * B, NZ), F32)], 6, 10**9, smem=(2, 3, 4))(
+        rows, cell, on, when, head, x_even
+    )
     sources = sources.reshape(3, B, B, NZ)
     x_odd = swap(x_odd, "gx", 1)
     x_even = swap(x_even, "gx", 0)

time: 55.8 us -> 53.2 us (0.953)
  waiting for transfers between devices: 12.4 us -> 9.91 us
  Pallas kernels: 9.1 us -> 8.13 us
  starting transfers between devices: 32.1 us -> 33 us
    ppermute x8, waiting for transfers between devices: 12.4 us -> 9.91 us  [swap(): return lax.ppermute(shard, axis, pairs)]
    pallas_call x2, Pallas kernels: 5.12 us -> 4.14 us  [the longest x1 2.81 us: body(): call(renew_kernel, [shape((5, 1, PD), F32), shape((2, PD), F32), shape((4...]
    ppermute x8, starting transfers between devices: 32.1 us -> 33 us  [swap(): return lax.ppermute(shard, axis, pairs)]
  transfers between devices with their start and end apart: 8 -> 8, of which waited for: 3 -> 3; matrix products, arithmetic and copies ran while one was open for 0% -> 0% of each run, Pallas kernels for 10% -> 8%
where the time goes in v6:
time: 53.2 us; the launch traced here: 52.9 us
  starting transfers between devices  33 us (62%)
  waiting for transfers between devices  9.91 us (19%)
  Pallas kernels  8.13 us (15%)
  local copies, waits for them, and re-layouts  0.99 us (2%)
  between operations  0.87 us (2%)
    ppermute x8, starting transfers between devices, swap(): return lax.ppermute(shard, axis, pairs)  33 us
    ppermute x8, waiting for transfers between devices, swap(): return lax.ppermute(shard, axis, pairs)  9.91 us
    pallas_call x1, Pallas kernels, body(): call(renew_kernel, [shape((5, 1, PD), F32), shape((2, PD), F32), shape((4...  2.81 us
    pallas_call x1, Pallas kernels, body(): call(finish_kernel, [shape((5, B, B, NZ), F32), shape((B, B, NZ), F32), s...  1.89 us
    pallas_call x1, Pallas kernels, body(): call(spread_kernel, [shape((3, B * B, NZ), F32)], 6, 10 ** 9, smem=(2, 3,...  1.32 us
  transfers between devices with their start and end apart: 8, of which 3 were waited for; matrix products, arithmetic and copies ran while one was open for 0% of the time, Pallas kernels for 8%

profile of v6, /device:TPU:48, one launch (start us, length us, event | category | flops | bytes accessed | tf_op | source)
XLA Modules:
  0.0 52.9 jit_solution(6625547115715350601)
XLA Ops:
  0.7 0.9 %copy-done = f32[5,8,8,256]{3,2,1,0:T(8,128)S(1)} copy-done((f32[5,8,8,256]{3,2,1,0:T(8,128)S(1)}, f32[5,8,8,256]{3,2,1,0:T(8,128)}, u32[]{:S(2)}) %copy-start) | copy-done | bytes 327704
  1.6 0.0 copy-done.1
  1.6 0.0 copy-start.5
  1.6 0.1 shard_map.121
  1.7 0.7 %collective-permute-start = (f32[12,8,256]{2,1,0:T(8,128)S(1)}, f32[12,8,256]{2,1,0:T(8,128)S(1)}, u32[]{:S(2)}, u32[]{:S(2)}) collective-permute-start(f32[12,8,256]{2,1,0:T(8,128)S(1)} %get-tuple-element.21), channel_id=1, source_target_pairs={{1,2},{2,1},{3,4},{4,3},{5,6},{6,5},{9,10},{10,9},{11,12},{12,11},... | collective-permute-start | bytes 294920 | tf_op jit(solution)/shard_map/ppermute | solution.py:58
  2.4 6.1 %collective-permute-start.1 = (f32[12,8,256]{2,1,0:T(8,128)S(1)}, f32[12,8,256]{2,1,0:T(8,128)S(1)}, u32[]{:S(2)}, u32[]{:S(2)}) collective-permute-start(f32[12,8,256]{2,1,0:T(8,128)S(1)} %get-tuple-element.22), channel_id=1, source_target_pairs={{0,1},{1,0},{2,3},{3,2},{4,5},{5,4},{6,7},{7,6},{8,9},{9,8},{10,11... | collective-permute-start | bytes 294920 | tf_op jit(solution)/shard_map/ppermute | solution.py:58
  8.5 2.8 %shard_map.122 = (f32[5,1,4096]{2,1,0:T(1,128)}, f32[2,4096]{1,0:T(2,128)S(1)}, f32[4,2,8,256]{3,2,1,0:T(8,128)S(1)}) custom-call(f32[5,8,8,256]{3,2,1,0:T(8,128)S(1)} %copy-done, f32[4,1,4096]{2,1,0:T(1,128)S(1)} %copy-done.2, f32[1,4096]{1,0:T(1,128)S(1)} %copy-done.3, s32[1,4096]{1,0:T(1,128)S(1)} %copy-done.5, s32[1,4096]{1,0:T(1,128)S(1)} %copy-done.4), custom_call_target="tpu_custom_call" | custom-call | flops 1000000000 | bytes 125000000 | tf_op jit(solution)/shard_map/pallas_call | solution.py:512
  11.4 0.0 collective-permute-done.y_odd
  11.4 0.0 collective-permute-done.1.y_even
  11.4 0.0 copy-start.6
  11.4 0.0 copy-start.7
  11.4 0.0 copy-start.8
  11.4 11.5 %collective-permute-start.2 = (f32[13,8,256]{2,1,0:T(8,128)S(1)}, f32[13,8,256]{2,1,0:T(8,128)S(1)}, u32[]{:S(2)}, u32[]{:S(2)}) collective-permute-start(f32[13,8,256]{2,1,0:T(8,128)S(1)} %get-tuple-element.24), channel_id=1, source_target_pairs={{8,16},{16,8},{24,32},{32,24},{40,48},{48,40},{56,64},{64,56},{72,... | collective-permute-start | bytes 319496 | tf_op jit(solution)/shard_map/ppermute | solution.py:58
  23.0 1.9 %collective-permute-start.3 = (f32[13,8,256]{2,1,0:T(8,128)S(1)}, f32[13,8,256]{2,1,0:T(8,128)S(1)}, u32[]{:S(2)}, u32[]{:S(2)}) collective-permute-start(f32[13,8,256]{2,1,0:T(8,128)S(1)} %get-tuple-element.25._), channel_id=1, source_target_pairs={{0,8},{8,0},{16,24},{24,16},{32,40},{40,32},{48,56},{56,48},{64,72... | collective-permute-start | bytes 319496 | tf_op jit(solution)/shard_map/ppermute | solution.py:58
  24.9 0.0 copy-done.6
  24.9 0.0 copy-done.7
  24.9 0.0 copy-done.8
  24.9 1.3 %shard_map.124 = f32[3,64,256]{2,1,0:T(8,128)S(1)} custom-call(f32[2,4096]{1,0:T(2,128)S(1)} %get-tuple-element.23._.rows, s32[1,4096]{1,0:T(1,128)S(1)} %copy-done.5, s32[1,8]{1,0:T(1,128)S(1)} %copy-done.6, s32[1,8]{1,0:T(1,128)S(1)} %copy-done.7, s32[1,8]{1,0:T(1,128)S(1)} %copy-done.8, f32[13,8,256]{2,1,0:T(8,128)S(1)} %get-tuple-element.25._), custom_call_target="tpu_custom_call" | custom-call | flops 1000000000 | bytes 125000000 | tf_op jit(solution)/shard_map/pallas_call | solution.py:520
  26.3 0.1 collective-permute-done.2.x_odd
  26.3 0.0 collective-permute-done.3.x_even
  26.3 0.9 %shard_map.125 = (f32[3,8,8,256]{3,2,1,0:T(8,128)S(1)}, f32[18,8,256]{2,1,0:T(8,128)S(1)}, f32[18,8,256]{2,1,0:T(8,128)S(1)}) custom-call(f32[5,8,8,256]{3,2,1,0:T(8,128)S(1)} %copy-done, f32[8,8,256]{2,1,0:T(8,128)S(1)} %copy-done.1, f32[12,8,256]{2,1,0:T(8,128)S(1)} %collective-permute-done.y_odd, f32[12,8,256]{2,1,0:T(8,128)S(1)} %collective-permute-done.1.y_even, ...), custom_call_target="tpu_custom_call" | custom-call | flops 10000000 | bytes 1250000 | tf_op jit(solution)/shard_map/pallas_call | solution.py:527
  27.3 0.7 %collective-permute-start.4 = (f32[18,8,256]{2,1,0:T(8,128)S(1)}, f32[18,8,256]{2,1,0:T(8,128)S(1)}, u32[]{:S(2)}, u32[]{:S(2)}) collective-permute-start(f32[18,8,256]{2,1,0:T(8,128)S(1)} %get-tuple-element.28._), channel_id=1, source_target_pairs={{1,2},{2,1},{3,4},{4,3},{5,6},{6,5},{9,10},{10,9},{11,12},{12,11},... | collective-permute-start | bytes 442376 | tf_op jit(solution)/shard_map/ppermute | solution.py:58
  28.0 6.1 %collective-permute-start.5 = (f32[18,8,256]{2,1,0:T(8,128)S(1)}, f32[18,8,256]{2,1,0:T(8,128)S(1)}, u32[]{:S(2)}, u32[]{:S(2)}) collective-permute-start(f32[18,8,256]{2,1,0:T(8,128)S(1)} %get-tuple-element.29.own), channel_id=1, source_target_pairs={{0,1},{1,0},{2,3},{3,2},{4,5},{5,4},{6,7},{7,6},{8,9},{9,8},{10,11... | collective-permute-start | bytes 442376 | tf_op jit(solution)/shard_map/ppermute | solution.py:58
  34.1 0.0 collective-permute-done.4.y_odd
  34.1 5.4 %collective-permute-done.5.y_even = f32[18,8,256]{2,1,0:T(8,128)S(1)} collective-permute-done((f32[18,8,256]{2,1,0:T(8,128)S(1)}, f32[18,8,256]{2,1,0:T(8,128)S(1)}, u32[]{:S(2)}, u32[]{:S(2)}) %collective-permute-start.5) | collective-permute-done | bytes 147488 | tf_op jit(solution)/shard_map/ppermute | solution.py:58
  39.5 0.7 %shard_map.127 = (f32[17,8,256]{2,1,0:T(8,128)S(1)}, f32[17,8,256]{2,1,0:T(8,128)S(1)}, f32[8,24,256]{2,1,0:T(8,128)S(1)}, f32[8,24,256]{2,1,0:T(8,128)S(1)}) custom-call(f32[18,8,256]{2,1,0:T(8,128)S(1)} %get-tuple-element.29.own, f32[18,8,256]{2,1,0:T(8,128)S(1)} %collective-permute-done.4.y_odd, f32[18,8,256]{2,1,0:T(8,128)S(1)} %collective-permute-done.5.y_even, ...), custom_call_target="tpu_custom_call" | custom-call | flops 10000000 | bytes 1250000 | tf_op jit(solution)/shard_map/pallas_call | solution.py:546
  40.2 4.1 %collective-permute-start.6 = (f32[17,8,256]{2,1,0:T(8,128)S(1)}, f32[17,8,256]{2,1,0:T(8,128)S(1)}, u32[]{:S(2)}, u32[]{:S(2)}) collective-permute-start(f32[17,8,256]{2,1,0:T(8,128)S(1)} %get-tuple-element.32), channel_id=1, source_target_pairs={{8,16},{16,8},{24,32},{32,24},{40,48},{48,40},{56,64},{64,56},{72,... | collective-permute-start | bytes 417800 | tf_op jit(solution)/shard_map/ppermute | solution.py:58
  44.3 1.9 %collective-permute-start.7 = (f32[17,8,256]{2,1,0:T(8,128)S(1)}, f32[17,8,256]{2,1,0:T(8,128)S(1)}, u32[]{:S(2)}, u32[]{:S(2)}) collective-permute-start(f32[17,8,256]{2,1,0:T(8,128)S(1)} %get-tuple-element.33), channel_id=1, source_target_pairs={{0,8},{8,0},{16,24},{24,16},{32,40},{40,32},{48,56},{56,48},{64,72... | collective-permute-start | bytes 417800 | tf_op jit(solution)/shard_map/ppermute | solution.py:58
  46.2 0.3 shard_map.126.star_rest
  46.6 4.4 %collective-permute-done.6.x_odd = f32[17,8,256]{2,1,0:T(8,128)S(1)} collective-permute-done((f32[17,8,256]{2,1,0:T(8,128)S(1)}, f32[17,8,256]{2,1,0:T(8,128)S(1)}, u32[]{:S(2)}, u32[]{:S(2)}) %collective-permute-start.6) | collective-permute-done | bytes 139296 | tf_op jit(solution)/shard_map/ppermute | solution.py:58
  51.0 0.0 collective-permute-done.7.x_even
  51.0 1.9 %shard_map.128 = (f32[5,8,8,256]{3,2,1,0:T(8,128)}, f32[8,8,256]{2,1,0:T(8,128)}, f32[4,5,1,512]{3,2,1,0:T(1,128)}) custom-call(f32[3,8,8,256]{3,2,1,0:T(8,128)S(1)} %get-tuple-element.27.star, f32[2,8,8,256]{3,2,1,0:T(8,128)S(1)} %shard_map.126.star_rest, f32[8,24,256]{2,1,0:T(8,128)S(1)} %get-tuple-element.30.first, ...), custom_call_target="tpu_custom_call" | custom-call | flops 10000000 | bytes 1250000 | tf_op jit(solution)/shard_map/pallas_call | solution.py:556
  (11 shorter events, 0.1 us)
Async XLA Ops:
  0.6 1.0 %copy-start = (f32[5,8,8,256]{3,2,1,0:T(8,128)S(1)}, f32[5,8,8,256]{3,2,1,0:T(8,128)}, u32[]{:S(2)}) copy-start(f32[5,8,8,256]{3,2,1,0:T(8,128)} %gas.9) | copy-start | bytes 983044
  0.6 1.0 %copy-start.1 = (f32[8,8,256]{2,1,0:T(8,128)S(1)}, f32[8,8,256]{2,1,0:T(8,128)}, u32[]{:S(2)}) copy-start(f32[8,8,256]{2,1,0:T(8,128)} %guess.5) | copy-start | bytes 196612
  1.6 6.9 %copy-start.2 = (f32[4,1,4096]{2,1,0:T(1,128)S(1)}, f32[4,1,4096]{2,1,0:T(1,128)}, u32[]{:S(2)}) copy-start(f32[4,1,4096]{2,1,0:T(1,128)} %motion.1) | copy-start | bytes 196612
  1.6 6.9 %copy-start.3 = (f32[1,4096]{1,0:T(1,128)S(1)}, f32[1,4096]{1,0:T(1,128)}, u32[]{:S(2)}) copy-start(f32[1,4096]{1,0:T(1,128)} %size.1) | copy-start | bytes 49156
  1.6 6.9 %copy-start.4 = (s32[1,4096]{1,0:T(1,128)S(1)}, s32[1,4096]{1,0:T(1,128)}, u32[]{:S(2)}) copy-start(s32[1,4096]{1,0:T(1,128)} %target.1) | copy-start | bytes 49156
  1.6 6.9 %copy-start.5 = (s32[1,4096]{1,0:T(1,128)S(1)}, s32[1,4096]{1,0:T(1,128)}, u32[]{:S(2)}) copy-start(s32[1,4096]{1,0:T(1,128)} %cell.3) | copy-start | bytes 49156
  1.7 9.6 %collective-permute-start = (f32[12,8,256]{2,1,0:T(8,128)S(1)}, f32[12,8,256]{2,1,0:T(8,128)S(1)}, u32[]{:S(2)}, u32[]{:S(2)}) collective-permute-start(f32[12,8,256]{2,1,0:T(8,128)S(1)} %get-tuple-element.21), channel_id=1, source_target_pairs={{1,2},{2,1},{3,4},{4,3},{5,6},{6,5},{9,10},{10,9},{11,12},{12,11},... | collective-permute-start | bytes 294920 | tf_op jit(solution)/shard_map/ppermute | solution.py:58
  2.4 9.0 %collective-permute-start.1 = (f32[12,8,256]{2,1,0:T(8,128)S(1)}, f32[12,8,256]{2,1,0:T(8,128)S(1)}, u32[]{:S(2)}, u32[]{:S(2)}) collective-permute-start(f32[12,8,256]{2,1,0:T(8,128)S(1)} %get-tuple-element.22), channel_id=1, source_target_pairs={{0,1},{1,0},{2,3},{3,2},{4,5},{5,4},{6,7},{7,6},{8,9},{9,8},{10,11... | collective-permute-start | bytes 294920 | tf_op jit(solution)/shard_map/ppermute | solution.py:58
  11.4 13.5 %copy-start.6 = (s32[1,8]{1,0:T(1,128)S(1)}, s32[1,8]{1,0:T(1,128)}, u32[]{:S(2)}) copy-start(s32[1,8]{1,0:T(1,128)} %on.1) | copy-start | bytes 100
  11.4 13.5 %copy-start.7 = (s32[1,8]{1,0:T(1,128)S(1)}, s32[1,8]{1,0:T(1,128)}, u32[]{:S(2)}) copy-start(s32[1,8]{1,0:T(1,128)} %when.1) | copy-start | bytes 100
  11.4 13.5 %copy-start.8 = (s32[1,8]{1,0:T(1,128)S(1)}, s32[1,8]{1,0:T(1,128)}, u32[]{:S(2)}) copy-start(s32[1,8]{1,0:T(1,128)} %head.1) | copy-start | bytes 100
  11.4 14.9 %collective-permute-start.2 = (f32[13,8,256]{2,1,0:T(8,128)S(1)}, f32[13,8,256]{2,1,0:T(8,128)S(1)}, u32[]{:S(2)}, u32[]{:S(2)}) collective-permute-start(f32[13,8,256]{2,1,0:T(8,128)S(1)} %get-tuple-element.24), channel_id=1, source_target_pairs={{8,16},{16,8},{24,32},{32,24},{40,48},{48,40},{56,64},{64,56},{72,... | collective-permute-start | bytes 319496 | tf_op jit(solution)/shard_map/ppermute | solution.py:58
  23.0 3.3 %collective-permute-start.3 = (f32[13,8,256]{2,1,0:T(8,128)S(1)}, f32[13,8,256]{2,1,0:T(8,128)S(1)}, u32[]{:S(2)}, u32[]{:S(2)}) collective-permute-start(f32[13,8,256]{2,1,0:T(8,128)S(1)} %get-tuple-element.25._), channel_id=1, source_target_pairs={{0,8},{8,0},{16,24},{24,16},{32,40},{40,32},{48,56},{56,48},{64,72... | collective-permute-start | bytes 319496 | tf_op jit(solution)/shard_map/ppermute | solution.py:58
  27.3 6.8 %collective-permute-start.4 = (f32[18,8,256]{2,1,0:T(8,128)S(1)}, f32[18,8,256]{2,1,0:T(8,128)S(1)}, u32[]{:S(2)}, u32[]{:S(2)}) collective-permute-start(f32[18,8,256]{2,1,0:T(8,128)S(1)} %get-tuple-element.28._), channel_id=1, source_target_pairs={{1,2},{2,1},{3,4},{4,3},{5,6},{6,5},{9,10},{10,9},{11,12},{12,11},... | collective-permute-start | bytes 442376 | tf_op jit(solution)/shard_map/ppermute | solution.py:58
  28.0 11.5 %collective-permute-start.5 = (f32[18,8,256]{2,1,0:T(8,128)S(1)}, f32[18,8,256]{2,1,0:T(8,128)S(1)}, u32[]{:S(2)}, u32[]{:S(2)}) collective-permute-start(f32[18,8,256]{2,1,0:T(8,128)S(1)} %get-tuple-element.29.own), channel_id=1, source_target_pairs={{0,1},{1,0},{2,3},{3,2},{4,5},{5,4},{6,7},{7,6},{8,9},{9,8},{10,11... | collective-permute-start | bytes 442376 | tf_op jit(solution)/shard_map/ppermute | solution.py:58
  40.2 10.8 %collective-permute-start.6 = (f32[17,8,256]{2,1,0:T(8,128)S(1)}, f32[17,8,256]{2,1,0:T(8,128)S(1)}, u32[]{:S(2)}, u32[]{:S(2)}) collective-permute-start(f32[17,8,256]{2,1,0:T(8,128)S(1)} %get-tuple-element.32), channel_id=1, source_target_pairs={{8,16},{16,8},{24,32},{32,24},{40,48},{48,40},{56,64},{64,56},{72,... | collective-permute-start | bytes 417800 | tf_op jit(solution)/shard_map/ppermute | solution.py:58
  44.3 6.7 %collective-permute-start.7 = (f32[17,8,256]{2,1,0:T(8,128)S(1)}, f32[17,8,256]{2,1,0:T(8,128)S(1)}, u32[]{:S(2)}, u32[]{:S(2)}) collective-permute-start(f32[17,8,256]{2,1,0:T(8,128)S(1)} %get-tuple-element.33), channel_id=1, source_target_pairs={{0,8},{8,0},{16,24},{24,16},{32,40},{40,32},{48,56},{56,48},{64,72... | collective-permute-start | bytes 417800 | tf_op jit(solution)/shard_map/ppermute | solution.py:58

commit v7 on v6

--- a/solution.py
+++ b/solution.py
@@ -185,9 +185,11 @@
             sources[f, row, :] = sources[f, row, :] - taken
 
 
-def pack_x_kernel(gas, guess, y_odd, y_even, _, even, odd):
+def pack_x_kernel(gas, guess, y_odd, y_even, parcels, even, odd):
     def planes(low, high):
-        for side, near, step in ((low, 0, 1), (high, B - 1, -1)):
+        for side, near, step, heading in ((low, 0, 1, 1), (high, B - 1, -1, 0)):
+            side[NL + 1] = parcels[heading, 0]
+            side[NL + 2] = parcels[heading, 1]
             for r, (field, depth) in enumerate(X_LAYERS):
                 x = near + step * depth
                 side[r] = guess[x] if field == 5 else gas[field, x]
@@ -381,7 +383,7 @@
     return out
 
 
-def slab_kernel(own, y_odd, y_even, parcels, even, odd, first, source, f0, f1, low, high):
+def slab_kernel(own, y_odd, y_even, even, odd, first, source, f2, f3, f4, f5, f6, low, high):
     gy = lax.axis_index("gy")
     scale = weights((), (gy > 0, None, gy < lax.axis_size("gy") - 1))
     row = lax.broadcasted_iota(jnp.int32, (B, HALF), 0)
@@ -407,23 +409,20 @@
 
     for side, x in ((low, 0), (high, B - 1)):
         keep(side, 1, load(first, x))
-    now, later = first, f0
+    levels = {1: first, 2: f2, 3: f3, 4: f4, 5: f5, 6: f6, 7: f5}
     for k in range(2, 9):
         depth = 9 - k
+        now = levels[k - 1]
         for x in range(B):
             if depth <= x < B - depth:
                 continue
             others = [load(now, y) for y in (x - 1, x + 1) if 0 <= y < B]
             plane = relax(load(now, x), others, load(source, x), scale)
             if k < 8:
-                store(later, plane, x)
+                store(levels[k], plane, x)
             for side, face in ((low, 0), (high, B - 1)):
                 if x == face:
                     keep(side, k, plane)
-        now, later = (f0, f1) if k == 2 else (later, now)
-    for side, heading in ((low, 1), (high, 0)):
-        side[NH] = parcels[heading, 0]
-        side[NH + 1] = parcels[heading, 1]
 
     def send(low_out, high_out):
         low_out[...] = low[...]
@@ -432,7 +431,7 @@
     by_parity("gx", send, even, odd)
 
 
-def finish_kernel(star, star_rest, first, source, y_even, y_odd, x_odd, x_even, gas_next, pressure, arrived, o0, o1, r0, r1, hist):
+def finish_kernel(star, star_rest, first, source, f2, f3, f4, early_odd, early_even, y_even, y_odd, x_odd, x_even, gas_next, pressure, arrived, o0, o1, r0, r1, hist):
     gx = lax.axis_index("gx")
     gy = lax.axis_index("gy")
     flags_y = (gy > 0, None, gy < lax.axis_size("gy") - 1)
@@ -455,25 +454,41 @@
 
     by_parity("gy", take_y, y_even, y_odd)
     by_parity("gx", take_x, x_even, x_odd)
-    arrive(0, hist.at[0], NH)
-    arrive(1, hist.at[1], NH)
+
+    def take_early(left, right):
+        arrive(0, left, NL + 1)
+        arrive(1, right, NL + 1)
+
+    by_parity("gx", take_early, early_even, early_odd)
 
     def history(side, k):
         at = (B - 1 + k, k - 1, 2 * B - 1 - k)
         return [[hist[side, at[t], :, slice(HALF * h, HALF * h + HALF)] for h in range(2)] for t in range(3)]
 
-    owns = {1: first, **{k: (o0, o1)[k % 2] for k in range(2, 9)}}
+    slabs = {1: first, 2: f2, 3: f3, 4: f4}
+    owns = {k: (o0, o1)[k % 2] for k in range(2, 9)}
+
+    def alone(k, x):
+        return k in slabs and k - 1 <= x <= B - k
+
     responses = {k: (r0, r1)[k % 2] for k in range(2, 9)}
 
     def at(k, x):
         if 0 <= x < B:
-            return load(owns[k], x)
+            return load(slabs[k] if alone(k, x) else owns[k], x)
         side, depth = (0, -x) if x < 0 else (1, x - B + 1)
         return load(responses[k], side, depth - 1) if depth < k else None
 
     for k in range(2, 9):
         depth = min(k - 1, 9 - k)
         for x in range(-depth, B + depth):
+            if alone(k, x):
+                continue
+            if k == 2 and 0 <= x < B:
+                drive = history(0 if x == 0 else 1, 1)
+                drive = [[drive[t][h] * inner[t] for h in range(2)] for t in range(3)]
+                store(owns[k], add(load(f2, x), drive), x)
+                continue
             others = [at(k - 1, x - 1), at(k - 1, x + 1)]
             if 0 <= x < B:
                 if x == 0:
@@ -516,7 +531,7 @@
         10**9,
         scratch=[pltpu.VMEM((1, PD), jnp.int32)],
     )(gas, motion, size, cell, target)
-    x_even, x_odd = call(pack_x_kernel, [tiles(NL + 1)] * 2, 5, 10**6)(gas, guess, y_odd, y_even, rows)
+    x_even, x_odd = call(pack_x_kernel, [tiles(NL + 3)] * 2, 5, 10**6)(gas, guess, y_odd, y_even, parcels)
     [sources] = call(spread_kernel, [shape((3, B * B, NZ), F32)], 6, 10**9, smem=(2, 3, 4))(
         rows, cell, on, when, head, x_even
     )
@@ -543,23 +558,24 @@
     y_even = swap(ps_even, "gy", 0)
     slab = shape((B, 3 * B, NZ), F32)
     scratch = pltpu.VMEM((B, 3 * B, NZ), F32)
-    x_even, x_odd, first, source = call(
+    early_odd, early_even = x_odd, x_even
+    x_even, x_odd, *slabs = call(
         slab_kernel,
-        [tiles(NH + 2), tiles(NH + 2), slab, slab],
-        4,
+        [tiles(NH), tiles(NH)] + [slab] * 5,
+        3,
         10**7,
-        scratch=[scratch, scratch, pltpu.VMEM((NH + 2, B, NZ), F32), pltpu.VMEM((NH + 2, B, NZ), F32)],
-    )(ps_even, y_odd, y_even, parcels)
+        scratch=[scratch, scratch, pltpu.VMEM((NH, B, NZ), F32), pltpu.VMEM((NH, B, NZ), F32)],
+    )(ps_even, y_odd, y_even)
     x_odd = swap(x_odd, "gx", 1)
     x_even = swap(x_even, "gx", 0)
     response = pltpu.VMEM((2, 4, 3 * B, NZ), F32)
     gas_next, pressure, arrived = call(
         finish_kernel,
         [shape((5, B, B, NZ), F32), shape((B, B, NZ), F32), shape((4, 5, 1, CAP), F32)],
-        8,
+        13,
         10**7,
-        scratch=[scratch, scratch, response, response, pltpu.VMEM((2, NH + 2, B, NZ), F32)],
-    )(star, star_rest, first, source, y_even, y_odd, x_odd, x_even)
+        scratch=[scratch, scratch, response, response, pltpu.VMEM((2, NH, B, NZ), F32)],
+    )(star, star_rest, *slabs, early_odd, early_even, y_even, y_odd, x_odd, x_even)
     return gas_next, pressure, kept, arrived
 
 

time: 53.2 us -> 52.8 us (level)
  transfers between devices with their start and end apart: 8 -> 8, of which waited for: 3 -> 3; matrix products, arithmetic and copies ran while one was open for 0% -> 0% of each run, Pallas kernels for 8% -> 9%
where the time goes in v7:
time: 52.8 us; the launch traced here: 52.5 us
  starting transfers between devices  33 us (62%)
  waiting for transfers between devices  9.62 us (18%)
  Pallas kernels  7.99 us (15%)
  local copies, waits for them, and re-layouts  0.99 us (2%)
  between operations  0.87 us (2%)
    ppermute x8, starting transfers between devices, swap(): return lax.ppermute(shard, axis, pairs)  33 us
    ppermute x8, waiting for transfers between devices, swap(): return lax.ppermute(shard, axis, pairs)  9.62 us
    pallas_call x1, Pallas kernels, body(): call(renew_kernel, [shape((5, 1, PD), F32), shape((2, PD), F32), shape((4...  2.81 us
    pallas_call x1, Pallas kernels, body(): call(finish_kernel, [shape((5, B, B, NZ), F32), shape((B, B, NZ), F32), s...  1.73 us
    pallas_call x1, Pallas kernels, body(): call(spread_kernel, [shape((3, B * B, NZ), F32)], 6, 10 ** 9, smem=(2, 3,...  1.34 us
  transfers between devices with their start and end apart: 8, of which 3 were waited for; matrix products, arithmetic and copies ran while one was open for 0% of the time, Pallas kernels for 9%

profile of v7, /device:TPU:48, one launch (start us, length us, event | category | flops | bytes accessed | tf_op | source)
XLA Modules:
  0.0 52.5 jit_solution(4857801651899175810)
XLA Ops:
  0.6 0.0 copy-start
  0.6 0.0 copy-start.1
  0.7 0.9 %copy-done = f32[5,8,8,256]{3,2,1,0:T(8,128)S(1)} copy-done((f32[5,8,8,256]{3,2,1,0:T(8,128)S(1)}, f32[5,8,8,256]{3,2,1,0:T(8,128)}, u32[]{:S(2)}) %copy-start) | copy-done | bytes 327704
  1.6 0.0 copy-done.1
  1.6 0.0 copy-start.5
  1.6 0.1 shard_map.121
  1.7 0.7 %collective-permute-start = (f32[12,8,256]{2,1,0:T(8,128)S(1)}, f32[12,8,256]{2,1,0:T(8,128)S(1)}, u32[]{:S(2)}, u32[]{:S(2)}) collective-permute-start(f32[12,8,256]{2,1,0:T(8,128)S(1)} %get-tuple-element.24), channel_id=1, source_target_pairs={{1,2},{2,1},{3,4},{4,3},{5,6},{6,5},{9,10},{10,9},{11,12},{12,11},... | collective-permute-start | bytes 294920 | tf_op jit(solution)/shard_map/ppermute | solution.py:58
  2.4 6.1 %collective-permute-start.1 = (f32[12,8,256]{2,1,0:T(8,128)S(1)}, f32[12,8,256]{2,1,0:T(8,128)S(1)}, u32[]{:S(2)}, u32[]{:S(2)}) collective-permute-start(f32[12,8,256]{2,1,0:T(8,128)S(1)} %get-tuple-element.25), channel_id=1, source_target_pairs={{0,1},{1,0},{2,3},{3,2},{4,5},{5,4},{6,7},{7,6},{8,9},{9,8},{10,11... | collective-permute-start | bytes 294920 | tf_op jit(solution)/shard_map/ppermute | solution.py:58
  8.5 0.0 copy-done.2
  8.5 2.8 %shard_map.122 = (f32[5,1,4096]{2,1,0:T(1,128)}, f32[2,4096]{1,0:T(2,128)S(1)}, f32[4,2,8,256]{3,2,1,0:T(8,128)S(1)}) custom-call(f32[5,8,8,256]{3,2,1,0:T(8,128)S(1)} %copy-done, f32[4,1,4096]{2,1,0:T(1,128)S(1)} %copy-done.2, f32[1,4096]{1,0:T(1,128)S(1)} %copy-done.3, s32[1,4096]{1,0:T(1,128)S(1)} %copy-done.5, s32[1,4096]{1,0:T(1,128)S(1)} %copy-done.4), custom_call_target="tpu_custom_call" | custom-call | flops 1000000000 | bytes 125000000 | tf_op jit(solution)/shard_map/pallas_call | solution.py:527
  11.4 0.0 collective-permute-done.y_odd
  11.4 0.0 collective-permute-done.1.y_even
  11.4 11.4 %collective-permute-start.2 = (f32[15,8,256]{2,1,0:T(8,128)S(1)}, f32[15,8,256]{2,1,0:T(8,128)S(1)}, u32[]{:S(2)}, u32[]{:S(2)}) collective-permute-start(f32[15,8,256]{2,1,0:T(8,128)S(1)} %get-tuple-element.27), channel_id=1, source_target_pairs={{8,16},{16,8},{24,32},{32,24},{40,48},{48,40},{56,64},{64,56},{72,... | collective-permute-start | bytes 368648 | tf_op jit(solution)/shard_map/ppermute | solution.py:58
  22.8 0.0 copy-start.6
  22.8 0.0 copy-start.7
  22.8 0.0 copy-start.8
  22.8 2.1 %collective-permute-start.3 = (f32[15,8,256]{2,1,0:T(8,128)S(1)}, f32[15,8,256]{2,1,0:T(8,128)S(1)}, u32[]{:S(2)}, u32[]{:S(2)}) collective-permute-start(f32[15,8,256]{2,1,0:T(8,128)S(1)} %get-tuple-element.28._), channel_id=1, source_target_pairs={{0,8},{8,0},{16,24},{24,16},{32,40},{40,32},{48,56},{56,48},{64,72... | collective-permute-start | bytes 368648 | tf_op jit(solution)/shard_map/ppermute | solution.py:58
  24.9 1.3 %shard_map.124 = f32[3,64,256]{2,1,0:T(8,128)S(1)} custom-call(f32[2,4096]{1,0:T(2,128)S(1)} %get-tuple-element.29.rows, s32[1,4096]{1,0:T(1,128)S(1)} %copy-done.5, s32[1,8]{1,0:T(1,128)S(1)} %copy-done.6, s32[1,8]{1,0:T(1,128)S(1)} %copy-done.7, s32[1,8]{1,0:T(1,128)S(1)} %copy-done.8, f32[15,8,256]{2,1,0:T(8,128)S(1)} %get-tuple-element.28._), custom_call_target="tpu_custom_call" | custom-call | flops 1000000000 | bytes 125000000 | tf_op jit(solution)/shard_map/pallas_call | solution.py:535
  26.3 0.2 collective-permute-done.2.x_odd.early_odd
  26.5 0.0 collective-permute-done.3.x_even.early_even
  26.5 0.9 %shard_map.125 = (f32[3,8,8,256]{3,2,1,0:T(8,128)S(1)}, f32[18,8,256]{2,1,0:T(8,128)S(1)}, f32[18,8,256]{2,1,0:T(8,128)S(1)}) custom-call(f32[5,8,8,256]{3,2,1,0:T(8,128)S(1)} %copy-done, f32[8,8,256]{2,1,0:T(8,128)S(1)} %copy-done.1, f32[12,8,256]{2,1,0:T(8,128)S(1)} %collective-permute-done.y_odd, f32[12,8,256]{2,1,0:T(8,128)S(1)} %collective-permute-done.1.y_even, ...), custom_call_target="tpu_custom_call" | custom-call | flops 10000000 | bytes 1250000 | tf_op jit(solution)/shard_map/pallas_call | solution.py:542
  27.5 0.7 %collective-permute-start.4 = (f32[18,8,256]{2,1,0:T(8,128)S(1)}, f32[18,8,256]{2,1,0:T(8,128)S(1)}, u32[]{:S(2)}, u32[]{:S(2)}) collective-permute-start(f32[18,8,256]{2,1,0:T(8,128)S(1)} %get-tuple-element.31._), channel_id=1, source_target_pairs={{1,2},{2,1},{3,4},{4,3},{5,6},{6,5},{9,10},{10,9},{11,12},{12,11},... | collective-permute-start | bytes 442376 | tf_op jit(solution)/shard_map/ppermute | solution.py:58
  28.1 6.1 %collective-permute-start.5 = (f32[18,8,256]{2,1,0:T(8,128)S(1)}, f32[18,8,256]{2,1,0:T(8,128)S(1)}, u32[]{:S(2)}, u32[]{:S(2)}) collective-permute-start(f32[18,8,256]{2,1,0:T(8,128)S(1)} %get-tuple-element.32.own), channel_id=1, source_target_pairs={{0,1},{1,0},{2,3},{3,2},{4,5},{5,4},{6,7},{7,6},{8,9},{9,8},{10,11... | collective-permute-start | bytes 442376 | tf_op jit(solution)/shard_map/ppermute | solution.py:58
  34.3 0.0 collective-permute-done.4.y_odd
  34.3 5.2 %collective-permute-done.5.y_even = f32[18,8,256]{2,1,0:T(8,128)S(1)} collective-permute-done((f32[18,8,256]{2,1,0:T(8,128)S(1)}, f32[18,8,256]{2,1,0:T(8,128)S(1)}, u32[]{:S(2)}, u32[]{:S(2)}) %collective-permute-start.5) | collective-permute-done | bytes 147488 | tf_op jit(solution)/shard_map/ppermute | solution.py:58
  39.5 0.7 %shard_map.127 = (f32[15,8,256]{2,1,0:T(8,128)S(1)}, f32[15,8,256]{2,1,0:T(8,128)S(1)}, f32[8,24,256]{2,1,0:T(8,128)S(1)}, f32[8,24,256]{2,1,0:T(8,128)S(1)}, f3...) custom-call(f32[18,8,256]{2,1,0:T(8,128)S(1)} %get-tuple-element.32.own, ...), custom_call_target="tpu_custom_call" | custom-call | flops 10000000 | bytes 1250000 | tf_op jit(solution)/shard_map/pallas_call | solution.py:562
  40.2 4.1 %collective-permute-start.6 = (f32[15,8,256]{2,1,0:T(8,128)S(1)}, f32[15,8,256]{2,1,0:T(8,128)S(1)}, u32[]{:S(2)}, u32[]{:S(2)}) collective-permute-start(f32[15,8,256]{2,1,0:T(8,128)S(1)} %get-tuple-element.38), channel_id=1, source_target_pairs={{8,16},{16,8},{24,32},{32,24},{40,48},{48,40},{56,64},{64,56},{72,... | collective-permute-start | bytes 368648 | tf_op jit(solution)/shard_map/ppermute | solution.py:58
  44.3 1.9 %collective-permute-start.7 = (f32[15,8,256]{2,1,0:T(8,128)S(1)}, f32[15,8,256]{2,1,0:T(8,128)S(1)}, u32[]{:S(2)}, u32[]{:S(2)}) collective-permute-start(f32[15,8,256]{2,1,0:T(8,128)S(1)} %get-tuple-element.39), channel_id=1, source_target_pairs={{0,8},{8,0},{16,24},{24,16},{32,40},{40,32},{48,56},{56,48},{64,72... | collective-permute-start | bytes 368648 | tf_op jit(solution)/shard_map/ppermute | solution.py:58
  46.2 0.3 shard_map.126.star_rest
  46.6 4.2 %collective-permute-done.6.x_odd = f32[15,8,256]{2,1,0:T(8,128)S(1)} collective-permute-done((f32[15,8,256]{2,1,0:T(8,128)S(1)}, f32[15,8,256]{2,1,0:T(8,128)S(1)}, u32[]{:S(2)}, u32[]{:S(2)}) %collective-permute-start.6) | collective-permute-done | bytes 122912 | tf_op jit(solution)/shard_map/ppermute | solution.py:58
  50.7 0.0 collective-permute-done.7.x_even
  50.7 1.7 %shard_map.128 = (f32[5,8,8,256]{3,2,1,0:T(8,128)}, f32[8,8,256]{2,1,0:T(8,128)}, f32[4,5,1,512]{3,2,1,0:T(1,128)}) custom-call(f32[3,8,8,256]{3,2,1,0:T(8,128)S(1)} %get-tuple-element.30.star, f32[2,8,8,256]{3,2,1,0:T(8,128)S(1)} %shard_map.126.star_rest, f32[8,24,256]{2,1,0:T(8,128)S(1)} %get-tuple-element.33.first, ...), custom_call_target="tpu_custom_call" | custom-call | flops 10000000 | bytes 1250000 | tf_op jit(solution)/shard_map/pallas_call | solution.py:572
  (11 shorter events, 0.1 us)
Async XLA Ops:
  0.6 1.0 %copy-start = (f32[5,8,8,256]{3,2,1,0:T(8,128)S(1)}, f32[5,8,8,256]{3,2,1,0:T(8,128)}, u32[]{:S(2)}) copy-start(f32[5,8,8,256]{3,2,1,0:T(8,128)} %gas.9) | copy-start | bytes 983044
  0.6 1.0 %copy-start.1 = (f32[8,8,256]{2,1,0:T(8,128)S(1)}, f32[8,8,256]{2,1,0:T(8,128)}, u32[]{:S(2)}) copy-start(f32[8,8,256]{2,1,0:T(8,128)} %guess.5) | copy-start | bytes 196612
  1.6 6.9 %copy-start.2 = (f32[4,1,4096]{2,1,0:T(1,128)S(1)}, f32[4,1,4096]{2,1,0:T(1,128)}, u32[]{:S(2)}) copy-start(f32[4,1,4096]{2,1,0:T(1,128)} %motion.1) | copy-start | bytes 196612
  1.6 6.9 %copy-start.3 = (f32[1,4096]{1,0:T(1,128)S(1)}, f32[1,4096]{1,0:T(1,128)}, u32[]{:S(2)}) copy-start(f32[1,4096]{1,0:T(1,128)} %size.1) | copy-start | bytes 49156
  1.6 6.9 %copy-start.4 = (s32[1,4096]{1,0:T(1,128)S(1)}, s32[1,4096]{1,0:T(1,128)}, u32[]{:S(2)}) copy-start(s32[1,4096]{1,0:T(1,128)} %target.1) | copy-start | bytes 49156
  1.6 6.9 %copy-start.5 = (s32[1,4096]{1,0:T(1,128)S(1)}, s32[1,4096]{1,0:T(1,128)}, u32[]{:S(2)}) copy-start(s32[1,4096]{1,0:T(1,128)} %cell.3) | copy-start | bytes 49156
  1.7 9.6 %collective-permute-start = (f32[12,8,256]{2,1,0:T(8,128)S(1)}, f32[12,8,256]{2,1,0:T(8,128)S(1)}, u32[]{:S(2)}, u32[]{:S(2)}) collective-permute-start(f32[12,8,256]{2,1,0:T(8,128)S(1)} %get-tuple-element.24), channel_id=1, source_target_pairs={{1,2},{2,1},{3,4},{4,3},{5,6},{6,5},{9,10},{10,9},{11,12},{12,11},... | collective-permute-start | bytes 294920 | tf_op jit(solution)/shard_map/ppermute | solution.py:58
  2.4 9.0 %collective-permute-start.1 = (f32[12,8,256]{2,1,0:T(8,128)S(1)}, f32[12,8,256]{2,1,0:T(8,128)S(1)}, u32[]{:S(2)}, u32[]{:S(2)}) collective-permute-start(f32[12,8,256]{2,1,0:T(8,128)S(1)} %get-tuple-element.25), channel_id=1, source_target_pairs={{0,1},{1,0},{2,3},{3,2},{4,5},{5,4},{6,7},{7,6},{8,9},{9,8},{10,11... | collective-permute-start | bytes 294920 | tf_op jit(solution)/shard_map/ppermute | solution.py:58
  11.4 15.1 %collective-permute-start.2 = (f32[15,8,256]{2,1,0:T(8,128)S(1)}, f32[15,8,256]{2,1,0:T(8,128)S(1)}, u32[]{:S(2)}, u32[]{:S(2)}) collective-permute-start(f32[15,8,256]{2,1,0:T(8,128)S(1)} %get-tuple-element.27), channel_id=1, source_target_pairs={{8,16},{16,8},{24,32},{32,24},{40,48},{48,40},{56,64},{64,56},{72,... | collective-permute-start | bytes 368648 | tf_op jit(solution)/shard_map/ppermute | solution.py:58
  22.8 2.1 %copy-start.6 = (s32[1,8]{1,0:T(1,128)S(1)}, s32[1,8]{1,0:T(1,128)}, u32[]{:S(2)}) copy-start(s32[1,8]{1,0:T(1,128)} %on.1) | copy-start | bytes 100
  22.8 2.1 %copy-start.7 = (s32[1,8]{1,0:T(1,128)S(1)}, s32[1,8]{1,0:T(1,128)}, u32[]{:S(2)}) copy-start(s32[1,8]{1,0:T(1,128)} %when.1) | copy-start | bytes 100
  22.8 2.1 %copy-start.8 = (s32[1,8]{1,0:T(1,128)S(1)}, s32[1,8]{1,0:T(1,128)}, u32[]{:S(2)}) copy-start(s32[1,8]{1,0:T(1,128)} %head.1) | copy-start | bytes 100
  22.8 3.7 %collective-permute-start.3 = (f32[15,8,256]{2,1,0:T(8,128)S(1)}, f32[15,8,256]{2,1,0:T(8,128)S(1)}, u32[]{:S(2)}, u32[]{:S(2)}) collective-permute-start(f32[15,8,256]{2,1,0:T(8,128)S(1)} %get-tuple-element.28._), channel_id=1, source_target_pairs={{0,8},{8,0},{16,24},{24,16},{32,40},{40,32},{48,56},{56,48},{64,72... | collective-permute-start | bytes 368648 | tf_op jit(solution)/shard_map/ppermute | solution.py:58
  27.5 6.8 %collective-permute-start.4 = (f32[18,8,256]{2,1,0:T(8,128)S(1)}, f32[18,8,256]{2,1,0:T(8,128)S(1)}, u32[]{:S(2)}, u32[]{:S(2)}) collective-permute-start(f32[18,8,256]{2,1,0:T(8,128)S(1)} %get-tuple-element.31._), channel_id=1, source_target_pairs={{1,2},{2,1},{3,4},{4,3},{5,6},{6,5},{9,10},{10,9},{11,12},{12,11},... | collective-permute-start | bytes 442376 | tf_op jit(solution)/shard_map/ppermute | solution.py:58
  28.1 11.3 %collective-permute-start.5 = (f32[18,8,256]{2,1,0:T(8,128)S(1)}, f32[18,8,256]{2,1,0:T(8,128)S(1)}, u32[]{:S(2)}, u32[]{:S(2)}) collective-permute-start(f32[18,8,256]{2,1,0:T(8,128)S(1)} %get-tuple-element.32.own), channel_id=1, source_target_pairs={{0,1},{1,0},{2,3},{3,2},{4,5},{5,4},{6,7},{7,6},{8,9},{9,8},{10,11... | collective-permute-start | bytes 442376 | tf_op jit(solution)/shard_map/ppermute | solution.py:58
  40.2 10.5 %collective-permute-start.6 = (f32[15,8,256]{2,1,0:T(8,128)S(1)}, f32[15,8,256]{2,1,0:T(8,128)S(1)}, u32[]{:S(2)}, u32[]{:S(2)}) collective-permute-start(f32[15,8,256]{2,1,0:T(8,128)S(1)} %get-tuple-element.38), channel_id=1, source_target_pairs={{8,16},{16,8},{24,32},{32,24},{40,48},{48,40},{56,64},{64,56},{72,... | collective-permute-start | bytes 368648 | tf_op jit(solution)/shard_map/ppermute | solution.py:58
  44.3 6.4 %collective-permute-start.7 = (f32[15,8,256]{2,1,0:T(8,128)S(1)}, f32[15,8,256]{2,1,0:T(8,128)S(1)}, u32[]{:S(2)}, u32[]{:S(2)}) collective-permute-start(f32[15,8,256]{2,1,0:T(8,128)S(1)} %get-tuple-element.39), channel_id=1, source_target_pairs={{0,8},{8,0},{16,24},{24,16},{32,40},{40,32},{48,56},{56,48},{64,72... | collective-permute-start | bytes 368648 | tf_op jit(solution)/shard_map/ppermute | solution.py:58

commit v8 on v7

--- a/solution.py
+++ b/solution.py
@@ -231,7 +231,7 @@
         e[k, 3 : 3 + B, B : 2 * B, :] = gas[f]
 
 
-def predict_kernel(gas, guess, y_odd, y_even, x_odd, x_even, sources, parcels, star, even, odd, e, wide, tall, q):
+def predict_kernel(gas, guess, y_odd, y_even, x_odd, x_even, sources, parcels, star, source_out, even, odd, e, wide, tall, q):
     gx = lax.axis_index("gx")
     gy = lax.axis_index("gy")
     has_left, has_right = gx > 0, gx < lax.axis_size("gx") - 1
@@ -287,14 +287,16 @@
         around = q[x + 2, B : 2 * B, :] + q[x, B : 2 * B, :]
         around = around + q[x + 1, B + 1 : 2 * B + 1, :] + q[x + 1, B - 1 : 2 * B - 1, :]
         field = (around + beside(centre, 1) + beside(centre, -1) - source) * (1.0 / 6.0)
+        source_out[x] = source
         for side in (even, odd):
             side[x] = field
             side[B + x] = source
 
     def attach(low, high):
-        for side, heading in ((high, 2), (low, 3)):
-            side[2 * B] = parcels[heading, 0]
-            side[2 * B + 1] = parcels[heading, 1]
+        for side, heading, row in ((high, 2, 0), (low, 3, B - 1)):
+            for x in range(B):
+                side[B + x, row : row + 1, :] = parcels[heading, 0, x : x + 1, :]
+            side[2 * B] = parcels[heading, 1]
 
     by_parity("gy", attach, even, odd)
 
@@ -383,13 +385,13 @@
     return out
 
 
-def slab_kernel(own, y_odd, y_even, even, odd, first, source, f2, f3, f4, f5, f6, low, high):
+def slab_kernel(own, own_source, y_odd, y_even, even, odd, first, source, f2, f3, f4, f5, f6, low, high):
     gy = lax.axis_index("gy")
     scale = weights((), (gy > 0, None, gy < lax.axis_size("gy") - 1))
     row = lax.broadcasted_iota(jnp.int32, (B, HALF), 0)
     for x in range(B):
         first[x, B : 2 * B, :] = own[x]
-        source[x, B : 2 * B, :] = own[B + x]
+        source[x, B : 2 * B, :] = own_source[x]
 
     def fill(below, above):
         for x in range(B):
@@ -445,8 +447,11 @@
                 arrived[d, f, :, half * NZ : (half + 1) * NZ] = halo[at + r // B, r % B : r % B + 1, :]
 
     def take_y(below, above):
-        arrive(2, below, 2 * B)
-        arrive(3, above, 2 * B)
+        for d, halo, row in ((2, below, 0), (3, above, B - 1)):
+            for r in range(10):
+                at, line = (B + r, row) if r < B else (2 * B, r - B)
+                part = slice(r % 2 * NZ, r % 2 * NZ + NZ)
+                arrived[d, r // 2, :, part] = halo[at, line : line + 1, :]
 
     def take_x(left, right):
         hist[0] = left[...]
@@ -539,9 +544,9 @@
     x_odd = swap(x_odd, "gx", 1)
     x_even = swap(x_even, "gx", 0)
     wide = pltpu.VMEM((5, B + 6, 3 * B, NZ), F32)
-    star, ps_even, ps_odd = call(
+    star, own_source, ps_even, ps_odd = call(
         predict_kernel,
-        [shape((3, B, B, NZ), F32), tiles(2 * B + 2), tiles(2 * B + 2)],
+        [shape((3, B, B, NZ), F32), tiles(B), tiles(2 * B + 1), tiles(2 * B + 1)],
         8,
         10**7,
         scratch=[
@@ -562,10 +567,10 @@
     x_even, x_odd, *slabs = call(
         slab_kernel,
         [tiles(NH), tiles(NH)] + [slab] * 5,
-        3,
+        4,
         10**7,
         scratch=[scratch, scratch, pltpu.VMEM((NH, B, NZ), F32), pltpu.VMEM((NH, B, NZ), F32)],
-    )(ps_even, y_odd, y_even)
+    )(ps_even, own_source, y_odd, y_even)
     x_odd = swap(x_odd, "gx", 1)
     x_even = swap(x_even, "gx", 0)
     response = pltpu.VMEM((2, 4, 3 * B, NZ), F32)

time: 52.8 us -> 52.5 us (level)
  no operation moved by 1% of the time
where the time goes in v8:
time: 52.5 us; the launch traced here: 52.1 us
  starting transfers between devices  33.1 us (63%)
  waiting for transfers between devices  9.18 us (17%)
  Pallas kernels  8.02 us (15%)
  local copies, waits for them, and re-layouts  0.99 us (2%)
  between operations  0.87 us (2%)
    ppermute x8, starting transfers between devices, swap(): return lax.ppermute(shard, axis, pairs)  33.1 us
    ppermute x8, waiting for transfers between devices, swap(): return lax.ppermute(shard, axis, pairs)  9.18 us
    pallas_call x1, Pallas kernels, body(): call(renew_kernel, [shape((5, 1, PD), F32), shape((2, PD), F32), shape((4...  2.82 us
    pallas_call x1, Pallas kernels, body(): call(finish_kernel, [shape((5, B, B, NZ), F32), shape((B, B, NZ), F32), s...  1.75 us
    pallas_call x1, Pallas kernels, body(): call(spread_kernel, [shape((3, B * B, NZ), F32)], 6, 10 ** 9, smem=(2, 3,...  1.34 us
  transfers between devices with their start and end apart: 8, of which 3 were waited for; matrix products, arithmetic and copies ran while one was open for 0% of the time, Pallas kernels for 9%

profile of v8, /device:TPU:48, one launch (start us, length us, event | category | flops | bytes accessed | tf_op | source)
XLA Modules:
  0.0 52.1 jit_solution(7916115510468005099)
XLA Ops:
  0.6 0.0 copy-start
  0.7 0.9 %copy-done = f32[5,8,8,256]{3,2,1,0:T(8,128)S(1)} copy-done((f32[5,8,8,256]{3,2,1,0:T(8,128)S(1)}, f32[5,8,8,256]{3,2,1,0:T(8,128)}, u32[]{:S(2)}) %copy-start) | copy-done | bytes 327704
  1.6 0.0 copy-start.5
  1.6 0.1 shard_map.121
  1.7 0.7 %collective-permute-start = (f32[12,8,256]{2,1,0:T(8,128)S(1)}, f32[12,8,256]{2,1,0:T(8,128)S(1)}, u32[]{:S(2)}, u32[]{:S(2)}) collective-permute-start(f32[12,8,256]{2,1,0:T(8,128)S(1)} %get-tuple-element.25), channel_id=1, source_target_pairs={{1,2},{2,1},{3,4},{4,3},{5,6},{6,5},{9,10},{10,9},{11,12},{12,11},... | collective-permute-start | bytes 294920 | tf_op jit(solution)/shard_map/ppermute | solution.py:58
  2.4 6.1 %collective-permute-start.1 = (f32[12,8,256]{2,1,0:T(8,128)S(1)}, f32[12,8,256]{2,1,0:T(8,128)S(1)}, u32[]{:S(2)}, u32[]{:S(2)}) collective-permute-start(f32[12,8,256]{2,1,0:T(8,128)S(1)} %get-tuple-element.26), channel_id=1, source_target_pairs={{0,1},{1,0},{2,3},{3,2},{4,5},{5,4},{6,7},{7,6},{8,9},{9,8},{10,11... | collective-permute-start | bytes 294920 | tf_op jit(solution)/shard_map/ppermute | solution.py:58
  8.5 2.8 %shard_map.122 = (f32[5,1,4096]{2,1,0:T(1,128)}, f32[2,4096]{1,0:T(2,128)S(1)}, f32[4,2,8,256]{3,2,1,0:T(8,128)S(1)}) custom-call(f32[5,8,8,256]{3,2,1,0:T(8,128)S(1)} %copy-done, f32[4,1,4096]{2,1,0:T(1,128)S(1)} %copy-done.2, f32[1,4096]{1,0:T(1,128)S(1)} %copy-done.3, s32[1,4096]{1,0:T(1,128)S(1)} %copy-done.5, s32[1,4096]{1,0:T(1,128)S(1)} %copy-done.4), custom_call_target="tpu_custom_call" | custom-call | flops 1000000000 | bytes 125000000 | tf_op jit(solution)/shard_map/pallas_call | solution.py:532
  11.4 0.0 collective-permute-done.y_odd
  11.4 0.0 collective-permute-done.1.y_even
  11.4 11.4 %collective-permute-start.2 = (f32[15,8,256]{2,1,0:T(8,128)S(1)}, f32[15,8,256]{2,1,0:T(8,128)S(1)}, u32[]{:S(2)}, u32[]{:S(2)}) collective-permute-start(f32[15,8,256]{2,1,0:T(8,128)S(1)} %get-tuple-element.28), channel_id=1, source_target_pairs={{8,16},{16,8},{24,32},{32,24},{40,48},{48,40},{56,64},{64,56},{72,... | collective-permute-start | bytes 368648 | tf_op jit(solution)/shard_map/ppermute | solution.py:58
  22.8 0.0 copy-start.6
  22.8 0.0 copy-start.7
  22.8 0.0 copy-start.8
  22.9 2.1 %collective-permute-start.3 = (f32[15,8,256]{2,1,0:T(8,128)S(1)}, f32[15,8,256]{2,1,0:T(8,128)S(1)}, u32[]{:S(2)}, u32[]{:S(2)}) collective-permute-start(f32[15,8,256]{2,1,0:T(8,128)S(1)} %get-tuple-element.29._), channel_id=1, source_target_pairs={{0,8},{8,0},{16,24},{24,16},{32,40},{40,32},{48,56},{56,48},{64,72... | collective-permute-start | bytes 368648 | tf_op jit(solution)/shard_map/ppermute | solution.py:58
  24.9 0.0 copy-done.6
  24.9 0.0 copy-done.7
  24.9 0.0 copy-done.8
  24.9 1.3 %shard_map.124 = f32[3,64,256]{2,1,0:T(8,128)S(1)} custom-call(f32[2,4096]{1,0:T(2,128)S(1)} %get-tuple-element.30.rows, s32[1,4096]{1,0:T(1,128)S(1)} %copy-done.5, s32[1,8]{1,0:T(1,128)S(1)} %copy-done.6, s32[1,8]{1,0:T(1,128)S(1)} %copy-done.7, s32[1,8]{1,0:T(1,128)S(1)} %copy-done.8, f32[15,8,256]{2,1,0:T(8,128)S(1)} %get-tuple-element.29._), custom_call_target="tpu_custom_call" | custom-call | flops 1000000000 | bytes 125000000 | tf_op jit(solution)/shard_map/pallas_call | solution.py:540
  26.3 0.2 collective-permute-done.2.x_odd.early_odd
  26.5 0.0 collective-permute-done.3.x_even.early_even
  26.5 1.0 %shard_map.125 = (f32[3,8,8,256]{3,2,1,0:T(8,128)S(1)}, f32[8,8,256]{2,1,0:T(8,128)S(1)}, f32[17,8,256]{2,1,0:T(8,128)S(1)}, f32[17,8,256]{2,1,0:T(8,128)S(1)}) custom-call(f32[5,8,8,256]{3,2,1,0:T(8,128)S(1)} %copy-done, f32[8,8,256]{2,1,0:T(8,128)S(1)} %copy-done.1, f32[12,8,256]{2,1,0:T(8,128)S(1)} %collective-permute-done.y_odd, ...), custom_call_target="tpu_custom_call" | custom-call | flops 10000000 | bytes 1250000 | tf_op jit(solution)/shard_map/pallas_call | solution.py:547
  27.5 0.7 %collective-permute-start.4 = (f32[17,8,256]{2,1,0:T(8,128)S(1)}, f32[17,8,256]{2,1,0:T(8,128)S(1)}, u32[]{:S(2)}, u32[]{:S(2)}) collective-permute-start(f32[17,8,256]{2,1,0:T(8,128)S(1)} %get-tuple-element.32._), channel_id=1, source_target_pairs={{1,2},{2,1},{3,4},{4,3},{5,6},{6,5},{9,10},{10,9},{11,12},{12,11},... | collective-permute-start | bytes 417800 | tf_op jit(solution)/shard_map/ppermute | solution.py:58
  28.2 6.1 %collective-permute-start.5 = (f32[17,8,256]{2,1,0:T(8,128)S(1)}, f32[17,8,256]{2,1,0:T(8,128)S(1)}, u32[]{:S(2)}, u32[]{:S(2)}) collective-permute-start(f32[17,8,256]{2,1,0:T(8,128)S(1)} %get-tuple-element.33.own), channel_id=1, source_target_pairs={{0,1},{1,0},{2,3},{3,2},{4,5},{5,4},{6,7},{7,6},{8,9},{9,8},{10,11... | collective-permute-start | bytes 417800 | tf_op jit(solution)/shard_map/ppermute | solution.py:58
  34.3 0.0 collective-permute-done.4.y_odd
  34.3 4.9 %collective-permute-done.5.y_even = f32[17,8,256]{2,1,0:T(8,128)S(1)} collective-permute-done((f32[17,8,256]{2,1,0:T(8,128)S(1)}, f32[17,8,256]{2,1,0:T(8,128)S(1)}, u32[]{:S(2)}, u32[]{:S(2)}) %collective-permute-start.5) | collective-permute-done | bytes 139296 | tf_op jit(solution)/shard_map/ppermute | solution.py:58
  39.2 0.7 %shard_map.127 = (f32[15,8,256]{2,1,0:T(8,128)S(1)}, f32[15,8,256]{2,1,0:T(8,128)S(1)}, f32[8,24,256]{2,1,0:T(8,128)S(1)}, f32[8,24,256]{2,1,0:T(8,128)S(1)}, f3...) custom-call(f32[17,8,256]{2,1,0:T(8,128)S(1)} %get-tuple-element.33.own, ...), custom_call_target="tpu_custom_call" | custom-call | flops 10000000 | bytes 1250000 | tf_op jit(solution)/shard_map/pallas_call | solution.py:567
  39.9 4.2 %collective-permute-start.6 = (f32[15,8,256]{2,1,0:T(8,128)S(1)}, f32[15,8,256]{2,1,0:T(8,128)S(1)}, u32[]{:S(2)}, u32[]{:S(2)}) collective-permute-start(f32[15,8,256]{2,1,0:T(8,128)S(1)} %get-tuple-element.40), channel_id=1, source_target_pairs={{8,16},{16,8},{24,32},{32,24},{40,48},{48,40},{56,64},{64,56},{72,... | collective-permute-start | bytes 368648 | tf_op jit(solution)/shard_map/ppermute | solution.py:58
  44.1 1.9 %collective-permute-start.7 = (f32[15,8,256]{2,1,0:T(8,128)S(1)}, f32[15,8,256]{2,1,0:T(8,128)S(1)}, u32[]{:S(2)}, u32[]{:S(2)}) collective-permute-start(f32[15,8,256]{2,1,0:T(8,128)S(1)} %get-tuple-element.41), channel_id=1, source_target_pairs={{0,8},{8,0},{16,24},{24,16},{32,40},{40,32},{48,56},{56,48},{64,72... | collective-permute-start | bytes 368648 | tf_op jit(solution)/shard_map/ppermute | solution.py:58
  46.0 0.3 shard_map.126.star_rest
  46.3 4.1 %collective-permute-done.6.x_odd = f32[15,8,256]{2,1,0:T(8,128)S(1)} collective-permute-done((f32[15,8,256]{2,1,0:T(8,128)S(1)}, f32[15,8,256]{2,1,0:T(8,128)S(1)}, u32[]{:S(2)}, u32[]{:S(2)}) %collective-permute-start.6) | collective-permute-done | bytes 122912 | tf_op jit(solution)/shard_map/ppermute | solution.py:58
  50.4 0.0 collective-permute-done.7.x_even
  50.4 1.7 %shard_map.128 = (f32[5,8,8,256]{3,2,1,0:T(8,128)}, f32[8,8,256]{2,1,0:T(8,128)}, f32[4,5,1,512]{3,2,1,0:T(1,128)}) custom-call(f32[3,8,8,256]{3,2,1,0:T(8,128)S(1)} %get-tuple-element.31.star, f32[2,8,8,256]{3,2,1,0:T(8,128)S(1)} %shard_map.126.star_rest, f32[8,24,256]{2,1,0:T(8,128)S(1)} %get-tuple-element.35.first, ...), custom_call_target="tpu_custom_call" | custom-call | flops 10000000 | bytes 1250000 | tf_op jit(solution)/shard_map/pallas_call | solution.py:577
  (11 shorter events, 0.1 us)
Async XLA Ops:
  0.6 1.0 %copy-start = (f32[5,8,8,256]{3,2,1,0:T(8,128)S(1)}, f32[5,8,8,256]{3,2,1,0:T(8,128)}, u32[]{:S(2)}) copy-start(f32[5,8,8,256]{3,2,1,0:T(8,128)} %gas.9) | copy-start | bytes 983044
  0.6 1.0 %copy-start.1 = (f32[8,8,256]{2,1,0:T(8,128)S(1)}, f32[8,8,256]{2,1,0:T(8,128)}, u32[]{:S(2)}) copy-start(f32[8,8,256]{2,1,0:T(8,128)} %guess.5) | copy-start | bytes 196612
  1.6 6.9 %copy-start.2 = (f32[4,1,4096]{2,1,0:T(1,128)S(1)}, f32[4,1,4096]{2,1,0:T(1,128)}, u32[]{:S(2)}) copy-start(f32[4,1,4096]{2,1,0:T(1,128)} %motion.1) | copy-start | bytes 196612
  1.6 6.9 %copy-start.3 = (f32[1,4096]{1,0:T(1,128)S(1)}, f32[1,4096]{1,0:T(1,128)}, u32[]{:S(2)}) copy-start(f32[1,4096]{1,0:T(1,128)} %size.1) | copy-start | bytes 49156
  1.6 6.9 %copy-start.4 = (s32[1,4096]{1,0:T(1,128)S(1)}, s32[1,4096]{1,0:T(1,128)}, u32[]{:S(2)}) copy-start(s32[1,4096]{1,0:T(1,128)} %target.1) | copy-start | bytes 49156
  1.6 6.9 %copy-start.5 = (s32[1,4096]{1,0:T(1,128)S(1)}, s32[1,4096]{1,0:T(1,128)}, u32[]{:S(2)}) copy-start(s32[1,4096]{1,0:T(1,128)} %cell.3) | copy-start | bytes 49156
  1.7 9.6 %collective-permute-start = (f32[12,8,256]{2,1,0:T(8,128)S(1)}, f32[12,8,256]{2,1,0:T(8,128)S(1)}, u32[]{:S(2)}, u32[]{:S(2)}) collective-permute-start(f32[12,8,256]{2,1,0:T(8,128)S(1)} %get-tuple-element.25), channel_id=1, source_target_pairs={{1,2},{2,1},{3,4},{4,3},{5,6},{6,5},{9,10},{10,9},{11,12},{12,11},... | collective-permute-start | bytes 294920 | tf_op jit(solution)/shard_map/ppermute | solution.py:58
  2.4 9.0 %collective-permute-start.1 = (f32[12,8,256]{2,1,0:T(8,128)S(1)}, f32[12,8,256]{2,1,0:T(8,128)S(1)}, u32[]{:S(2)}, u32[]{:S(2)}) collective-permute-start(f32[12,8,256]{2,1,0:T(8,128)S(1)} %get-tuple-element.26), channel_id=1, source_target_pairs={{0,1},{1,0},{2,3},{3,2},{4,5},{5,4},{6,7},{7,6},{8,9},{9,8},{10,11... | collective-permute-start | bytes 294920 | tf_op jit(solution)/shard_map/ppermute | solution.py:58
  11.4 15.1 %collective-permute-start.2 = (f32[15,8,256]{2,1,0:T(8,128)S(1)}, f32[15,8,256]{2,1,0:T(8,128)S(1)}, u32[]{:S(2)}, u32[]{:S(2)}) collective-permute-start(f32[15,8,256]{2,1,0:T(8,128)S(1)} %get-tuple-element.28), channel_id=1, source_target_pairs={{8,16},{16,8},{24,32},{32,24},{40,48},{48,40},{56,64},{64,56},{72,... | collective-permute-start | bytes 368648 | tf_op jit(solution)/shard_map/ppermute | solution.py:58
  22.8 2.1 %copy-start.6 = (s32[1,8]{1,0:T(1,128)S(1)}, s32[1,8]{1,0:T(1,128)}, u32[]{:S(2)}) copy-start(s32[1,8]{1,0:T(1,128)} %on.1) | copy-start | bytes 100
  22.8 2.1 %copy-start.7 = (s32[1,8]{1,0:T(1,128)S(1)}, s32[1,8]{1,0:T(1,128)}, u32[]{:S(2)}) copy-start(s32[1,8]{1,0:T(1,128)} %when.1) | copy-start | bytes 100
  22.8 2.1 %copy-start.8 = (s32[1,8]{1,0:T(1,128)S(1)}, s32[1,8]{1,0:T(1,128)}, u32[]{:S(2)}) copy-start(s32[1,8]{1,0:T(1,128)} %head.1) | copy-start | bytes 100
  22.9 3.7 %collective-permute-start.3 = (f32[15,8,256]{2,1,0:T(8,128)S(1)}, f32[15,8,256]{2,1,0:T(8,128)S(1)}, u32[]{:S(2)}, u32[]{:S(2)}) collective-permute-start(f32[15,8,256]{2,1,0:T(8,128)S(1)} %get-tuple-element.29._), channel_id=1, source_target_pairs={{0,8},{8,0},{16,24},{24,16},{32,40},{40,32},{48,56},{56,48},{64,72... | collective-permute-start | bytes 368648 | tf_op jit(solution)/shard_map/ppermute | solution.py:58
  27.5 6.8 %collective-permute-start.4 = (f32[17,8,256]{2,1,0:T(8,128)S(1)}, f32[17,8,256]{2,1,0:T(8,128)S(1)}, u32[]{:S(2)}, u32[]{:S(2)}) collective-permute-start(f32[17,8,256]{2,1,0:T(8,128)S(1)} %get-tuple-element.32._), channel_id=1, source_target_pairs={{1,2},{2,1},{3,4},{4,3},{5,6},{6,5},{9,10},{10,9},{11,12},{12,11},... | collective-permute-start | bytes 417800 | tf_op jit(solution)/shard_map/ppermute | solution.py:58
  28.2 11.0 %collective-permute-start.5 = (f32[17,8,256]{2,1,0:T(8,128)S(1)}, f32[17,8,256]{2,1,0:T(8,128)S(1)}, u32[]{:S(2)}, u32[]{:S(2)}) collective-permute-start(f32[17,8,256]{2,1,0:T(8,128)S(1)} %get-tuple-element.33.own), channel_id=1, source_target_pairs={{0,1},{1,0},{2,3},{3,2},{4,5},{5,4},{6,7},{7,6},{8,9},{9,8},{10,11... | collective-permute-start | bytes 417800 | tf_op jit(solution)/shard_map/ppermute | solution.py:58
  39.9 10.5 %collective-permute-start.6 = (f32[15,8,256]{2,1,0:T(8,128)S(1)}, f32[15,8,256]{2,1,0:T(8,128)S(1)}, u32[]{:S(2)}, u32[]{:S(2)}) collective-permute-start(f32[15,8,256]{2,1,0:T(8,128)S(1)} %get-tuple-element.40), channel_id=1, source_target_pairs={{8,16},{16,8},{24,32},{32,24},{40,48},{48,40},{56,64},{64,56},{72,... | collective-permute-start | bytes 368648 | tf_op jit(solution)/shard_map/ppermute | solution.py:58
  44.1 6.3 %collective-permute-start.7 = (f32[15,8,256]{2,1,0:T(8,128)S(1)}, f32[15,8,256]{2,1,0:T(8,128)S(1)}, u32[]{:S(2)}, u32[]{:S(2)}) collective-permute-start(f32[15,8,256]{2,1,0:T(8,128)S(1)} %get-tuple-element.41), channel_id=1, source_target_pairs={{0,8},{8,0},{16,24},{24,16},{32,40},{40,32},{48,56},{56,48},{64,72... | collective-permute-start | bytes 368648 | tf_op jit(solution)/shard_map/ppermute | solution.py:58

commit v9 on v8

--- a/solution.py
+++ b/solution.py
@@ -10,6 +10,7 @@
 PD = 4096
 CAP = 512
 CHUNK = 512
+LONG = 2048
 F32 = jnp.float32
 BF16 = jnp.bfloat16
 VMEM = pl.BlockSpec(memory_space=pltpu.VMEM)
@@ -76,8 +77,8 @@
     return high, value - high
 
 
-def counting(rows):
-    return lax.broadcasted_iota(jnp.int32, (rows, CHUNK), 0).astype(F32).astype(BF16)
+def counting(rows, lanes=CHUNK):
+    return lax.broadcasted_iota(jnp.int32, (rows, lanes), 0).astype(F32).astype(BF16)
 
 
 def exact(numbers):
@@ -157,12 +158,12 @@
 
 
 def spread_kernel(rows, cell, on, when, head, _, sources):
-    at_z = counting(NZ)
-    at_xy = counting(B * B)
+    at_z = counting(NZ, LONG)
+    at_xy = counting(B * B, LONG)
     total = jnp.zeros((4 * B * B, NZ), F32)
     across = (((1,), (1,)), ((), ()))
-    for n in range(PD // CHUNK):
-        part = slice(n * CHUNK, (n + 1) * CHUNK)
+    for n in range(PD // LONG):
+        part = slice(n * LONG, (n + 1) * LONG)
         cells = cell[:, part]
         in_z = one_hot(at_z, cells & (NZ - 1))
         in_xy = at_xy == exact(cells >> 8)

time: 52.5 us -> 52.5 us (level)
  no operation moved by 1% of the time
where the time goes in v9:
time: 52.5 us; the launch traced here: 52.1 us
  starting transfers between devices  33.1 us (63%)
  waiting for transfers between devices  9.19 us (18%)
  Pallas kernels  8.03 us (15%)
  local copies, waits for them, and re-layouts  0.99 us (2%)
  between operations  0.87 us (2%)
    ppermute x8, starting transfers between devices, swap(): return lax.ppermute(shard, axis, pairs)  33.1 us
    ppermute x8, waiting for transfers between devices, swap(): return lax.ppermute(shard, axis, pairs)  9.19 us
    pallas_call x1, Pallas kernels, body(): call(renew_kernel, [shape((5, 1, PD), F32), shape((2, PD), F32), shape((4...  2.82 us
    pallas_call x1, Pallas kernels, body(): call(finish_kernel, [shape((5, B, B, NZ), F32), shape((B, B, NZ), F32), s...  1.75 us
    pallas_call x1, Pallas kernels, body(): call(spread_kernel, [shape((3, B * B, NZ), F32)], 6, 10 ** 9, smem=(2, 3,...  1.35 us
  transfers between devices with their start and end apart: 8, of which 3 were waited for; matrix products, arithmetic and copies ran while one was open for 0% of the time, Pallas kernels for 9%

profile of v9, /device:TPU:48, one launch (start us, length us, event | category | flops | bytes accessed | tf_op | source)
XLA Modules:
  0.0 52.1 jit_solution(10763786292855820988)
XLA Ops:
  0.6 0.0 copy-start
  0.7 0.9 %copy-done = f32[5,8,8,256]{3,2,1,0:T(8,128)S(1)} copy-done((f32[5,8,8,256]{3,2,1,0:T(8,128)S(1)}, f32[5,8,8,256]{3,2,1,0:T(8,128)}, u32[]{:S(2)}) %copy-start) | copy-done | bytes 327704
  1.6 0.0 copy-start.5
  1.6 0.1 shard_map.121
  1.7 0.7 %collective-permute-start = (f32[12,8,256]{2,1,0:T(8,128)S(1)}, f32[12,8,256]{2,1,0:T(8,128)S(1)}, u32[]{:S(2)}, u32[]{:S(2)}) collective-permute-start(f32[12,8,256]{2,1,0:T(8,128)S(1)} %get-tuple-element.25), channel_id=1, source_target_pairs={{1,2},{2,1},{3,4},{4,3},{5,6},{6,5},{9,10},{10,9},{11,12},{12,11},... | collective-permute-start | bytes 294920 | tf_op jit(solution)/shard_map/ppermute | solution.py:59
  2.4 6.1 %collective-permute-start.1 = (f32[12,8,256]{2,1,0:T(8,128)S(1)}, f32[12,8,256]{2,1,0:T(8,128)S(1)}, u32[]{:S(2)}, u32[]{:S(2)}) collective-permute-start(f32[12,8,256]{2,1,0:T(8,128)S(1)} %get-tuple-element.26), channel_id=1, source_target_pairs={{0,1},{1,0},{2,3},{3,2},{4,5},{5,4},{6,7},{7,6},{8,9},{9,8},{10,11... | collective-permute-start | bytes 294920 | tf_op jit(solution)/shard_map/ppermute | solution.py:59
  8.5 2.8 %shard_map.122 = (f32[5,1,4096]{2,1,0:T(1,128)}, f32[2,4096]{1,0:T(2,128)S(1)}, f32[4,2,8,256]{3,2,1,0:T(8,128)S(1)}) custom-call(f32[5,8,8,256]{3,2,1,0:T(8,128)S(1)} %copy-done, f32[4,1,4096]{2,1,0:T(1,128)S(1)} %copy-done.2, f32[1,4096]{1,0:T(1,128)S(1)} %copy-done.3, s32[1,4096]{1,0:T(1,128)S(1)} %copy-done.5, s32[1,4096]{1,0:T(1,128)S(1)} %copy-done.4), custom_call_target="tpu_custom_call" | custom-call | flops 1000000000 | bytes 125000000 | tf_op jit(solution)/shard_map/pallas_call | solution.py:533
  11.4 0.0 collective-permute-done.y_odd
  11.4 0.0 collective-permute-done.1.y_even
  11.4 11.4 %collective-permute-start.2 = (f32[15,8,256]{2,1,0:T(8,128)S(1)}, f32[15,8,256]{2,1,0:T(8,128)S(1)}, u32[]{:S(2)}, u32[]{:S(2)}) collective-permute-start(f32[15,8,256]{2,1,0:T(8,128)S(1)} %get-tuple-element.28), channel_id=1, source_target_pairs={{8,16},{16,8},{24,32},{32,24},{40,48},{48,40},{56,64},{64,56},{72,... | collective-permute-start | bytes 368648 | tf_op jit(solution)/shard_map/ppermute | solution.py:59
  22.8 0.0 copy-start.6
  22.8 0.0 copy-start.7
  22.8 0.0 copy-start.8
  22.9 2.1 %collective-permute-start.3 = (f32[15,8,256]{2,1,0:T(8,128)S(1)}, f32[15,8,256]{2,1,0:T(8,128)S(1)}, u32[]{:S(2)}, u32[]{:S(2)}) collective-permute-start(f32[15,8,256]{2,1,0:T(8,128)S(1)} %get-tuple-element.29._), channel_id=1, source_target_pairs={{0,8},{8,0},{16,24},{24,16},{32,40},{40,32},{48,56},{56,48},{64,72... | collective-permute-start | bytes 368648 | tf_op jit(solution)/shard_map/ppermute | solution.py:59
  24.9 0.0 copy-done.6
  24.9 0.0 copy-done.7
  24.9 0.0 copy-done.8
  24.9 1.4 %shard_map.124 = f32[3,64,256]{2,1,0:T(8,128)S(1)} custom-call(f32[2,4096]{1,0:T(2,128)S(1)} %get-tuple-element.30.rows, s32[1,4096]{1,0:T(1,128)S(1)} %copy-done.5, s32[1,8]{1,0:T(1,128)S(1)} %copy-done.6, s32[1,8]{1,0:T(1,128)S(1)} %copy-done.7, s32[1,8]{1,0:T(1,128)S(1)} %copy-done.8, f32[15,8,256]{2,1,0:T(8,128)S(1)} %get-tuple-element.29._), custom_call_target="tpu_custom_call" | custom-call | flops 1000000000 | bytes 125000000 | tf_op jit(solution)/shard_map/pallas_call | solution.py:541
  26.3 0.2 collective-permute-done.2.x_odd.early_odd
  26.5 0.0 collective-permute-done.3.x_even.early_even
  26.5 1.0 %shard_map.125 = (f32[3,8,8,256]{3,2,1,0:T(8,128)S(1)}, f32[8,8,256]{2,1,0:T(8,128)S(1)}, f32[17,8,256]{2,1,0:T(8,128)S(1)}, f32[17,8,256]{2,1,0:T(8,128)S(1)}) custom-call(f32[5,8,8,256]{3,2,1,0:T(8,128)S(1)} %copy-done, f32[8,8,256]{2,1,0:T(8,128)S(1)} %copy-done.1, f32[12,8,256]{2,1,0:T(8,128)S(1)} %collective-permute-done.y_odd, ...), custom_call_target="tpu_custom_call" | custom-call | flops 10000000 | bytes 1250000 | tf_op jit(solution)/shard_map/pallas_call | solution.py:548
  27.5 0.7 %collective-permute-start.4 = (f32[17,8,256]{2,1,0:T(8,128)S(1)}, f32[17,8,256]{2,1,0:T(8,128)S(1)}, u32[]{:S(2)}, u32[]{:S(2)}) collective-permute-start(f32[17,8,256]{2,1,0:T(8,128)S(1)} %get-tuple-element.32._), channel_id=1, source_target_pairs={{1,2},{2,1},{3,4},{4,3},{5,6},{6,5},{9,10},{10,9},{11,12},{12,11},... | collective-permute-start | bytes 417800 | tf_op jit(solution)/shard_map/ppermute | solution.py:59
  28.2 6.1 %collective-permute-start.5 = (f32[17,8,256]{2,1,0:T(8,128)S(1)}, f32[17,8,256]{2,1,0:T(8,128)S(1)}, u32[]{:S(2)}, u32[]{:S(2)}) collective-permute-start(f32[17,8,256]{2,1,0:T(8,128)S(1)} %get-tuple-element.33.own), channel_id=1, source_target_pairs={{0,1},{1,0},{2,3},{3,2},{4,5},{5,4},{6,7},{7,6},{8,9},{9,8},{10,11... | collective-permute-start | bytes 417800 | tf_op jit(solution)/shard_map/ppermute | solution.py:59
  34.3 0.0 collective-permute-done.4.y_odd
  34.3 4.9 %collective-permute-done.5.y_even = f32[17,8,256]{2,1,0:T(8,128)S(1)} collective-permute-done((f32[17,8,256]{2,1,0:T(8,128)S(1)}, f32[17,8,256]{2,1,0:T(8,128)S(1)}, u32[]{:S(2)}, u32[]{:S(2)}) %collective-permute-start.5) | collective-permute-done | bytes 139296 | tf_op jit(solution)/shard_map/ppermute | solution.py:59
  39.2 0.7 %shard_map.127 = (f32[15,8,256]{2,1,0:T(8,128)S(1)}, f32[15,8,256]{2,1,0:T(8,128)S(1)}, f32[8,24,256]{2,1,0:T(8,128)S(1)}, f32[8,24,256]{2,1,0:T(8,128)S(1)}, f3...) custom-call(f32[17,8,256]{2,1,0:T(8,128)S(1)} %get-tuple-element.33.own, ...), custom_call_target="tpu_custom_call" | custom-call | flops 10000000 | bytes 1250000 | tf_op jit(solution)/shard_map/pallas_call | solution.py:568
  39.9 4.2 %collective-permute-start.6 = (f32[15,8,256]{2,1,0:T(8,128)S(1)}, f32[15,8,256]{2,1,0:T(8,128)S(1)}, u32[]{:S(2)}, u32[]{:S(2)}) collective-permute-start(f32[15,8,256]{2,1,0:T(8,128)S(1)} %get-tuple-element.40), channel_id=1, source_target_pairs={{8,16},{16,8},{24,32},{32,24},{40,48},{48,40},{56,64},{64,56},{72,... | collective-permute-start | bytes 368648 | tf_op jit(solution)/shard_map/ppermute | solution.py:59
  44.1 1.9 %collective-permute-start.7 = (f32[15,8,256]{2,1,0:T(8,128)S(1)}, f32[15,8,256]{2,1,0:T(8,128)S(1)}, u32[]{:S(2)}, u32[]{:S(2)}) collective-permute-start(f32[15,8,256]{2,1,0:T(8,128)S(1)} %get-tuple-element.41), channel_id=1, source_target_pairs={{0,8},{8,0},{16,24},{24,16},{32,40},{40,32},{48,56},{56,48},{64,72... | collective-permute-start | bytes 368648 | tf_op jit(solution)/shard_map/ppermute | solution.py:59
  46.0 0.3 shard_map.126.star_rest
  46.3 4.1 %collective-permute-done.6.x_odd = f32[15,8,256]{2,1,0:T(8,128)S(1)} collective-permute-done((f32[15,8,256]{2,1,0:T(8,128)S(1)}, f32[15,8,256]{2,1,0:T(8,128)S(1)}, u32[]{:S(2)}, u32[]{:S(2)}) %collective-permute-start.6) | collective-permute-done | bytes 122912 | tf_op jit(solution)/shard_map/ppermute | solution.py:59
  50.4 0.0 collective-permute-done.7.x_even
  50.4 1.7 %shard_map.128 = (f32[5,8,8,256]{3,2,1,0:T(8,128)}, f32[8,8,256]{2,1,0:T(8,128)}, f32[4,5,1,512]{3,2,1,0:T(1,128)}) custom-call(f32[3,8,8,256]{3,2,1,0:T(8,128)S(1)} %get-tuple-element.31.star, f32[2,8,8,256]{3,2,1,0:T(8,128)S(1)} %shard_map.126.star_rest, f32[8,24,256]{2,1,0:T(8,128)S(1)} %get-tuple-element.35.first, ...), custom_call_target="tpu_custom_call" | custom-call | flops 10000000 | bytes 1250000 | tf_op jit(solution)/shard_map/pallas_call | solution.py:578
  (11 shorter events, 0.1 us)
Async XLA Ops:
  0.6 1.0 %copy-start = (f32[5,8,8,256]{3,2,1,0:T(8,128)S(1)}, f32[5,8,8,256]{3,2,1,0:T(8,128)}, u32[]{:S(2)}) copy-start(f32[5,8,8,256]{3,2,1,0:T(8,128)} %gas.9) | copy-start | bytes 983044
  0.6 1.0 %copy-start.1 = (f32[8,8,256]{2,1,0:T(8,128)S(1)}, f32[8,8,256]{2,1,0:T(8,128)}, u32[]{:S(2)}) copy-start(f32[8,8,256]{2,1,0:T(8,128)} %guess.5) | copy-start | bytes 196612
  1.6 6.9 %copy-start.2 = (f32[4,1,4096]{2,1,0:T(1,128)S(1)}, f32[4,1,4096]{2,1,0:T(1,128)}, u32[]{:S(2)}) copy-start(f32[4,1,4096]{2,1,0:T(1,128)} %motion.1) | copy-start | bytes 196612
  1.6 6.9 %copy-start.3 = (f32[1,4096]{1,0:T(1,128)S(1)}, f32[1,4096]{1,0:T(1,128)}, u32[]{:S(2)}) copy-start(f32[1,4096]{1,0:T(1,128)} %size.1) | copy-start | bytes 49156
  1.6 6.9 %copy-start.4 = (s32[1,4096]{1,0:T(1,128)S(1)}, s32[1,4096]{1,0:T(1,128)}, u32[]{:S(2)}) copy-start(s32[1,4096]{1,0:T(1,128)} %target.1) | copy-start | bytes 49156
  1.6 6.9 %copy-start.5 = (s32[1,4096]{1,0:T(1,128)S(1)}, s32[1,4096]{1,0:T(1,128)}, u32[]{:S(2)}) copy-start(s32[1,4096]{1,0:T(1,128)} %cell.3) | copy-start | bytes 49156
  1.7 9.6 %collective-permute-start = (f32[12,8,256]{2,1,0:T(8,128)S(1)}, f32[12,8,256]{2,1,0:T(8,128)S(1)}, u32[]{:S(2)}, u32[]{:S(2)}) collective-permute-start(f32[12,8,256]{2,1,0:T(8,128)S(1)} %get-tuple-element.25), channel_id=1, source_target_pairs={{1,2},{2,1},{3,4},{4,3},{5,6},{6,5},{9,10},{10,9},{11,12},{12,11},... | collective-permute-start | bytes 294920 | tf_op jit(solution)/shard_map/ppermute | solution.py:59
  2.4 9.0 %collective-permute-start.1 = (f32[12,8,256]{2,1,0:T(8,128)S(1)}, f32[12,8,256]{2,1,0:T(8,128)S(1)}, u32[]{:S(2)}, u32[]{:S(2)}) collective-permute-start(f32[12,8,256]{2,1,0:T(8,128)S(1)} %get-tuple-element.26), channel_id=1, source_target_pairs={{0,1},{1,0},{2,3},{3,2},{4,5},{5,4},{6,7},{7,6},{8,9},{9,8},{10,11... | collective-permute-start | bytes 294920 | tf_op jit(solution)/shard_map/ppermute | solution.py:59
  11.4 15.1 %collective-permute-start.2 = (f32[15,8,256]{2,1,0:T(8,128)S(1)}, f32[15,8,256]{2,1,0:T(8,128)S(1)}, u32[]{:S(2)}, u32[]{:S(2)}) collective-permute-start(f32[15,8,256]{2,1,0:T(8,128)S(1)} %get-tuple-element.28), channel_id=1, source_target_pairs={{8,16},{16,8},{24,32},{32,24},{40,48},{48,40},{56,64},{64,56},{72,... | collective-permute-start | bytes 368648 | tf_op jit(solution)/shard_map/ppermute | solution.py:59
  22.8 2.1 %copy-start.6 = (s32[1,8]{1,0:T(1,128)S(1)}, s32[1,8]{1,0:T(1,128)}, u32[]{:S(2)}) copy-start(s32[1,8]{1,0:T(1,128)} %on.1) | copy-start | bytes 100
  22.8 2.1 %copy-start.7 = (s32[1,8]{1,0:T(1,128)S(1)}, s32[1,8]{1,0:T(1,128)}, u32[]{:S(2)}) copy-start(s32[1,8]{1,0:T(1,128)} %when.1) | copy-start | bytes 100
  22.8 2.1 %copy-start.8 = (s32[1,8]{1,0:T(1,128)S(1)}, s32[1,8]{1,0:T(1,128)}, u32[]{:S(2)}) copy-start(s32[1,8]{1,0:T(1,128)} %head.1) | copy-start | bytes 100
  22.9 3.7 %collective-permute-start.3 = (f32[15,8,256]{2,1,0:T(8,128)S(1)}, f32[15,8,256]{2,1,0:T(8,128)S(1)}, u32[]{:S(2)}, u32[]{:S(2)}) collective-permute-start(f32[15,8,256]{2,1,0:T(8,128)S(1)} %get-tuple-element.29._), channel_id=1, source_target_pairs={{0,8},{8,0},{16,24},{24,16},{32,40},{40,32},{48,56},{56,48},{64,72... | collective-permute-start | bytes 368648 | tf_op jit(solution)/shard_map/ppermute | solution.py:59
  27.5 6.8 %collective-permute-start.4 = (f32[17,8,256]{2,1,0:T(8,128)S(1)}, f32[17,8,256]{2,1,0:T(8,128)S(1)}, u32[]{:S(2)}, u32[]{:S(2)}) collective-permute-start(f32[17,8,256]{2,1,0:T(8,128)S(1)} %get-tuple-element.32._), channel_id=1, source_target_pairs={{1,2},{2,1},{3,4},{4,3},{5,6},{6,5},{9,10},{10,9},{11,12},{12,11},... | collective-permute-start | bytes 417800 | tf_op jit(solution)/shard_map/ppermute | solution.py:59
  28.2 11.0 %collective-permute-start.5 = (f32[17,8,256]{2,1,0:T(8,128)S(1)}, f32[17,8,256]{2,1,0:T(8,128)S(1)}, u32[]{:S(2)}, u32[]{:S(2)}) collective-permute-start(f32[17,8,256]{2,1,0:T(8,128)S(1)} %get-tuple-element.33.own), channel_id=1, source_target_pairs={{0,1},{1,0},{2,3},{3,2},{4,5},{5,4},{6,7},{7,6},{8,9},{9,8},{10,11... | collective-permute-start | bytes 417800 | tf_op jit(solution)/shard_map/ppermute | solution.py:59
  39.9 10.5 %collective-permute-start.6 = (f32[15,8,256]{2,1,0:T(8,128)S(1)}, f32[15,8,256]{2,1,0:T(8,128)S(1)}, u32[]{:S(2)}, u32[]{:S(2)}) collective-permute-start(f32[15,8,256]{2,1,0:T(8,128)S(1)} %get-tuple-element.40), channel_id=1, source_target_pairs={{8,16},{16,8},{24,32},{32,24},{40,48},{48,40},{56,64},{64,56},{72,... | collective-permute-start | bytes 368648 | tf_op jit(solution)/shard_map/ppermute | solution.py:59
  44.1 6.3 %collective-permute-start.7 = (f32[15,8,256]{2,1,0:T(8,128)S(1)}, f32[15,8,256]{2,1,0:T(8,128)S(1)}, u32[]{:S(2)}, u32[]{:S(2)}) collective-permute-start(f32[15,8,256]{2,1,0:T(8,128)S(1)} %get-tuple-element.41), channel_id=1, source_target_pairs={{0,8},{8,0},{16,24},{24,16},{32,40},{40,32},{48,56},{56,48},{64,72... | collective-permute-start | bytes 368648 | tf_op jit(solution)/shard_map/ppermute | solution.py:59
